TPU v7x, 32 devices: a whole 2x2x4 slice. The times are simulated.
32 devices in a mesh: grp: 2 (over y), tile: 4 (over z), lev: 2 (over x), sub: 2 (over core).
Axes of the slice: x: 2, y: 2, z: 4, core: 2. Of those that a mesh axis runs over, the one named last changes fastest.
Arguments:
- control: bfloat16 [2048, 64, 192], P('tile', 'lev', ('grp', 'sub')), parts along dimension 2, may hold values from -6 to 6
- node_count: int32 [4], P('tile'), may hold values from 256 to 512, as said below
- vert_coef: bfloat16 [64, 64], replicated
- send_list: int32 [4, 4, 1], replicated, may hold values from 0 to 1
- conv_slots: int32 [4, 2, 9], P('tile'), may hold values from 0 to 5, as said below
- conv_coef: bfloat16 [4, 2, 9, 256, 256], P('tile'), may hold values from -0.125 to 0.125
- interp_slots: int32 [8, 3, 3], P('tile'), may hold values from 0 to 5
- interp_coef: bfloat16 [8, 3, 3, 256, 256], P(('tile', 'sub')), may hold values from -0.21875 to 0.21875
Outputs:
- model_field: bfloat16 [6144, 64, 192], P(('tile', 'sub'), 'lev', 'grp'), parts along dimension 2
There are 2 independent parts, one for each index of `grp`. A program takes and returns all parts, laid end to end along the dimension named above; an argument that names none is the same for every part. Nothing has to cross between parts.
Inputs may be any that keep to these rules, and one draw needn't show every extreme that they name: `node_count`: some tile holds 512 valid nodes in every draw. `conv_slots`: entry k = 0 is the block's own local block; every lent entry of a tile's list is read by some block of that tile.
All inputs are finite; a program needn't handle non-finite values.
Results may differ from a plain program's by a relative error of at most 0.02.
Values may be sent and summed in bfloat16 or wider, within the bound.
No kernel may reach another device: no remote copies, remote signals or barrier semaphores. Data moves between devices by JAX's collectives and lax.ppermute only.
A program may use at most 64 MiB of HBM per device.

v0:
```python
import jax
import jax.numpy as jnp
from jax import lax
from jax.sharding import PartitionSpec as P


def local(
    control, node_count, vert_coef, send_list, conv_slots, conv_coef, interp_slots, interp_coef
):
    node_rows, level_rows, member_rows = control.shape
    block_len = conv_coef.shape[-1]
    block_count = conv_coef.shape[1]
    columns = level_rows * member_rows
    tile_count = lax.axis_size("tile")
    halves = lax.axis_size("sub")
    tile_place = lax.axis_index("tile")
    level_place = lax.axis_index("lev")
    half_place = lax.axis_index("sub")
    position = lax.broadcasted_iota(jnp.int32, (node_rows, 1, 1), 0)
    masked = jnp.where(position < node_count[0], control, jnp.zeros_like(control))
    own_weights = lax.dynamic_slice_in_dim(vert_coef, level_place * level_rows, level_rows, 1)
    partial_value = jnp.einsum(
        "al,nlm->nam", own_weights, masked, preferred_element_type=jnp.float32
    )
    vertical = lax.psum_scatter(
        partial_value.astype(jnp.bfloat16), "lev", scatter_dimension=1, tiled=True
    )
    blocks = vertical.reshape(block_count, block_len, columns)
    incoming_ids = lax.dynamic_index_in_dim(send_list, tile_place, 1, keepdims=False)
    source_base = (jnp.arange(tile_count, dtype=jnp.int32) * block_count)[:, None]
    everything = lax.all_gather(blocks, "tile", axis=0, tiled=True)
    received = everything[source_base + incoming_ids]
    extended = jnp.concatenate([blocks, received.reshape(-1, block_len, columns)], 0)
    chosen = extended[conv_slots[0]]
    spread = jnp.einsum(
        "bkij,bkjc->bic", conv_coef[0], chosen, preferred_element_type=jnp.float32
    ).astype(jnp.bfloat16)
    spread_every = lax.all_gather(spread, "tile", axis=0, tiled=True)
    spread_lent = spread_every[source_base + incoming_ids]
    spread_ext = jnp.concatenate([spread, spread_lent.reshape(-1, block_len, columns)], 0)
    own_slots = lax.dynamic_index_in_dim(interp_slots, half_place, 0, keepdims=False)
    members_all = lax.all_gather(spread_ext, "sub", axis=2, tiled=True)
    picked = members_all[own_slots]
    result = jnp.einsum(
        "pjab,pjbc->pac", interp_coef[0], picked, preferred_element_type=jnp.float32
    )
    point_rows = result.shape[0] * block_len
    shaped = result.reshape(point_rows, halves, level_rows, member_rows)
    return (
        shaped.transpose(0, 2, 1, 3)
        .reshape(point_rows, level_rows, halves * member_rows)
        .astype(jnp.bfloat16)
    )


def solution(mesh):
    placed = (
        P("tile", "lev", ("grp", "sub")),
        P("tile"),
        P(),
        P(),
        P("tile", None, None),
        P("tile", None, None, None, None),
        P("tile", None, None),
        P(("tile", "sub"), None, None, None, None),
    )
    return jax.shard_map(
        local,
        mesh=mesh,
        in_specs=placed,
        out_specs=P(("tile", "sub"), "lev", "grp"),
        check_vma=False,
    )
```

profile of v0, /device:TPU:1, one launch (start us, length us, event | category | flops | bytes accessed | tf_op | source)
XLA Modules:
  0.0 430.3 jit_solution(5523677921340774529)
XLA Ops:
  6.5 0.0 copy-start
  6.5 0.0 copy-start.3
  6.5 0.0 reduce-scatter.2.cloned.1.call-start
  7.4 1.5 broadcast_select_fusion
  8.9 0.0 copy-done.3
  8.9 3.0 convert_bitcast_fusion
  11.9 0.0 reduce-scatter.2.cloned.1.call-update
  11.9 0.0 all-gather.4.cloned.1.call-start
  12.0 45.5 %reduce-scatter.2.cloned.1.call-done = bf16[512,32,48]{0,1,2:T(8,128)(2,1)} async-done(((bf16[512,64,48]{0,1,2:T(8,128)(2,1)}), bf16[512,32,48]{0,1,2:T(8,128)(2,1)}) %reduce-scatter.2.cloned.1.call-update) | async-done | bytes 1572880 | tf_op jit(solution)/shard_map/reduce_scatter | solution.py:25
  57.5 3.4 copy.27
  60.9 3.5 reshape.88
  64.4 0.0 copy-start.5
  64.4 0.0 copy-start.4
  64.4 5.0 %copy.29 = bf16[2,256,1536]{2,1,0:T(8,128)(2,1)} copy(bf16[2,256,1536]{1,0,2:T(2,128)(2,1)} %reshape.88) | data formatting | bytes 3145728 | tf_op jit(solution)/shard_map/reshape | solution.py:28
  69.4 0.0 all-gather.4.cloned.1.call-update
  69.4 0.0 all-gather.6.cloned.1.call-start
  69.5 0.0 copy-done.5
  69.5 0.1 reshape.101
  69.6 0.0 copy-done.4
  69.6 0.2 fusion.8
  69.9 115.3 %all-gather.4.cloned.1.call-done = bf16[8,256,1536]{2,1,0:T(8,128)(2,1)} async-done(((bf16[2,256,1536]{2,1,0:T(8,128)(2,1)}), bf16[8,256,1536]{2,1,0:T(8,128)(2,1)}) %all-gather.4.cloned.1.call-update) | async-done | bytes 6291472 | tf_op jit(solution)/shard_map/all_gather | solution.py:31
  185.2 5.2 %gather_fusion = bf16[4,256,1536]{2,1,0:T(8,128)(2,1)} fusion(bf16[8,256,1536]{2,1,0:T(8,128)(2,1)} %all-gather.4.cloned.1.call-done, s32[1024]{0:T(1024)S(1)} %pad_clamp_fusion.2), kind=kCustom, calls=%fused_computation | custom fusion | bytes 6291472 | tf_op jit(solution)/shard_map/gather | solution.py:32
  190.4 4.9 %pad_maximum_fusion = bf16[6,256,1536]{2,1,0:T(8,128)(2,1)} fusion(bf16[4,256,1536]{2,1,0:T(8,128)(2,1)} %gather_fusion, bf16[2,256,1536]{2,1,0:T(8,128)(2,1)} %copy.29), kind=kLoop, calls=%fused_computation.5 | loop fusion | flops 2359296 | bytes 9437184 | tf_op jit(solution)/shard_map/concatenate | solution.py:33
  195.4 9.3 %gather_fusion.1 = bf16[18,256,1536]{2,1,0:T(8,128)(2,1)} fusion(bf16[6,256,1536]{2,1,0:T(8,128)(2,1)} %pad_maximum_fusion, s32[1024]{0:T(1024)S(1)} %pad_clamp_fusion.1), kind=kCustom, calls=%fused_computation.1 | custom fusion | bytes 28311624 | tf_op jit(solution)/shard_map/gather | solution.py:34
  204.7 0.0 copy-done
  204.7 10.2 %fusion.2 = bf16[2,256,1536]{1,2,0:T(8,128)(2,1)} fusion(bf16[2,9,256,1536]{3,2,1,0:T(8,128)(2,1)} %bitcast.48, bf16[1,2,9,256,256]{4,3,2,1,0:T(8,128)(2,1)S(1)} %copy-done), kind=kOutput, calls=%fused_computation.11 | convolution fusion | flops 3624665088 | bytes 18087936 | tf_op jit(solution)/shard_map/bkij,bkjc->bic/dot_general | solution.py:35
  214.9 2.6 copy.32
  217.5 0.0 all-gather.6.cloned.1.call-update
  217.5 0.0 copy-start.2
  217.5 0.2 all-gather.8.cloned.1.call-start
  217.8 113.5 %all-gather.6.cloned.1.call-done = bf16[8,256,1536]{2,1,0:T(8,128)(2,1)} async-done(((bf16[2,256,1536]{2,1,0:T(8,128)(2,1)}), bf16[8,256,1536]{2,1,0:T(8,128)(2,1)}) %all-gather.6.cloned.1.call-update) | async-done | bytes 6291472 | tf_op jit(solution)/shard_map/all_gather | solution.py:38
  331.3 5.2 %gather_fusion.2 = bf16[4,256,1536]{2,1,0:T(8,128)(2,1)} fusion(bf16[8,256,1536]{2,1,0:T(8,128)(2,1)} %all-gather.6.cloned.1.call-done, s32[1024]{0:T(1024)S(1)} %pad_clamp_fusion.2), kind=kCustom, calls=%fused_computation.2 | custom fusion | bytes 6291472 | tf_op jit(solution)/shard_map/gather | solution.py:39
  336.5 0.0 copy-done.2
  336.5 4.5 %pad_maximum_fusion.1 = bf16[6,256,1536]{2,1,0:T(8,128)(2,1)} fusion(bf16[4,256,1536]{2,1,0:T(8,128)(2,1)} %gather_fusion.2, bf16[2,256,1536]{2,1,0:T(8,128)(2,1)S(1)} %copy-done.2), kind=kLoop, calls=%fused_computation.6 | loop fusion | flops 2359296 | bytes 9437184 | tf_op jit(solution)/shard_map/concatenate | solution.py:40
  341.0 0.0 copy-start.6
  341.0 0.0 all-gather.8.cloned.1.call-update
  341.0 0.7 copy-done.6
  341.7 0.1 reshape.117
  341.8 0.0 copy-start.7
  341.8 19.6 %all-gather.8.cloned.1.call-done = bf16[6,256,3072]{2,1,0:T(8,128)(2,1)} async-done(((bf16[6,256,1536]{2,1,0:T(8,128)(2,1)}), bf16[6,256,3072]{2,1,0:T(8,128)(2,1)}) %all-gather.8.cloned.1.call-update) | async-done | bytes 9437200 | tf_op jit(solution)/shard_map/all_gather | solution.py:42
  361.4 10.6 %gather_fusion.3 = bf16[9,256,3072]{2,1,0:T(8,128)(2,1)} fusion(bf16[6,256,3072]{2,1,0:T(8,128)(2,1)} %all-gather.8.cloned.1.call-done, s32[1024]{0:T(1024)S(1)} %pad_clamp_fusion), kind=kCustom, calls=%fused_computation.3 | custom fusion | bytes 28311588 | tf_op jit(solution)/shard_map/gather | solution.py:43
  372.0 0.0 copy-done.7
  372.0 8.2 %fusion = bf16[3,256,3072]{1,2,0:T(8,128)(2,1)S(1)} fusion(bf16[3,3,256,3072]{3,2,1,0:T(8,128)(2,1)} %bitcast.47, bf16[1,3,3,256,256]{4,3,2,1,0:T(8,128)(2,1)S(1)} %copy-done.7), kind=kOutput, calls=%fused_computation.7 | convolution fusion | flops 3626237952 | bytes 20054016 | tf_op jit(solution)/shard_map/pjab,pjbc->pac/dot_general | solution.py:44
  380.2 25.2 %copy.34 = bf16[3,256,3072]{1,0,2:T(4,128)(2,1)} copy(bf16[3,256,3072]{1,2,0:T(8,128)(2,1)S(1)} %fusion) | data formatting | bytes 9437184 | tf_op jit(solution)/shard_map/convert_element_type | solution.py:52
  405.4 13.0 %convert_element_type.33 = bf16[768,2,32,48]{0,3,2,1:T(8,128)(2,1)} reshape(bf16[3,256,3072]{1,0,2:T(4,128)(2,1)} %copy.34) | data formatting | bytes 9437184 | tf_op jit(solution)/shard_map/convert_element_type | solution.py:52
  418.4 0.0 copy-start.1
  418.4 5.3 %copy.35 = bf16[768,32,2,48]{0,3,2,1:T(8,128)(2,1)} copy(bf16[768,32,2,48]{0,3,1,2:T(8,128)(2,1)} %bitcast.46) | data formatting | bytes 9437184 | tf_op jit(solution)/shard_map/convert_element_type | solution.py:52
  423.8 0.0 copy-done.1
  (6 shorter events, 0.1 us)
Async XLA Ops:
  6.5 198.1 %copy-start = (bf16[1,2,9,256,256]{4,3,2,1,0:T(8,128)(2,1)S(1)}, bf16[1,2,9,256,256]{4,3,2,1,0:T(8,128)(2,1)}, u32[]{:S(2)}) copy-start(bf16[1,2,9,256,256]{4,3,2,1,0:T(8,128)(2,1)} %param.13) | copy-start | bytes 7077892
  6.5 2.4 copy-start.3
  6.5 50.9 %reduce-scatter.2.cloned.1.call-start = ((), (), s32[]{:S(2)}) async-start(), calls=%async_computation.1 | async-start | bytes 4718592 | tf_op jit(solution)/shard_map/reduce_scatter | solution.py:25
  11.9 173.3 %all-gather.4.cloned.1.call-start = ((), (), s32[]{:S(2)}) async-start(), calls=%async_computation.2 | async-start | bytes 7864320 | tf_op jit(solution)/shard_map/all_gather | solution.py:31
  64.4 5.1 %copy-start.5 = (s32[1,2,9]{2,1,0:T(2,128)S(1)}, s32[1,2,9]{2,1,0:T(2,128)}, u32[]{:S(2)}) copy-start(s32[1,2,9]{2,1,0:T(2,128)} %param.12) | copy-start | bytes 220
  64.4 5.2 %copy-start.4 = (s32[4,4,1]{1,2,0:T(1,128)S(1)}, s32[4,4,1]{1,2,0:T(1,128)}, u32[]{:S(2)}) copy-start(s32[4,4,1]{1,2,0:T(1,128)} %param.11) | copy-start | bytes 196
  69.4 261.8 %all-gather.6.cloned.1.call-start = ((), (), s32[]{:S(2)}) async-start(), calls=%async_computation.3 | async-start | bytes 7864320 | tf_op jit(solution)/shard_map/all_gather | solution.py:38
  217.5 119.0 %copy-start.2 = (bf16[2,256,1536]{2,1,0:T(8,128)(2,1)S(1)}, bf16[2,256,1536]{2,1,0:T(8,128)(2,1)}, u32[]{:S(2)}) copy-start(bf16[2,256,1536]{2,1,0:T(8,128)(2,1)} %copy.32) | copy-start | bytes 4718596
  217.5 143.8 %all-gather.8.cloned.1.call-start = ((), (), s32[]{:S(2)}) async-start(), calls=%async_computation.4 | async-start | bytes 14155776 | tf_op jit(solution)/shard_map/all_gather | solution.py:42
  341.0 0.7 copy-start.6
  341.8 30.2 %copy-start.7 = (bf16[1,3,3,256,256]{4,3,2,1,0:T(8,128)(2,1)S(1)}, bf16[1,3,3,256,256]{4,3,2,1,0:T(8,128)(2,1)}, u32[]{:S(2)}) copy-start(bf16[1,3,3,256,256]{4,3,2,1,0:T(8,128)(2,1)} %param.15) | copy-start | bytes 3538948
  418.4 5.3 %copy-start.1 = (bf16[1,2,9,256,256]{4,3,2,1,0:T(8,128)(2,1)S(1)}, bf16[1,2,9,256,256]{4,3,2,1,0:T(8,128)(2,1)}, u32[]{:S(2)}) copy-start(bf16[1,2,9,256,256]{4,3,2,1,0:T(8,128)(2,1)} %param.13) | copy-start | bytes 7077892
Sparse Core Ops, SparseCore 0:
  12.0 45.4 reduce-scatter.1
  69.6 115.5 all-gather.3
  217.7 113.5 all-gather.5
  341.1 20.1 all-gather.7
where the time goes:
time: 431 us; the launch traced here: 430 us
  waiting for transfers between devices  294 us (68%)
  local copies, waits for them, and re-layouts  89.3 us (21%)
  matrix products  21.4 us (5%)
  between operations  14 us (3%)
  other arithmetic  11.2 us (3%)
    all_gather x1, waiting for transfers between devices, local(): everything = lax.all_gather(blocks, 'tile', axis=0, tiled=True)  115 us
    all_gather x1, waiting for transfers between devices, local(): spread_every = lax.all_gather(spread, 'tile', axis=0, tiled=True)  113 us
    reduce_scatter x1, waiting for transfers between devices, local(): lax.psum_scatter(partial_value.astype(jnp.bfloat16), 'lev', scatter_dimen...  45.5 us
    convert_element_type x3, local copies, waits for them, and re-layouts, local(): return shaped.transpose(0, 2, 1, 3).reshape(point_rows, level_rows, halve...  43.6 us
    all_gather x1, waiting for transfers between devices, local(): members_all = lax.all_gather(spread_ext, 'sub', axis=2, tiled=True)  19.6 us
    gather x1, local copies, waits for them, and re-layouts, local(): picked = members_all[own_slots]  10.6 us
    dot_general x1, matrix products, local(): jnp.einsum('bkij,bkjc->bic', conv_coef[0], chosen, preferred_element_type...  10.2 us
    gather x1, local copies, waits for them, and re-layouts, local(): chosen = extended[conv_slots[0]]  9.32 us
  transfers between devices with their start and end apart: 4, of which 4 were waited for; matrix products, arithmetic and copies ran while one was open for 0% of the time, Pallas kernels for 0%

commit v1 on v0

--- a/solution.py
+++ b/solution.py
@@ -1,10 +1,259 @@
+import functools
+
 import jax
 import jax.numpy as jnp
 from jax import lax
+from jax.experimental import pallas as pl
+from jax.experimental.pallas import tpu as pltpu
 from jax.sharding import PartitionSpec as P
 
+CHUNK = 16
+VMEM_LIMIT = 48 * 1024 * 1024
+SMEM = pl.BlockSpec(memory_space=pltpu.SMEM)
+VMEM = pl.BlockSpec(memory_space=pltpu.VMEM)
+HBM = pl.BlockSpec(memory_space=pl.ANY)
+BF16 = jnp.bfloat16
+F32 = jnp.float32
+
+
+def params():
+    return pltpu.CompilerParams(vmem_limit_bytes=VMEM_LIMIT)
+
+
+def dot_nt(a, b):
+    return lax.dot_general(a, b, (((1,), (1,)), ((), ())), preferred_element_type=F32)
+
+
+def merge_kernel(tiles, place, send, slots, coef, out, total):
+    blocks, taps = coef.shape[:2]
+    own = blocks
+    t = place[0]
+    total[...] = jnp.zeros_like(total)
+    for b in range(blocks):
+        for k in range(taps):
+            slot = slots[0, b, k]
+            lender = jnp.maximum(slot - own, 0)
+            distance = lax.rem(t - lender + tiles, tiles)
+            lent = jnp.where(distance == 0, send[lender, t, 0], own - 1 + distance)
+            entry = jnp.where(slot < own, slot, lent)
+            total[b, entry] += coef[b, k].astype(F32)
+    out[...] = total[...].astype(BF16)
+
+
+def weight_kernel(levels, place, vert, out):
+    rows = levels * CHUNK
+    total = vert.shape[0]
+    lev = place[1]
+    shape = (rows, total)
+    pick = lax.broadcasted_iota(jnp.int32, shape, 0) // CHUNK + lev * levels
+    left = (lax.broadcasted_iota(jnp.int32, shape, 1) == pick).astype(BF16)
+    spread = jnp.dot(left, vert[...], preferred_element_type=F32).astype(BF16)
+    row = lax.broadcasted_iota(jnp.int32, (rows, rows), 0)
+    col = lax.broadcasted_iota(jnp.int32, (rows, rows), 1)
+    same = lax.rem(row, CHUNK) == lax.rem(col, CHUNK)
+    for side in range(2):
+        base = jnp.where(lev == side, 0, levels)
+        wanted = lax.broadcasted_iota(jnp.int32, shape, 0) // CHUNK + base
+        right = (lax.broadcasted_iota(jnp.int32, shape, 1) == wanted).astype(BF16)
+        full = dot_nt(spread, right)
+        out[side] = jnp.where(same, full, 0.0).astype(BF16)
+
+
+def vertical_kernel(count, weight, own, other, out):
+    value = jnp.dot(weight[0], own[...], preferred_element_type=F32)
+    value += jnp.dot(weight[1], other[...], preferred_element_type=F32)
+    node = lax.broadcasted_iota(jnp.int32, value.shape, 1)
+    value = jnp.where(node < count[0], value, 0.0).astype(BF16)
+    size = out.shape[-1]
+    for b in range(out.shape[0]):
+        out[b] = value[:, b * size : (b + 1) * size]
+
+
+def spread_kernel(tiles, place, send, coef_own, coef_lent, own, *rest):
+    rights, lefts = rest[: tiles - 1], rest[tiles - 1 : 2 * tiles - 2]
+    out, held, sems = rest[2 * tiles - 2 :]
+    t = place[0]
+    blocks = own.shape[0]
+    copies = [pltpu.make_async_copy(own, held.at[0], sems.at[0])]
+    copies[0].start()
+    for d in range(1, tiles):
+        from_left = t >= d
+
+        @pl.when(from_left)
+        def _():
+            pltpu.make_async_copy(rights[d - 1], held.at[d], sems.at[d]).start()
+
+        @pl.when(jnp.logical_not(from_left))
+        def _():
+            pltpu.make_async_copy(lefts[tiles - d - 1], held.at[d], sems.at[d]).start()
+
+        copies.append(pltpu.make_async_copy(rights[d - 1], held.at[d], sems.at[d]))
+    for copy in copies:
+        copy.wait()
+    for j in range(blocks + tiles - 1):
+        away = max(0, j - blocks + 1)
+        source = lax.rem(t - away + tiles, tiles)
+        total = None
+        for e in range(blocks + tiles - 1):
+            hop = max(0, e - blocks + 1)
+            lender = lax.rem(source - hop + tiles, tiles)
+            if e < blocks:
+                block = e
+            else:
+                block = send[lender, source, 0]
+            distance = lax.rem(t - lender + tiles, tiles)
+            if j < blocks:
+                matrix = coef_own[j, e]
+            else:
+                matrix = coef_lent[:, away - 1, e].reshape(coef_own.shape[-2:])
+            part = dot_nt(held[distance, block], matrix)
+            total = part if total is None else total + part
+        out[j] = total.astype(BF16)
+
+
+def interp_kernel(tiles, place, send, slots, coef, field, *rest):
+    out = rest[-1]
+    own = field.shape[0] - tiles + 1
+    t, sub = place[0], place[2]
+    p = pl.program_id(0)
+    total = None
+    for j in range(coef.shape[2]):
+        slot = slots[sub, p, j]
+        lender = jnp.maximum(slot - own, 0)
+        distance = lax.rem(t - lender + tiles, tiles)
+        lent = jnp.where(distance == 0, send[lender, t, 0], own - 1 + distance)
+        entry = jnp.where(slot < own, slot, lent)
+        part = dot_nt(field[entry], coef[0, 0, j])
+        total = part if total is None else total + part
+    out[...] = total.astype(BF16).reshape(out.shape)
+
+
+def interpolate(chunk, half, tiles, place, send, slots, coef, field, shape, before):
+    levels, members, points = shape
+    count = coef.shape[1]
+    chunks = members // 2 // CHUNK
+    size = coef.shape[-1]
+
+    def place_out(p, place, send, slots):
+        sub = place[2]
+        side = sub if half == 0 else 1 - sub
+        return (0, side * chunks + chunk, p)
+
+    in_specs = [
+        pl.BlockSpec((1, 1) + coef.shape[2:], lambda p, *_: (0, p, 0, 0, 0)),
+        pl.BlockSpec(field.shape, lambda p, *_: (0, 0, 0)),
+    ]
+    operands = [coef, field]
+    aliases = {}
+    if before is not None:
+        in_specs.append(HBM)
+        operands.append(before)
+        aliases = {5: 0}
+    return pl.pallas_call(
+        functools.partial(interp_kernel, tiles),
+        grid_spec=pltpu.PrefetchScalarGridSpec(
+            num_scalar_prefetch=3,
+            grid=(count,),
+            in_specs=in_specs,
+            out_specs=pl.BlockSpec((levels, CHUNK, size), place_out),
+        ),
+        out_shape=jax.ShapeDtypeStruct(shape, BF16),
+        input_output_aliases=aliases,
+        compiler_params=params(),
+        name="interpolate",
+    )(place, send, slots, *operands)
+
 
 def local(
+    control, node_count, vert_coef, send_list, conv_slots, conv_coef, interp_slots, interp_coef
+):
+    nodes, levels, members = control.shape
+    _, blocks, taps, size, _ = conv_coef.shape
+    tiles = lax.axis_size("tile")
+    halves = lax.axis_size("sub")
+    points = interp_coef.shape[1] * size
+    t, lev, sub, grp = (lax.axis_index(n) for n in ("tile", "lev", "sub", "grp"))
+    place = jnp.stack([t, lev, sub]).astype(jnp.int32)
+    chunks = members // CHUNK
+    rows = levels * CHUNK
+    entries = blocks + tiles - 1
+    swap = [(0, 1), (1, 0)]
+    right = [(i, i + 1) for i in range(tiles - 1)]
+    left = [(i + 1, i) for i in range(tiles - 1)]
+
+    state = control.transpose(1, 2, 0)
+    mine = [state[:, c * CHUNK : (c + 1) * CHUNK].reshape(rows, nodes) for c in range(chunks)]
+    theirs = [lax.ppermute(x, "lev", swap) for x in mine]
+
+    merged = pl.pallas_call(
+        functools.partial(merge_kernel, tiles),
+        in_specs=[SMEM, SMEM, SMEM, VMEM],
+        out_specs=VMEM,
+        out_shape=jax.ShapeDtypeStruct((blocks, entries, size, size), BF16),
+        scratch_shapes=[pltpu.VMEM((blocks, entries, size, size), F32)],
+        compiler_params=params(),
+        name="merge_taps",
+    )(place, send_list, conv_slots, conv_coef[0])
+
+    shares = lax.axis_size("grp") * lax.axis_size("lev") * halves
+    share = (grp * lax.axis_size("lev") + lev) * halves + sub
+    part = size // shares
+    pieces = []
+    for d in range(1, tiles):
+        target = lax.rem(t + d, tiles)
+        block = send_list[t, target, 0]
+        piece = lax.dynamic_slice(
+            merged, (block, 0, share * part, 0), (1, entries, part, size)
+        )[0]
+        ring = [(i, (i + d) % tiles) for i in range(tiles)]
+        pieces.append(lax.ppermute(piece, "tile", ring))
+    coef_lent = lax.all_gather(jnp.stack(pieces), ("grp", "lev", "sub"))
+
+    weight = pl.pallas_call(
+        functools.partial(weight_kernel, levels),
+        in_specs=[SMEM, VMEM],
+        out_specs=VMEM,
+        out_shape=jax.ShapeDtypeStruct((2, rows, rows), BF16),
+        compiler_params=params(),
+        name="level_weights",
+    )(place, vert_coef)
+
+    result = None
+    for c in range(chunks):
+        vertical = pl.pallas_call(
+            vertical_kernel,
+            in_specs=[SMEM, VMEM, VMEM, VMEM],
+            out_specs=VMEM,
+            out_shape=jax.ShapeDtypeStruct((blocks, rows, size), BF16),
+            compiler_params=params(),
+            name="vertical",
+        )(node_count, weight, mine[c], theirs[c])
+        rights, lefts = [vertical], [vertical]
+        for hop in range(tiles - 1):
+            rights.append(lax.ppermute(rights[-1], "tile", right[hop:]))
+            lefts.append(lax.ppermute(lefts[-1], "tile", left[: tiles - 1 - hop]))
+        fields = pl.pallas_call(
+            functools.partial(spread_kernel, tiles),
+            in_specs=[SMEM, SMEM, VMEM, VMEM] + [HBM] * (2 * tiles - 1),
+            out_specs=VMEM,
+            out_shape=jax.ShapeDtypeStruct((entries, rows, size), BF16),
+            scratch_shapes=[
+                pltpu.VMEM((tiles, blocks, rows, size), BF16),
+                pltpu.SemaphoreType.DMA((tiles,)),
+            ],
+            compiler_params=params(),
+            name="spread",
+        )(place, send_list, merged, coef_lent, vertical, *rights[1:], *lefts[1:])
+        other = lax.ppermute(fields, "sub", swap)
+        shape = (levels, halves * members, points)
+        for half, field in enumerate((fields, other)):
+            result = interpolate(
+                c, half, tiles, place, send_list, interp_slots, interp_coef, field, shape, result
+            )
+    return result.transpose(2, 0, 1)
+
+
+def plain(
     control, node_count, vert_coef, send_list, conv_slots, conv_coef, interp_slots, interp_coef
 ):
     node_rows, level_rows, member_rows = control.shape
@@ -64,8 +313,9 @@
         P("tile", None, None),
         P(("tile", "sub"), None, None, None, None),
     )
+    short = mesh.shape["tile"] <= 4 and mesh.shape["lev"] == 2 and mesh.shape["sub"] == 2
     return jax.shard_map(
-        local,
+        local if short else plain,
         mesh=mesh,
         in_specs=placed,
         out_specs=P(("tile", "sub"), "lev", "grp"),

time: 431 us -> 190 us (0.44)
  waiting for transfers between devices: 294 us -> 70.4 us
  local copies, waits for them, and re-layouts: 89.3 us -> 16.6 us
  starting transfers between devices: 0.31 us -> 44.4 us
  Pallas kernels: 0 us -> 36.8 us
  matrix products: 21.4 us -> 0 us
  other arithmetic: 11.2 us -> 0.82 us
  between operations: 14 us -> 20.1 us
    all_gather x3 -> x1, waiting for transfers between devices: 248 us -> 0.01 us  [local(): coef_lent = lax.all_gather(jnp.stack(pieces), ('grp', 'lev', 'sub'))]
    ppermute x0 -> x27, waiting for transfers between devices: none -> 70.4 us  [the longest x9 35.8 us: local(): lefts.append(lax.ppermute(lefts[-1], 'tile', left[:tiles - 1 - hop]))]
    convert_element_type x4 -> x0, local copies, waits for them, and re-layouts: 46.1 us -> none  [the longest x3 43.6 us: local(): return shaped.transpose(0, 2, 1, 3).reshape(point_rows, level_rows, halve...]
    reduce_scatter x1 -> x0, waiting for transfers between devices: 45.5 us -> none  [local(): lax.psum_scatter(partial_value.astype(jnp.bfloat16), 'lev', scatter_dimen...]
    ppermute x0 -> x27, starting transfers between devices: none -> 44.4 us  [the longest x9 19.2 us: local(): rights.append(lax.ppermute(rights[-1], 'tile', right[hop:]))]
    pallas_call x0 -> x14, Pallas kernels: none -> 36.8 us  [the longest x6 17.8 us: interpolate(): pl.pallas_call(functools.partial(interp_kernel, tiles), grid_spec=pltpu.P...]
    gather x4 -> x0, local copies, waits for them, and re-layouts: 30.4 us -> none  [the longest x1 10.6 us: local(): picked = members_all[own_slots]]
    dot_general x3 -> x0, matrix products: 21.4 us -> none  [the longest x1 10.2 us: local(): jnp.einsum('bkij,bkjc->bic', conv_coef[0], chosen, preferred_element_type...]
  transfers between devices with their start and end apart: 4 -> 28, of which waited for: 4 -> 11; matrix products, arithmetic and copies ran while one was open for 0% -> 0% of each run, Pallas kernels for 0% -> 17%
where the time goes in v1:
time: 190 us; the launch traced here: 189 us
  waiting for transfers between devices  70.4 us (37%)
  starting transfers between devices  44.4 us (23%)
  Pallas kernels  36.8 us (19%)
  between operations  20.1 us (11%)
  local copies, waits for them, and re-layouts  16.6 us (9%)
    ppermute x9, waiting for transfers between devices, local(): lefts.append(lax.ppermute(lefts[-1], 'tile', left[:tiles - 1 - hop]))  35.8 us
    ppermute x3, waiting for transfers between devices, local(): theirs = [lax.ppermute(x, 'lev', swap) for x in mine]  27 us
    ppermute x9, starting transfers between devices, local(): rights.append(lax.ppermute(rights[-1], 'tile', right[hop:]))  19.2 us
    pallas_call x6, Pallas kernels, interpolate(): pl.pallas_call(functools.partial(interp_kernel, tiles), grid_spec=pltpu.P...  17.8 us
    unnamed x44, local copies, waits for them, and re-layouts  15.1 us
    pallas_call x3, Pallas kernels, local(): pl.pallas_call(functools.partial(spread_kernel, tiles), in_specs=[SMEM, S...  14.4 us
    ppermute x9, starting transfers between devices, local(): lefts.append(lax.ppermute(lefts[-1], 'tile', left[:tiles - 1 - hop]))  11.6 us
    ppermute x3, waiting for transfers between devices, local(): pieces.append(lax.ppermute(piece, 'tile', ring))  7.58 us
  transfers between devices with their start and end apart: 28, of which 11 were waited for; matrix products, arithmetic and copies ran while one was open for 0% of the time, Pallas kernels for 17%

profile of v1, /device:TPU:1, one launch (start us, length us, event | category | flops | bytes accessed | tf_op | source)
XLA Modules:
  0.0 189.1 jit_solution(16828399502916492932)
XLA Ops:
  6.5 1.4 constant_dynamic-slice_fusion.2
  14.5 1.7 copy-done.2
  16.9 1.4 merge_taps.1.coef_own
  18.3 2.2 %collective-permute-start = (bf16[5,32,256]{2,1,0:T(8,128)(2,1)S(1)}, bf16[5,32,256]{2,1,0:T(8,128)(2,1)S(1)}, u32[]{:S(2)}, u32[]{:S(2)}) collective-permute-start(bf16[5,32,256]{2,1,0:T(8,128)(2,1)S(1)} %get-tuple-element.8), channel_id=1, source_target_pairs={{0,4},{4,8},{8,12},{12,0},{1,5},{5,9},{9,13},{13,1},{2,6},{6,10},{... | collective-permute-start | bytes 245768 | tf_op jit(solution)/shard_map/ppermute | solution.py:209
  20.5 2.1 %collective-permute-start.2 = (bf16[5,32,256]{2,1,0:T(8,128)(2,1)S(1)}, bf16[5,32,256]{2,1,0:T(8,128)(2,1)S(1)}, u32[]{:S(2)}, u32[]{:S(2)}) collective-permute-start(bf16[5,32,256]{2,1,0:T(8,128)(2,1)S(1)} %get-tuple-element.9), channel_id=1, source_target_pairs={{0,12},{4,0},{8,4},{12,8},{1,13},{5,1},{9,5},{13,9},{2,14},{6,2},{... | collective-permute-start | bytes 245768 | tf_op jit(solution)/shard_map/ppermute | solution.py:209
  23.0 1.7 collective-permute-done
  24.7 1.3 collective-permute-done.2
  26.0 4.6 %collective-permute-done.1 = bf16[5,32,256]{2,1,0:T(8,128)(2,1)S(1)} collective-permute-done((bf16[5,32,256]{2,1,0:T(8,128)(2,1)S(1)}, bf16[5,32,256]{2,1,0:T(8,128)(2,1)S(1)}, u32[]{:S(2)}, u32[]{:S(2)}) %collective-permute-start.1) | collective-permute-done | bytes 81952 | tf_op jit(solution)/shard_map/ppermute | solution.py:209
  34.6 1.1 level_weights.1.weight
  35.7 11.3 %collective-permute-done.11.other = bf16[512,512]{1,0:T(8,128)(2,1)S(1)} collective-permute-done((bf16[512,512]{1,0:T(8,128)(2,1)S(1)}, bf16[512,512]{1,0:T(8,128)(2,1)S(1)}, u32[]{:S(2)}, u32[]{:S(2)}) %collective-permute-start.11) | collective-permute-done | bytes 524320 | tf_op jit(solution)/shard_map/ppermute | solution.py:186
  47.8 1.3 collective-permute-start.15
  49.1 4.0 %collective-permute-start.12 = (bf16[2,512,256]{2,1,0:T(8,128)(2,1)S(1)}, bf16[2,512,256]{2,1,0:T(8,128)(2,1)S(1)}, u32[]{:S(2)}, u32[]{:S(2)}) collective-permute-start(bf16[2,512,256]{2,1,0:T(8,128)(2,1)S(1)} %vertical.4.own), channel_id=1, source_target_pairs={{0,4},{4,8},{8,12},{1,5},{5,9},{9,13},{2,6},{6,10},{10,14},{3,7},{... | collective-permute-start | bytes 1572872 | tf_op jit(solution)/shard_map/ppermute | solution.py:233
  53.1 9.1 %collective-permute-done.19.other = bf16[512,512]{1,0:T(8,128)(2,1)S(1)} collective-permute-done((bf16[512,512]{1,0:T(8,128)(2,1)S(1)}, bf16[512,512]{1,0:T(8,128)(2,1)S(1)}, u32[]{:S(2)}, u32[]{:S(2)}) %collective-permute-start.19) | collective-permute-done | bytes 524320 | tf_op jit(solution)/shard_map/ppermute | solution.py:186
  62.9 1.3 collective-permute-start.23
  64.2 4.0 %collective-permute-start.20 = (bf16[2,512,256]{2,1,0:T(8,128)(2,1)S(1)}, bf16[2,512,256]{2,1,0:T(8,128)(2,1)S(1)}, u32[]{:S(2)}, u32[]{:S(2)}) collective-permute-start(bf16[2,512,256]{2,1,0:T(8,128)(2,1)S(1)} %vertical.5.own), channel_id=1, source_target_pairs={{0,4},{4,8},{8,12},{1,5},{5,9},{9,13},{2,6},{6,10},{10,14},{3,7},{... | collective-permute-start | bytes 1572872 | tf_op jit(solution)/shard_map/ppermute | solution.py:233
  68.2 6.6 %collective-permute-done.3.other = bf16[512,512]{1,0:T(8,128)(2,1)S(1)} collective-permute-done((bf16[512,512]{1,0:T(8,128)(2,1)S(1)}, bf16[512,512]{1,0:T(8,128)(2,1)S(1)}, u32[]{:S(2)}, u32[]{:S(2)}) %collective-permute-start.3) | collective-permute-done | bytes 524320 | tf_op jit(solution)/shard_map/ppermute | solution.py:186
  75.5 1.3 collective-permute-start.7
  76.8 4.0 %collective-permute-start.4 = (bf16[2,512,256]{2,1,0:T(8,128)(2,1)S(1)}, bf16[2,512,256]{2,1,0:T(8,128)(2,1)S(1)}, u32[]{:S(2)}, u32[]{:S(2)}) collective-permute-start(bf16[2,512,256]{2,1,0:T(8,128)(2,1)S(1)} %vertical.3.own), channel_id=1, source_target_pairs={{0,4},{4,8},{8,12},{1,5},{5,9},{9,13},{2,6},{6,10},{10,14},{3,7},{... | collective-permute-start | bytes 1572872 | tf_op jit(solution)/shard_map/ppermute | solution.py:233
  80.8 1.3 collective-permute-start.16
  82.2 1.3 collective-permute-start.24
  85.8 3.5 %collective-permute-done.7.rest_3_ = bf16[2,512,256]{2,1,0:T(8,128)(2,1)S(1)} collective-permute-done((bf16[2,512,256]{2,1,0:T(8,128)(2,1)S(1)}, bf16[2,512,256]{2,1,0:T(8,128)(2,1)S(1)}, u32[]{:S(2)}, u32[]{:S(2)}) %collective-permute-start.7) | collective-permute-done | bytes 524320 | tf_op jit(solution)/shard_map/ppermute | solution.py:234
  89.3 1.5 collective-permute-start.13
  90.8 1.3 collective-permute-start.8
  92.1 8.6 %collective-permute-done.16.rest_4_ = bf16[2,512,256]{2,1,0:T(8,128)(2,1)} collective-permute-done((bf16[2,512,256]{2,1,0:T(8,128)(2,1)S(1)}, bf16[2,512,256]{2,1,0:T(8,128)(2,1)}, u32[]{:S(2)}, u32[]{:S(2)}) %collective-permute-start.16) | collective-permute-done | bytes 524320 | tf_op jit(solution)/shard_map/ppermute | solution.py:234
  100.7 1.5 collective-permute-start.5
  102.9 8.9 %collective-permute-done.24.rest_4_ = bf16[2,512,256]{2,1,0:T(8,128)(2,1)S(1)} collective-permute-done((bf16[2,512,256]{2,1,0:T(8,128)(2,1)S(1)}, bf16[2,512,256]{2,1,0:T(8,128)(2,1)S(1)}, u32[]{:S(2)}, u32[]{:S(2)}) %collective-permute-start.24) | collective-permute-done | bytes 524320 | tf_op jit(solution)/shard_map/ppermute | solution.py:234
  111.8 1.3 collective-permute-start.25
  115.4 1.3 collective-permute-start.17
  116.7 6.4 %collective-permute-done.8.rest_4_ = bf16[2,512,256]{2,1,0:T(8,128)(2,1)} collective-permute-done((bf16[2,512,256]{2,1,0:T(8,128)(2,1)S(1)}, bf16[2,512,256]{2,1,0:T(8,128)(2,1)}, u32[]{:S(2)}, u32[]{:S(2)}) %collective-permute-start.8) | collective-permute-done | bytes 524320 | tf_op jit(solution)/shard_map/ppermute | solution.py:234
  123.1 1.5 collective-permute-start.14
  124.6 1.3 collective-permute-start.9
  125.9 8.4 %collective-permute-done.25.rest_5_ = bf16[2,512,256]{2,1,0:T(8,128)(2,1)S(1)} collective-permute-done((bf16[2,512,256]{2,1,0:T(8,128)(2,1)S(1)}, bf16[2,512,256]{2,1,0:T(8,128)(2,1)S(1)}, u32[]{:S(2)}, u32[]{:S(2)}) %collective-permute-start.25) | collective-permute-done | bytes 524320 | tf_op jit(solution)/shard_map/ppermute | solution.py:234
  135.1 1.5 collective-permute-start.6
  137.3 1.0 copy-done.6
  138.4 1.0 copy-done.8
  140.5 1.0 copy-done.12
  141.5 1.0 copy-done.14
  143.6 4.1 %spread.5.field = bf16[5,512,256]{2,1,0:T(8,128)(2,1)S(1)} custom-call(s32[3]{0:T(128)S(1)} %pad_add_fusion.place, s32[4,4,1]{2,1,0:T(4,128)S(1)} %copy.44.send, bf16[2,5,256,256]{3,2,1,0:T(8,128)(2,1)} %copy-done.1, bf16[8,3,5,32,256]{4,3,2,1,0:T(8,128)(2,1)} %bitcast.29, bf16[2,512,256]{2,1,0:T(8,128)(2,1)S(1)} %vertical.5.own, ...), custom_call_target="tpu_custom_call" | custom-call | tf_op jit(solution)/shard_map/spread/pallas_call | solution.py:235
  147.7 4.5 %collective-permute-start.26 = (bf16[5,512,256]{2,1,0:T(8,128)(2,1)S(1)}, bf16[5,512,256]{2,1,0:T(8,128)(2,1)S(1)}, u32[]{:S(2)}, u32[]{:S(2)}) collective-permute-start(bf16[5,512,256]{2,1,0:T(8,128)(2,1)S(1)} %spread.5.field), channel_id=1, source_target_pairs={{0,1},{1,0},{2,3},{3,2},{4,5},{5,4},{6,7},{7,6},{8,9},{9,8},{10,11... | collective-permute-start | bytes 3932168 | tf_op jit(solution)/shard_map/ppermute | solution.py:247
  152.2 5.1 %spread.4.field = bf16[5,512,256]{2,1,0:T(8,128)(2,1)S(1)} custom-call(s32[3]{0:T(128)S(1)} %pad_add_fusion.place, s32[4,4,1]{2,1,0:T(4,128)S(1)} %copy.44.send, bf16[2,5,256,256]{3,2,1,0:T(8,128)(2,1)} %copy-done.1, bf16[8,3,5,32,256]{4,3,2,1,0:T(8,128)(2,1)} %bitcast.30, bf16[2,512,256]{2,1,0:T(8,128)(2,1)S(1)} %vertical.4.own, ...), custom_call_target="tpu_custom_call" | custom-call | tf_op jit(solution)/shard_map/spread/pallas_call | solution.py:235
  157.5 5.2 %spread.3.field = bf16[5,512,256]{2,1,0:T(8,128)(2,1)S(1)} custom-call(s32[3]{0:T(128)S(1)} %pad_add_fusion.place, s32[4,4,1]{2,1,0:T(4,128)S(1)} %copy.44.send, bf16[2,5,256,256]{3,2,1,0:T(8,128)(2,1)} %copy-done.1, bf16[8,3,5,32,256]{4,3,2,1,0:T(8,128)(2,1)} %bitcast.31, bf16[2,512,256]{2,1,0:T(8,128)(2,1)S(1)} %vertical.3.own, ...), custom_call_target="tpu_custom_call" | custom-call | tf_op jit(solution)/shard_map/spread/pallas_call | solution.py:235
  162.7 1.8 collective-permute-start.10
  164.5 3.0 %interpolate.6.rest_0_ = bf16[32,96,768]{2,1,0:T(8,128)(2,1)} custom-call(s32[3]{0:T(128)S(1)} %pad_add_fusion.place, s32[4,4,1]{2,1,0:T(4,128)S(1)} %copy.44.send, s32[2,3,3]{2,1,0:T(4,128)S(1)} %copy.45.slots, bf16[1,3,3,256,256]{4,3,2,1,0:T(8,128)(2,1)S(1)} %copy-done, bf16[5,512,256]{2,1,0:T(8,128)(2,1)S(1)} %spread.5.field), custom_call_target="tpu_custom_call" | custom-call | tf_op jit(solution)/shard_map/interpolate/pallas_call | solution.py:152
  167.4 3.0 %interpolate.7.rest_0_ = bf16[32,96,768]{2,1,0:T(8,128)(2,1)} custom-call(s32[3]{0:T(128)S(1)} %pad_add_fusion.place, s32[4,4,1]{2,1,0:T(4,128)S(1)} %copy.44.send, s32[2,3,3]{2,1,0:T(4,128)S(1)} %copy.45.slots, bf16[1,3,3,256,256]{4,3,2,1,0:T(8,128)(2,1)S(1)} %copy-done, ...), custom_call_target="tpu_custom_call", output_to_operand_aliasing={{}: (5, {})} | custom-call | tf_op jit(solution)/shard_map/interpolate/pallas_call | solution.py:152
  170.4 3.0 %interpolate.8.rest_0_ = bf16[32,96,768]{2,1,0:T(8,128)(2,1)} custom-call(s32[3]{0:T(128)S(1)} %pad_add_fusion.place, s32[4,4,1]{2,1,0:T(4,128)S(1)} %copy.44.send, s32[2,3,3]{2,1,0:T(4,128)S(1)} %copy.45.slots, bf16[1,3,3,256,256]{4,3,2,1,0:T(8,128)(2,1)S(1)} %copy-done, bf16[5,512,256]{2,1,0:T(8,128)(2,1)S(1)} %spread.4.field, ...), custom_call_target="tpu_custom_call", output_to_operand_aliasing={{}: (5, {})} | custom-call | tf_op jit(solution)/shard_map/interpolate/pallas_call | solution.py:152
  173.4 3.0 %interpolate.9.rest_0_ = bf16[32,96,768]{2,1,0:T(8,128)(2,1)} custom-call(s32[3]{0:T(128)S(1)} %pad_add_fusion.place, s32[4,4,1]{2,1,0:T(4,128)S(1)} %copy.44.send, s32[2,3,3]{2,1,0:T(4,128)S(1)} %copy.45.slots, bf16[1,3,3,256,256]{4,3,2,1,0:T(8,128)(2,1)S(1)} %copy-done, ...), custom_call_target="tpu_custom_call", output_to_operand_aliasing={{}: (5, {})} | custom-call | tf_op jit(solution)/shard_map/interpolate/pallas_call | solution.py:152
  176.4 3.0 %interpolate.10.rest_0_ = bf16[32,96,768]{2,1,0:T(8,128)(2,1)} custom-call(s32[3]{0:T(128)S(1)} %pad_add_fusion.place, s32[4,4,1]{2,1,0:T(4,128)S(1)} %copy.44.send, s32[2,3,3]{2,1,0:T(4,128)S(1)} %copy.45.slots, bf16[1,3,3,256,256]{4,3,2,1,0:T(8,128)(2,1)S(1)} %copy-done, bf16[5,512,256]{2,1,0:T(8,128)(2,1)S(1)} %spread.3.field, ...), custom_call_target="tpu_custom_call", output_to_operand_aliasing={{}: (5, {})} | custom-call | tf_op jit(solution)/shard_map/interpolate/pallas_call | solution.py:152
  179.3 3.0 %interpolate.11 = bf16[32,96,768]{2,1,0:T(8,128)(2,1)} custom-call(s32[3]{0:T(128)S(1)} %pad_add_fusion.place, s32[4,4,1]{2,1,0:T(4,128)S(1)} %copy.44.send, s32[2,3,3]{2,1,0:T(4,128)S(1)} %copy.45.slots, bf16[1,3,3,256,256]{4,3,2,1,0:T(8,128)(2,1)S(1)} %copy-done, ...), custom_call_target="tpu_custom_call", output_to_operand_aliasing={{}: (5, {})} | custom-call | tf_op jit(solution)/shard_map/interpolate/pallas_call | solution.py:152
  (72 shorter events, 16.7 us)
Async XLA Ops:
  6.5 130.8 %all-gather.3.cloned.1.call-start = ((), (), s32[]{:S(2)}) async-start(), calls=%async_computation | async-start | bytes 2211840 | tf_op jit(solution)/shard_map/all_gather | solution.py:210
  14.5 1.7 copy-start.2
  16.9 14.5 %copy-start.19 = (bf16[512,32,48]{0,2,1:T(8,128)(2,1)S(1)}, bf16[512,32,48]{0,2,1:T(8,128)(2,1)}, u32[]{:S(2)}) copy-start(bf16[512,32,48]{0,2,1:T(8,128)(2,1)} %param.8) | copy-start | bytes 4718596
  18.3 13.2 %copy-start.1 = (bf16[2,5,256,256]{3,2,1,0:T(8,128)(2,1)}, bf16[2,5,256,256]{3,2,1,0:T(8,128)(2,1)S(1)}, u32[]{:S(2)}) copy-start(bf16[2,5,256,256]{3,2,1,0:T(8,128)(2,1)S(1)} %merge_taps.1.coef_own) | copy-start | bytes 3932164
  18.3 6.4 %collective-permute-start = (bf16[5,32,256]{2,1,0:T(8,128)(2,1)S(1)}, bf16[5,32,256]{2,1,0:T(8,128)(2,1)S(1)}, u32[]{:S(2)}, u32[]{:S(2)}) collective-permute-start(bf16[5,32,256]{2,1,0:T(8,128)(2,1)S(1)} %get-tuple-element.8), channel_id=1, source_target_pairs={{0,4},{4,8},{8,12},{12,0},{1,5},{5,9},{9,13},{13,1},{2,6},{6,10},{... | collective-permute-start | bytes 245768 | tf_op jit(solution)/shard_map/ppermute | solution.py:209
  20.5 5.5 %collective-permute-start.2 = (bf16[5,32,256]{2,1,0:T(8,128)(2,1)S(1)}, bf16[5,32,256]{2,1,0:T(8,128)(2,1)S(1)}, u32[]{:S(2)}, u32[]{:S(2)}) collective-permute-start(bf16[5,32,256]{2,1,0:T(8,128)(2,1)S(1)} %get-tuple-element.9), channel_id=1, source_target_pairs={{0,12},{4,0},{8,4},{12,8},{1,13},{5,1},{9,5},{13,9},{2,14},{6,2},{... | collective-permute-start | bytes 245768 | tf_op jit(solution)/shard_map/ppermute | solution.py:209
  22.6 8.0 %collective-permute-start.1 = (bf16[5,32,256]{2,1,0:T(8,128)(2,1)S(1)}, bf16[5,32,256]{2,1,0:T(8,128)(2,1)S(1)}, u32[]{:S(2)}, u32[]{:S(2)}) collective-permute-start(bf16[5,32,256]{2,1,0:T(8,128)(2,1)S(1)} %get-tuple-element.10), channel_id=1, source_target_pairs={{0,8},{4,12},{8,0},{12,4},{1,9},{5,13},{9,1},{13,5},{2,10},{6,14},... | collective-permute-start | bytes 245768 | tf_op jit(solution)/shard_map/ppermute | solution.py:209
  31.4 3.3 %copy-start.17 = (bf16[64,64]{1,0:T(8,128)(2,1)S(1)}, bf16[64,64]{1,0:T(8,128)(2,1)}, u32[]{:S(2)}) copy-start(bf16[64,64]{1,0:T(8,128)(2,1)} %vert.1) | copy-start | bytes 24580
  31.5 15.5 %collective-permute-start.11 = (bf16[512,512]{1,0:T(8,128)(2,1)S(1)}, bf16[512,512]{1,0:T(8,128)(2,1)S(1)}, u32[]{:S(2)}, u32[]{:S(2)}) collective-permute-start(bf16[512,512]{1,0:T(8,128)(2,1)S(1)} %bitcast.27), channel_id=1, source_target_pairs={{0,2},{2,0},{1,3},{3,1},{4,6},{6,4},{5,7},{7,5},{8,10},{10,8},{9,1... | collective-permute-start | bytes 1572872 | tf_op jit(solution)/shard_map/ppermute | solution.py:186
  32.5 29.6 %collective-permute-start.19 = (bf16[512,512]{1,0:T(8,128)(2,1)S(1)}, bf16[512,512]{1,0:T(8,128)(2,1)S(1)}, u32[]{:S(2)}, u32[]{:S(2)}) collective-permute-start(bf16[512,512]{1,0:T(8,128)(2,1)S(1)} %bitcast.25), channel_id=1, source_target_pairs={{0,2},{2,0},{1,3},{3,1},{4,6},{6,4},{5,7},{7,5},{8,10},{10,8},{9,1... | collective-permute-start | bytes 1572872 | tf_op jit(solution)/shard_map/ppermute | solution.py:186
  33.0 41.8 %collective-permute-start.3 = (bf16[512,512]{1,0:T(8,128)(2,1)S(1)}, bf16[512,512]{1,0:T(8,128)(2,1)S(1)}, u32[]{:S(2)}, u32[]{:S(2)}) collective-permute-start(bf16[512,512]{1,0:T(8,128)(2,1)S(1)} %bitcast.23), channel_id=1, source_target_pairs={{0,2},{2,0},{1,3},{3,1},{4,6},{6,4},{5,7},{7,5},{8,10},{10,8},{9,1... | collective-permute-start | bytes 1572872 | tf_op jit(solution)/shard_map/ppermute | solution.py:186
  47.8 29.0 %collective-permute-start.15 = (bf16[2,512,256]{2,1,0:T(8,128)(2,1)S(1)}, bf16[2,512,256]{2,1,0:T(8,128)(2,1)S(1)}, u32[]{:S(2)}, u32[]{:S(2)}) collective-permute-start(bf16[2,512,256]{2,1,0:T(8,128)(2,1)S(1)} %vertical.4.own), channel_id=1, source_target_pairs={{4,0},{8,4},{12,8},{5,1},{9,5},{13,9},{6,2},{10,6},{14,10},{7,3},{... | collective-permute-start | bytes 1572872 | tf_op jit(solution)/shard_map/ppermute | solution.py:234
  49.1 31.8 %collective-permute-start.12 = (bf16[2,512,256]{2,1,0:T(8,128)(2,1)S(1)}, bf16[2,512,256]{2,1,0:T(8,128)(2,1)S(1)}, u32[]{:S(2)}, u32[]{:S(2)}) collective-permute-start(bf16[2,512,256]{2,1,0:T(8,128)(2,1)S(1)} %vertical.4.own), channel_id=1, source_target_pairs={{0,4},{4,8},{8,12},{1,5},{5,9},{9,13},{2,6},{6,10},{10,14},{3,7},{... | collective-permute-start | bytes 1572872 | tf_op jit(solution)/shard_map/ppermute | solution.py:233
  62.9 19.3 %collective-permute-start.23 = (bf16[2,512,256]{2,1,0:T(8,128)(2,1)S(1)}, bf16[2,512,256]{2,1,0:T(8,128)(2,1)S(1)}, u32[]{:S(2)}, u32[]{:S(2)}) collective-permute-start(bf16[2,512,256]{2,1,0:T(8,128)(2,1)S(1)} %vertical.5.own), channel_id=1, source_target_pairs={{4,0},{8,4},{12,8},{5,1},{9,5},{13,9},{6,2},{10,6},{14,10},{7,3},{... | collective-permute-start | bytes 1572872 | tf_op jit(solution)/shard_map/ppermute | solution.py:234
  64.2 20.1 %collective-permute-start.20 = (bf16[2,512,256]{2,1,0:T(8,128)(2,1)S(1)}, bf16[2,512,256]{2,1,0:T(8,128)(2,1)S(1)}, u32[]{:S(2)}, u32[]{:S(2)}) collective-permute-start(bf16[2,512,256]{2,1,0:T(8,128)(2,1)S(1)} %vertical.5.own), channel_id=1, source_target_pairs={{0,4},{4,8},{8,12},{1,5},{5,9},{9,13},{2,6},{6,10},{10,14},{3,7},{... | collective-permute-start | bytes 1572872 | tf_op jit(solution)/shard_map/ppermute | solution.py:233
  75.5 13.8 %collective-permute-start.7 = (bf16[2,512,256]{2,1,0:T(8,128)(2,1)S(1)}, bf16[2,512,256]{2,1,0:T(8,128)(2,1)S(1)}, u32[]{:S(2)}, u32[]{:S(2)}) collective-permute-start(bf16[2,512,256]{2,1,0:T(8,128)(2,1)S(1)} %vertical.3.own), channel_id=1, source_target_pairs={{4,0},{8,4},{12,8},{5,1},{9,5},{13,9},{6,2},{10,6},{14,10},{7,3},{... | collective-permute-start | bytes 1572872 | tf_op jit(solution)/shard_map/ppermute | solution.py:234
  76.8 14.0 %collective-permute-start.4 = (bf16[2,512,256]{2,1,0:T(8,128)(2,1)S(1)}, bf16[2,512,256]{2,1,0:T(8,128)(2,1)S(1)}, u32[]{:S(2)}, u32[]{:S(2)}) collective-permute-start(bf16[2,512,256]{2,1,0:T(8,128)(2,1)S(1)} %vertical.3.own), channel_id=1, source_target_pairs={{0,4},{4,8},{8,12},{1,5},{5,9},{9,13},{2,6},{6,10},{10,14},{3,7},{... | collective-permute-start | bytes 1572872 | tf_op jit(solution)/shard_map/ppermute | solution.py:233
  80.8 19.8 %collective-permute-start.16 = (bf16[2,512,256]{2,1,0:T(8,128)(2,1)S(1)}, bf16[2,512,256]{2,1,0:T(8,128)(2,1)}, u32[]{:S(2)}, u32[]{:S(2)}) collective-permute-start(bf16[2,512,256]{2,1,0:T(8,128)(2,1)S(1)} %collective-permute-done.15.rest_3_), channel_id=1, source_target_pairs={{4,0},{8,4},{5,1},{9,5},{6,2},{10,6},{7,3},{11,7},{20,16},{24,20},... | collective-permute-start | bytes 1572872 | tf_op jit(solution)/shard_map/ppermute | solution.py:234
  82.2 29.6 %collective-permute-start.24 = (bf16[2,512,256]{2,1,0:T(8,128)(2,1)S(1)}, bf16[2,512,256]{2,1,0:T(8,128)(2,1)S(1)}, u32[]{:S(2)}, u32[]{:S(2)}) collective-permute-start(bf16[2,512,256]{2,1,0:T(8,128)(2,1)S(1)} %collective-permute-done.23.rest_3_), channel_id=1, source_target_pairs={{4,0},{8,4},{5,1},{9,5},{6,2},{10,6},{7,3},{11,7},{20,16},{24,20},... | collective-permute-start | bytes 1572872 | tf_op jit(solution)/shard_map/ppermute | solution.py:234
  83.5 0.8 copy-start.5
  84.3 29.6 %collective-permute-start.21 = (bf16[2,512,256]{2,1,0:T(8,128)(2,1)S(1)}, bf16[2,512,256]{2,1,0:T(8,128)(2,1)S(1)}, u32[]{:S(2)}, u32[]{:S(2)}) collective-permute-start(bf16[2,512,256]{2,1,0:T(8,128)(2,1)S(1)} %collective-permute-done.20.rest_0_), channel_id=1, source_target_pairs={{4,8},{8,12},{5,9},{9,13},{6,10},{10,14},{7,11},{11,15},{20,24},{2... | collective-permute-start | bytes 1572872 | tf_op jit(solution)/shard_map/ppermute | solution.py:233
  85.0 0.8 copy-start.7
  89.3 26.1 %collective-permute-start.13 = (bf16[2,512,256]{2,1,0:T(8,128)(2,1)S(1)}, bf16[2,512,256]{2,1,0:T(8,128)(2,1)}, u32[]{:S(2)}, u32[]{:S(2)}) collective-permute-start(bf16[2,512,256]{2,1,0:T(8,128)(2,1)S(1)} %collective-permute-done.12.rest_0_), channel_id=1, source_target_pairs={{4,8},{8,12},{5,9},{9,13},{6,10},{10,14},{7,11},{11,15},{20,24},{2... | collective-permute-start | bytes 1572872 | tf_op jit(solution)/shard_map/ppermute | solution.py:233
  90.8 32.4 %collective-permute-start.8 = (bf16[2,512,256]{2,1,0:T(8,128)(2,1)S(1)}, bf16[2,512,256]{2,1,0:T(8,128)(2,1)}, u32[]{:S(2)}, u32[]{:S(2)}) collective-permute-start(bf16[2,512,256]{2,1,0:T(8,128)(2,1)S(1)} %collective-permute-done.7.rest_3_), channel_id=1, source_target_pairs={{4,0},{8,4},{5,1},{9,5},{6,2},{10,6},{7,3},{11,7},{20,16},{24,20},... | collective-permute-start | bytes 1572872 | tf_op jit(solution)/shard_map/ppermute | solution.py:234
  100.7 23.9 %collective-permute-start.5 = (bf16[2,512,256]{2,1,0:T(8,128)(2,1)S(1)}, bf16[2,512,256]{2,1,0:T(8,128)(2,1)}, u32[]{:S(2)}, u32[]{:S(2)}) collective-permute-start(bf16[2,512,256]{2,1,0:T(8,128)(2,1)S(1)} %collective-permute-done.4.rest_0_), channel_id=1, source_target_pairs={{4,8},{8,12},{5,9},{9,13},{6,10},{10,14},{7,11},{11,15},{20,24},{2... | collective-permute-start | bytes 1572872 | tf_op jit(solution)/shard_map/ppermute | solution.py:233
  102.1 0.8 copy-start.3
  111.8 22.5 %collective-permute-start.25 = (bf16[2,512,256]{2,1,0:T(8,128)(2,1)S(1)}, bf16[2,512,256]{2,1,0:T(8,128)(2,1)S(1)}, u32[]{:S(2)}, u32[]{:S(2)}) collective-permute-start(bf16[2,512,256]{2,1,0:T(8,128)(2,1)S(1)} %collective-permute-done.24.rest_4_), channel_id=1, source_target_pairs={{4,0},{5,1},{6,2},{7,3},{20,16},{21,17},{22,18},{23,19}} | collective-permute-start | bytes 1572872 | tf_op jit(solution)/shard_map/ppermute | solution.py:234
  113.1 0.8 copy-start.9
  113.9 22.6 %collective-permute-start.22 = (bf16[2,512,256]{2,1,0:T(8,128)(2,1)S(1)}, bf16[2,512,256]{2,1,0:T(8,128)(2,1)S(1)}, u32[]{:S(2)}, u32[]{:S(2)}) collective-permute-start(bf16[2,512,256]{2,1,0:T(8,128)(2,1)S(1)} %collective-permute-done.21.rest_1_), channel_id=1, source_target_pairs={{8,12},{9,13},{10,14},{11,15},{24,28},{25,29},{26,30},{27,31}} | collective-permute-start | bytes 1572872 | tf_op jit(solution)/shard_map/ppermute | solution.py:233
  114.6 0.8 copy-start.11
  115.4 36.7 %collective-permute-start.17 = (bf16[2,512,256]{2,1,0:T(8,128)(2,1)}, bf16[2,512,256]{2,1,0:T(8,128)(2,1)}, u32[]{:S(2)}, u32[]{:S(2)}) collective-permute-start(bf16[2,512,256]{2,1,0:T(8,128)(2,1)} %collective-permute-done.16.rest_4_), channel_id=1, source_target_pairs={{4,0},{5,1},{6,2},{7,3},{20,16},{21,17},{22,18},{23,19}} | collective-permute-start | bytes 1572872 | tf_op jit(solution)/shard_map/ppermute | solution.py:234
  123.1 29.0 %collective-permute-start.14 = (bf16[2,512,256]{2,1,0:T(8,128)(2,1)}, bf16[2,512,256]{2,1,0:T(8,128)(2,1)}, u32[]{:S(2)}, u32[]{:S(2)}) collective-permute-start(bf16[2,512,256]{2,1,0:T(8,128)(2,1)} %collective-permute-done.13.rest_1_), channel_id=1, source_target_pairs={{8,12},{9,13},{10,14},{11,15},{24,28},{25,29},{26,30},{27,31}} | collective-permute-start | bytes 1572872 | tf_op jit(solution)/shard_map/ppermute | solution.py:233
  124.6 32.9 %collective-permute-start.9 = (bf16[2,512,256]{2,1,0:T(8,128)(2,1)}, bf16[2,512,256]{2,1,0:T(8,128)(2,1)}, u32[]{:S(2)}, u32[]{:S(2)}) collective-permute-start(bf16[2,512,256]{2,1,0:T(8,128)(2,1)} %collective-permute-done.8.rest_4_), channel_id=1, source_target_pairs={{4,0},{5,1},{6,2},{7,3},{20,16},{21,17},{22,18},{23,19}} | collective-permute-start | bytes 1572872 | tf_op jit(solution)/shard_map/ppermute | solution.py:234
  134.3 0.8 copy-start.13
  135.1 22.4 %collective-permute-start.6 = (bf16[2,512,256]{2,1,0:T(8,128)(2,1)}, bf16[2,512,256]{2,1,0:T(8,128)(2,1)}, u32[]{:S(2)}, u32[]{:S(2)}) collective-permute-start(bf16[2,512,256]{2,1,0:T(8,128)(2,1)} %collective-permute-done.5.rest_1_), channel_id=1, source_target_pairs={{8,12},{9,13},{10,14},{11,15},{24,28},{25,29},{26,30},{27,31}} | collective-permute-start | bytes 1572872 | tf_op jit(solution)/shard_map/ppermute | solution.py:233
  136.5 0.8 copy-start.15
  137.3 1.0 copy-start.6
  138.4 1.0 copy-start.8
  139.4 1.0 copy-start.10
  140.5 1.0 copy-start.12
  141.5 1.0 copy-start.14
  142.5 1.0 copy-start.16
  147.6 9.8 %copy-start.4 = (bf16[2,512,256]{2,1,0:T(8,128)(2,1)S(1)}, bf16[2,512,256]{2,1,0:T(8,128)(2,1)}, u32[]{:S(2)}) copy-start(bf16[2,512,256]{2,1,0:T(8,128)(2,1)} %copy-done.3) | copy-start | bytes 1572868
  147.7 19.8 %collective-permute-start.26 = (bf16[5,512,256]{2,1,0:T(8,128)(2,1)S(1)}, bf16[5,512,256]{2,1,0:T(8,128)(2,1)S(1)}, u32[]{:S(2)}, u32[]{:S(2)}) collective-permute-start(bf16[5,512,256]{2,1,0:T(8,128)(2,1)S(1)} %spread.5.field), channel_id=1, source_target_pairs={{0,1},{1,0},{2,3},{3,2},{4,5},{5,4},{6,7},{7,6},{8,9},{9,8},{10,11... | collective-permute-start | bytes 3932168 | tf_op jit(solution)/shard_map/ppermute | solution.py:247
  157.3 7.2 %copy-start.20 = (s32[2,3,3]{2,0,1:T(2,128)S(1)}, s32[2,3,3]{2,0,1:T(2,128)}, u32[]{:S(2)}) copy-start(s32[2,3,3]{2,0,1:T(2,128)} %param.14) | copy-start | bytes 220
  157.3 7.2 %copy-start = (bf16[1,3,3,256,256]{4,3,2,1,0:T(8,128)(2,1)S(1)}, bf16[1,3,3,256,256]{4,3,2,1,0:T(8,128)(2,1)}, u32[]{:S(2)}) copy-start(bf16[1,3,3,256,256]{4,3,2,1,0:T(8,128)(2,1)} %coef.11) | copy-start | bytes 3538948
  157.3 16.1 %collective-permute-start.18 = (bf16[5,512,256]{2,1,0:T(8,128)(2,1)S(1)}, bf16[5,512,256]{2,1,0:T(8,128)(2,1)S(1)}, u32[]{:S(2)}, u32[]{:S(2)}) collective-permute-start(bf16[5,512,256]{2,1,0:T(8,128)(2,1)S(1)} %spread.4.field), channel_id=1, source_target_pairs={{0,1},{1,0},{2,3},{3,2},{4,5},{5,4},{6,7},{7,6},{8,9},{9,8},{10,11... | collective-permute-start | bytes 3932168 | tf_op jit(solution)/shard_map/ppermute | solution.py:247
  162.7 16.7 %collective-permute-start.10 = (bf16[5,512,256]{2,1,0:T(8,128)(2,1)S(1)}, bf16[5,512,256]{2,1,0:T(8,128)(2,1)S(1)}, u32[]{:S(2)}, u32[]{:S(2)}) collective-permute-start(bf16[5,512,256]{2,1,0:T(8,128)(2,1)S(1)} %spread.3.field), channel_id=1, source_target_pairs={{0,1},{1,0},{2,3},{3,2},{4,5},{5,4},{6,7},{7,6},{8,9},{9,8},{10,11... | collective-permute-start | bytes 3932168 | tf_op jit(solution)/shard_map/ppermute | solution.py:247
  (1 other events, 0.7 us)
Sparse Core Ops, SparseCore 0:
  31.5 35.1 all-gather.2

commit v2 on v1

--- a/solution.py
+++ b/solution.py
@@ -8,7 +8,7 @@
 from jax.sharding import PartitionSpec as P
 
 CHUNK = 16
-VMEM_LIMIT = 48 * 1024 * 1024
+VMEM_LIMIT = 20 * 1024 * 1024
 SMEM = pl.BlockSpec(memory_space=pltpu.SMEM)
 VMEM = pl.BlockSpec(memory_space=pltpu.VMEM)
 HBM = pl.BlockSpec(memory_space=pl.ANY)
@@ -18,6 +18,10 @@
 
 def params():
     return pltpu.CompilerParams(vmem_limit_bytes=VMEM_LIMIT)
+
+
+def after(value, *others):
+    return lax.optimization_barrier((value, others))[0]
 
 
 def dot_nt(a, b):
@@ -33,7 +37,7 @@
         for k in range(taps):
             slot = slots[0, b, k]
             lender = jnp.maximum(slot - own, 0)
-            distance = lax.rem(t - lender + tiles, tiles)
+            distance = t ^ lender
             lent = jnp.where(distance == 0, send[lender, t, 0], own - 1 + distance)
             entry = jnp.where(slot < own, slot, lent)
             total[b, entry] += coef[b, k].astype(F32)
@@ -63,49 +67,51 @@
     value = jnp.dot(weight[0], own[...], preferred_element_type=F32)
     value += jnp.dot(weight[1], other[...], preferred_element_type=F32)
     node = lax.broadcasted_iota(jnp.int32, value.shape, 1)
-    value = jnp.where(node < count[0], value, 0.0).astype(BF16)
-    size = out.shape[-1]
-    for b in range(out.shape[0]):
-        out[b] = value[:, b * size : (b + 1) * size]
-
-
-def spread_kernel(tiles, place, send, coef_own, coef_lent, own, *rest):
-    rights, lefts = rest[: tiles - 1], rest[tiles - 1 : 2 * tiles - 2]
-    out, held, sems = rest[2 * tiles - 2 :]
-    t = place[0]
-    blocks = own.shape[0]
-    copies = [pltpu.make_async_copy(own, held.at[0], sems.at[0])]
-    copies[0].start()
-    for d in range(1, tiles):
-        from_left = t >= d
-
-        @pl.when(from_left)
-        def _():
-            pltpu.make_async_copy(rights[d - 1], held.at[d], sems.at[d]).start()
-
-        @pl.when(jnp.logical_not(from_left))
-        def _():
-            pltpu.make_async_copy(lefts[tiles - d - 1], held.at[d], sems.at[d]).start()
-
-        copies.append(pltpu.make_async_copy(rights[d - 1], held.at[d], sems.at[d]))
-    for copy in copies:
-        copy.wait()
+    out[...] = jnp.where(node < count[0], value, 0.0).astype(BF16)
+
+
+def spread_kernel(
+    tiles, place, send, coef_own, coef_lent, own, near, beyond, across, far, farthest, out, held, sems
+):
+    t, lev, sub, grp = (place[i] for i in range(4))
+    inner = jnp.logical_and(t > 0, t < tiles - 1)
+    blocks, _, size = held.shape[1:]
+
+    def fetch(source, d):
+        for b in range(blocks):
+            part = source.at[:, pl.ds(b * size, size)]
+            pltpu.make_async_copy(part, held.at[d, b], sems.at[d, b]).start()
+
+    fetch(own, 0)
+    fetch(near, 1)
+    pl.when(inner)(functools.partial(fetch, beyond, 2))
+    pl.when(inner)(functools.partial(fetch, across, 3))
+    pl.when(jnp.logical_not(inner))(functools.partial(fetch, far, 2))
+    pl.when(jnp.logical_not(inner))(functools.partial(fetch, farthest, 3))
+    for d in range(tiles):
+        for b in range(blocks):
+            pltpu.make_async_copy(held.at[d, b], held.at[d, b], sems.at[d, b]).wait()
     for j in range(blocks + tiles - 1):
         away = max(0, j - blocks + 1)
-        source = lax.rem(t - away + tiles, tiles)
+        source = t ^ away
         total = None
         for e in range(blocks + tiles - 1):
             hop = max(0, e - blocks + 1)
-            lender = lax.rem(source - hop + tiles, tiles)
+            lender = source ^ hop
             if e < blocks:
                 block = e
             else:
                 block = send[lender, source, 0]
-            distance = lax.rem(t - lender + tiles, tiles)
+            distance = t ^ lender
             if j < blocks:
                 matrix = coef_own[j, e]
             else:
-                matrix = coef_lent[:, away - 1, e].reshape(coef_own.shape[-2:])
+                matrix = jnp.concatenate(
+                    [
+                        coef_lent[c % 2 ^ sub, c // 4 ^ grp, c // 2 % 2 ^ lev, away - 1, e]
+                        for c in range(8)
+                    ]
+                )
             part = dot_nt(held[distance, block], matrix)
             total = part if total is None else total + part
         out[j] = total.astype(BF16)
@@ -120,7 +126,7 @@
     for j in range(coef.shape[2]):
         slot = slots[sub, p, j]
         lender = jnp.maximum(slot - own, 0)
-        distance = lax.rem(t - lender + tiles, tiles)
+        distance = t ^ lender
         lent = jnp.where(distance == 0, send[lender, t, 0], own - 1 + distance)
         entry = jnp.where(slot < own, slot, lent)
         part = dot_nt(field[entry], coef[0, 0, j])
@@ -173,13 +179,11 @@
     halves = lax.axis_size("sub")
     points = interp_coef.shape[1] * size
     t, lev, sub, grp = (lax.axis_index(n) for n in ("tile", "lev", "sub", "grp"))
-    place = jnp.stack([t, lev, sub]).astype(jnp.int32)
+    place = jnp.stack([t, lev, sub, grp]).astype(jnp.int32)
     chunks = members // CHUNK
     rows = levels * CHUNK
     entries = blocks + tiles - 1
     swap = [(0, 1), (1, 0)]
-    right = [(i, i + 1) for i in range(tiles - 1)]
-    left = [(i + 1, i) for i in range(tiles - 1)]
 
     state = control.transpose(1, 2, 0)
     mine = [state[:, c * CHUNK : (c + 1) * CHUNK].reshape(rows, nodes) for c in range(chunks)]
@@ -193,21 +197,7 @@
         scratch_shapes=[pltpu.VMEM((blocks, entries, size, size), F32)],
         compiler_params=params(),
         name="merge_taps",
-    )(place, send_list, conv_slots, conv_coef[0])
-
-    shares = lax.axis_size("grp") * lax.axis_size("lev") * halves
-    share = (grp * lax.axis_size("lev") + lev) * halves + sub
-    part = size // shares
-    pieces = []
-    for d in range(1, tiles):
-        target = lax.rem(t + d, tiles)
-        block = send_list[t, target, 0]
-        piece = lax.dynamic_slice(
-            merged, (block, 0, share * part, 0), (1, entries, part, size)
-        )[0]
-        ring = [(i, (i + d) % tiles) for i in range(tiles)]
-        pieces.append(lax.ppermute(piece, "tile", ring))
-    coef_lent = lax.all_gather(jnp.stack(pieces), ("grp", "lev", "sub"))
+    )(after(place, *mine), send_list, conv_slots, conv_coef[0])
 
     weight = pl.pallas_call(
         functools.partial(weight_kernel, levels),
@@ -216,40 +206,92 @@
         out_shape=jax.ShapeDtypeStruct((2, rows, rows), BF16),
         compiler_params=params(),
         name="level_weights",
-    )(place, vert_coef)
-
-    result = None
-    for c in range(chunks):
-        vertical = pl.pallas_call(
+    )(after(place, merged), vert_coef)
+
+    vertical = [
+        pl.pallas_call(
             vertical_kernel,
             in_specs=[SMEM, VMEM, VMEM, VMEM],
             out_specs=VMEM,
-            out_shape=jax.ShapeDtypeStruct((blocks, rows, size), BF16),
+            out_shape=jax.ShapeDtypeStruct((rows, nodes), BF16),
             compiler_params=params(),
             name="vertical",
-        )(node_count, weight, mine[c], theirs[c])
-        rights, lefts = [vertical], [vertical]
-        for hop in range(tiles - 1):
-            rights.append(lax.ppermute(rights[-1], "tile", right[hop:]))
-            lefts.append(lax.ppermute(lefts[-1], "tile", left[: tiles - 1 - hop]))
-        fields = pl.pallas_call(
+        )(node_count, weight, x, y)
+        for x, y in zip(mine, theirs)
+    ]
+    near, across, beyond, far, farthest = ([None] * chunks for _ in range(5))
+    edge_both = [(0, 1), (1, 0), (2, 3), (3, 2)]
+    middle = [(1, 2), (2, 1)]
+    edge_out = [(1, 0), (2, 3)]
+    edge = []
+
+    def edge_send(value, pairs):
+        if len(edge) > 1:
+            value = after(value, edge[-2])
+        edge.append(lax.ppermute(value, "tile", pairs))
+        return edge[-1]
+
+    def do_near(c):
+        near[c] = edge_send(vertical[c], edge_both)
+        across[c] = lax.ppermute(after(vertical[c], *edge[:-1][-2:-1]), "tile", middle)
+        beyond[c] = lax.ppermute(near[c], "tile", middle)
+
+    def do_far(c):
+        far[c] = edge_send(across[c], edge_out)
+
+    def do_farthest(c):
+        farthest[c] = edge_send(beyond[c], edge_out)
+
+    do_near(0)
+    do_far(0)
+    for c in range(1, chunks):
+        do_near(c)
+        do_farthest(c - 1)
+        do_far(c)
+    do_farthest(chunks - 1)
+
+    shares = lax.axis_size("grp") * lax.axis_size("lev") * halves
+    share = (grp * lax.axis_size("lev") + lev) * halves + sub
+    part = size // shares
+    pieces = []
+    for d in range(1, tiles):
+        target = t ^ d
+        block = send_list[t, target, 0]
+        piece = lax.dynamic_slice(
+            merged, (block, 0, share * part, 0), (1, entries, part, size)
+        )[0]
+        ring = [(i, i ^ d) for i in range(tiles)]
+        pieces.append(lax.ppermute(piece, "tile", ring))
+    gathered = after(jnp.stack(pieces), vertical[0])
+    for axis in ("lev", "grp", "sub"):
+        gathered = jnp.stack([gathered, lax.ppermute(gathered, axis, swap)])
+
+    def spread(place, c):
+        return pl.pallas_call(
             functools.partial(spread_kernel, tiles),
-            in_specs=[SMEM, SMEM, VMEM, VMEM] + [HBM] * (2 * tiles - 1),
+            in_specs=[SMEM, SMEM, VMEM, VMEM] + [HBM] * 6,
             out_specs=VMEM,
             out_shape=jax.ShapeDtypeStruct((entries, rows, size), BF16),
             scratch_shapes=[
                 pltpu.VMEM((tiles, blocks, rows, size), BF16),
-                pltpu.SemaphoreType.DMA((tiles,)),
+                pltpu.SemaphoreType.DMA((tiles, blocks)),
             ],
             compiler_params=params(),
             name="spread",
-        )(place, send_list, merged, coef_lent, vertical, *rights[1:], *lefts[1:])
+        )(place, send_list, merged, gathered, vertical[c], near[c], beyond[c], across[c], far[c], farthest[c])
+
+    shape = (levels, halves * members, points)
+    result = None
+    ready = []
+    for c in range(chunks):
+        fields = spread(after(place, *ready), c)
         other = lax.ppermute(fields, "sub", swap)
-        shape = (levels, halves * members, points)
         for half, field in enumerate((fields, other)):
             result = interpolate(
                 c, half, tiles, place, send_list, interp_slots, interp_coef, field, shape, result
             )
+            if half == 0:
+                ready = [result]
     return result.transpose(2, 0, 1)
 
 
@@ -313,7 +355,7 @@
         P("tile", None, None),
         P(("tile", "sub"), None, None, None, None),
     )
-    short = mesh.shape["tile"] <= 4 and mesh.shape["lev"] == 2 and mesh.shape["sub"] == 2
+    short = mesh.shape["tile"] == 4 and mesh.shape["lev"] == 2 and mesh.shape["sub"] == 2
     return jax.shard_map(
         local if short else plain,
         mesh=mesh,

time: 190 us -> 145 us (0.76)
  waiting for transfers between devices: 70.4 us -> 53.8 us
  between operations: 20.1 us -> 6.62 us
  local copies, waits for them, and re-layouts: 16.6 us -> 3.3 us
  Pallas kernels: 36.8 us -> 32 us
  starting transfers between devices: 44.4 us -> 48.4 us
    ppermute x3, waiting for transfers between devices: 27 us -> 4.54 us  [local(): theirs = [lax.ppermute(x, 'lev', swap) for x in mine]]
    unnamed x44 -> x14, local copies, waits for them, and re-layouts: 15.1 us -> 0.14 us
    ppermute x3, starting transfers between devices: 6.41 us -> 19.4 us  [local(): other = lax.ppermute(fields, 'sub', swap)]
    ppermute x18, waiting for transfers between devices: 35.8 us -> 45.7 us  [the longest x9 41.5 us: edge_send(): edge.append(lax.ppermute(value, 'tile', pairs))]
    ppermute x18, starting transfers between devices: 30.8 us -> 22.8 us  [the longest x9 12.4 us: edge_send(): edge.append(lax.ppermute(value, 'tile', pairs))]
    pallas_call x3, Pallas kernels: 14.4 us -> 8.42 us  [spread(): pl.pallas_call(functools.partial(spread_kernel, tiles), in_specs=[SMEM, S...]
    ppermute x3, waiting for transfers between devices: 7.58 us -> 3.57 us  [local(): pieces.append(lax.ppermute(piece, 'tile', ring))]
    slice x1, local copies, waits for them, and re-layouts: 0.12 us -> 2.47 us  [local(): state[:, c * CHUNK:(c + 1) * CHUNK].reshape(rows, nodes)]
  transfers between devices with their start and end apart: 28 -> 27, of which waited for: 11 -> 12; matrix products, arithmetic and copies ran while one was open for 0% -> 1% of each run, Pallas kernels for 17% -> 19%
where the time goes in v2:
time: 145 us
  waiting for transfers between devices  53.8 us (37%)
  starting transfers between devices  48.4 us (33%)
  Pallas kernels  32 us (22%)
  between operations  6.62 us (5%)
  local copies, waits for them, and re-layouts  3.3 us (2%)
    ppermute x9, waiting for transfers between devices, edge_send(): edge.append(lax.ppermute(value, 'tile', pairs))  41.5 us
    ppermute x3, starting transfers between devices, local(): other = lax.ppermute(fields, 'sub', swap)  19.4 us
    pallas_call x6, Pallas kernels, interpolate(): pl.pallas_call(functools.partial(interp_kernel, tiles), grid_spec=pltpu.P...  17.8 us
    ppermute x9, starting transfers between devices, edge_send(): edge.append(lax.ppermute(value, 'tile', pairs))  12.4 us
    pallas_call x3, Pallas kernels, spread(): pl.pallas_call(functools.partial(spread_kernel, tiles), in_specs=[SMEM, S...  8.42 us
    ppermute x3, starting transfers between devices, local(): gathered = jnp.stack([gathered, lax.ppermute(gathered, axis, swap)])  6.3 us
    ppermute x3, waiting for transfers between devices, local(): theirs = [lax.ppermute(x, 'lev', swap) for x in mine]  4.54 us
    ppermute x3, waiting for transfers between devices, local(): gathered = jnp.stack([gathered, lax.ppermute(gathered, axis, swap)])  4.26 us
  transfers between devices with their start and end apart: 27, of which 12 were waited for; matrix products, arithmetic and copies ran while one was open for 1% of the time, Pallas kernels for 19%

profile of v2, /device:TPU:1, one launch (start us, length us, event | category | flops | bytes accessed | tf_op | source)
XLA Modules:
  0.0 144.6 jit_solution(4935681542385198017)
XLA Ops:
  0.0 2.5 %fusion.2 = (bf16[32,16,512]{2,1,0:T(8,128)(2,1)S(1)}, bf16[32,16,512]{2,1,0:T(8,128)(2,1)S(1)}, bf16[32,16,512]{2,1,0:T(8,128)(2,1)}) fusion(bf16[32,48,512]{2,1,0:T(8,128)(2,1)} %bitcast.35), kind=kLoop, calls=%fused_computation.13 | loop fusion | bytes 3145728 | tf_op jit(solution)/shard_map/slice | solution.py:189
  2.5 2.0 %collective-permute-start.3 = (bf16[512,512]{1,0:T(8,128)(2,1)}, bf16[512,512]{1,0:T(8,128)(2,1)}, u32[]{:S(2)}, u32[]{:S(2)}) collective-permute-start(bf16[512,512]{1,0:T(8,128)(2,1)} %bitcast.5.own), channel_id=1, source_target_pairs={{0,2},{2,0},{1,3},{3,1},{4,6},{6,4},{5,7},{7,5},{8,10},{10,8},{9,1... | collective-permute-start | bytes 1572872 | tf_op jit(solution)/shard_map/ppermute | solution.py:190
  11.0 1.4 merge_taps.1.coef_own
  12.5 1.4 collective-permute-start
  13.8 2.3 %collective-permute-start.1 = (bf16[5,32,256]{2,1,0:T(8,128)(2,1)S(1)}, bf16[5,32,256]{2,1,0:T(8,128)(2,1)S(1)}, u32[]{:S(2)}, u32[]{:S(2)}) collective-permute-start(bf16[5,32,256]{2,1,0:T(8,128)(2,1)S(1)} %get-tuple-element.34), channel_id=1, source_target_pairs={{0,8},{4,12},{8,0},{12,4},{1,9},{5,13},{9,1},{13,5},{2,10},{6,14},... | collective-permute-start | bytes 245768 | tf_op jit(solution)/shard_map/ppermute | solution.py:264
  16.8 1.1 level_weights.1.weight
  17.9 0.9 collective-permute-done.1
  18.8 2.7 %collective-permute-done.2 = bf16[5,32,256]{2,1,0:T(8,128)(2,1)S(1)} collective-permute-done((bf16[5,32,256]{2,1,0:T(8,128)(2,1)S(1)}, bf16[5,32,256]{2,1,0:T(8,128)(2,1)S(1)}, u32[]{:S(2)}, u32[]{:S(2)}) %collective-permute-start.2) | collective-permute-done | bytes 81952 | tf_op jit(solution)/shard_map/ppermute | solution.py:264
  21.5 1.9 %vertical.3.own = bf16[512,512]{1,0:T(8,128)(2,1)S(1)} custom-call(s32[1]{0:T(128)S(6)} %copy.35.count, bf16[2,512,512]{2,1,0:T(8,128)(2,1)S(1)} %level_weights.1.weight, bf16[512,512]{1,0:T(8,128)(2,1)} %bitcast.5.own, bf16[512,512]{1,0:T(8,128)(2,1)} %collective-permute-done.3.other), custom_call_target="tpu_custom_call" | custom-call | tf_op jit(solution)/shard_map/vertical/pallas_call | solution.py:212
  23.8 1.2 collective-permute-start.7
  25.0 0.7 collective-permute-start.9
  25.6 2.9 %collective-permute-done.4 = bf16[3,5,32,256]{3,2,1,0:T(8,128)(2,1)S(1)} collective-permute-done((bf16[3,5,32,256]{3,2,1,0:T(8,128)(2,1)S(1)}, bf16[3,5,32,256]{3,2,1,0:T(8,128)(2,1)S(1)}, u32[]{:S(2)}, u32[]{:S(2)}) %collective-permute-start.4) | collective-permute-done | bytes 245792 | tf_op jit(solution)/shard_map/ppermute | solution.py:267
  28.6 1.3 collective-permute-start.5
  30.2 4.2 %collective-permute-done.7.near = bf16[512,512]{1,0:T(8,128)(2,1)S(1)} collective-permute-done((bf16[512,512]{1,0:T(8,128)(2,1)S(1)}, bf16[512,512]{1,0:T(8,128)(2,1)S(1)}, u32[]{:S(2)}, u32[]{:S(2)}) %collective-permute-start.7) | collective-permute-done | bytes 524320 | tf_op jit(solution)/shard_map/ppermute | solution.py:231
  34.4 0.7 collective-permute-start.8
  35.1 1.3 collective-permute-start.10
  36.4 1.4 collective-permute-done.5
  37.8 4.7 %collective-permute-start.6 = (bf16[2,2,3,5,32,256]{5,4,3,2,1,0:T(8,128)(2,1)S(1)}, bf16[2,2,3,5,32,256]{5,4,3,2,1,0:T(8,128)(2,1)S(1)}, u32[]{:S(2)}, u32[]{:S(2)}) collective-permute-start(bf16[2,2,3,5,32,256]{5,4,3,2,1,0:T(8,128)(2,1)S(1)} %get-tuple-element.36), channel_id=1, source_target_pairs={{0,1},{1,0},{2,3},{3,2},{4,5},{5,4},{6,7},{7,6},{8,9},{9,8},{10,11... | collective-permute-start | bytes 2949128 | tf_op jit(solution)/shard_map/ppermute | solution.py:267
  42.8 0.7 vertical.4.own
  43.5 3.4 %collective-permute-start.13 = (bf16[512,512]{1,0:T(8,128)(2,1)S(1)}, bf16[512,512]{1,0:T(8,128)(2,1)S(1)}, u32[]{:S(2)}, u32[]{:S(2)}) collective-permute-start(bf16[512,512]{1,0:T(8,128)(2,1)S(1)} %vertical.4.own), channel_id=1, source_target_pairs={{0,4},{4,0},{8,12},{12,8},{1,5},{5,1},{9,13},{13,9},{2,6},{6,2},{1... | collective-permute-start | bytes 1572872 | tf_op jit(solution)/shard_map/ppermute | solution.py:231
  46.9 0.7 collective-permute-start.15
  47.6 2.6 %collective-permute-done.10.far = bf16[512,512]{1,0:T(8,128)(2,1)S(1)} collective-permute-done((bf16[512,512]{1,0:T(8,128)(2,1)S(1)}, bf16[512,512]{1,0:T(8,128)(2,1)S(1)}, u32[]{:S(2)}, u32[]{:S(2)}) %collective-permute-start.10) | collective-permute-done | bytes 524320 | tf_op jit(solution)/shard_map/ppermute | solution.py:231
  50.2 1.3 collective-permute-start.11
  51.5 4.5 %collective-permute-done.19.other = bf16[512,512]{1,0:T(8,128)(2,1)S(1)} collective-permute-done((bf16[512,512]{1,0:T(8,128)(2,1)S(1)}, bf16[512,512]{1,0:T(8,128)(2,1)S(1)}, u32[]{:S(2)}, u32[]{:S(2)}) %collective-permute-start.19) | collective-permute-done | bytes 524320 | tf_op jit(solution)/shard_map/ppermute | solution.py:190
  56.0 0.7 vertical.5.own
  56.7 4.7 %collective-permute-done.13.near = bf16[512,512]{1,0:T(8,128)(2,1)S(1)} collective-permute-done((bf16[512,512]{1,0:T(8,128)(2,1)S(1)}, bf16[512,512]{1,0:T(8,128)(2,1)S(1)}, u32[]{:S(2)}, u32[]{:S(2)}) %collective-permute-start.13) | collective-permute-done | bytes 524320 | tf_op jit(solution)/shard_map/ppermute | solution.py:231
  61.4 1.3 collective-permute-start.16
  62.7 0.7 collective-permute-start.14
  63.4 9.2 %collective-permute-done.11.farthest = bf16[512,512]{1,0:T(8,128)(2,1)S(1)} collective-permute-done((bf16[512,512]{1,0:T(8,128)(2,1)S(1)}, bf16[512,512]{1,0:T(8,128)(2,1)S(1)}, u32[]{:S(2)}, u32[]{:S(2)}) %collective-permute-start.11) | collective-permute-done | bytes 524320 | tf_op jit(solution)/shard_map/ppermute | solution.py:231
  72.9 2.8 %spread.3.field = bf16[5,512,256]{2,1,0:T(8,128)(2,1)S(1)} custom-call(s32[4]{0:T(128)S(1)} %pad_add_fusion.place, s32[4,4,1]{2,1,0:T(4,128)S(1)} %copy.28.send, bf16[2,5,256,256]{3,2,1,0:T(8,128)(2,1)S(1)} %merge_taps.1.coef_own, bf16[2,2,2,3,5,32,256]{6,5,4,3,2,1,0:T(8,128)(2,1)S(1)} %pad_maximum_fusion.coef_lent, bf16[512,512]{1,0:T(8,128)(2,1)S(1)} %vertical.3.own, ...), custom_call_target="tpu_custom_call" | custom-call | tf_op jit(solution)/shard_map/spread/pallas_call | solution.py:270
  75.7 7.7 %collective-permute-start.18 = (bf16[5,512,256]{2,1,0:T(8,128)(2,1)S(1)}, bf16[5,512,256]{2,1,0:T(8,128)(2,1)S(1)}, u32[]{:S(2)}, u32[]{:S(2)}) collective-permute-start(bf16[5,512,256]{2,1,0:T(8,128)(2,1)S(1)} %spread.3.field), channel_id=1, source_target_pairs={{0,1},{1,0},{2,3},{3,2},{4,5},{5,4},{6,7},{7,6},{8,9},{9,8},{10,11... | collective-permute-start | bytes 3932168 | tf_op jit(solution)/shard_map/ppermute | solution.py:288
  84.1 1.3 collective-permute-start.17
  85.4 9.8 %collective-permute-done.20.near = bf16[512,512]{1,0:T(8,128)(2,1)S(1)} collective-permute-done((bf16[512,512]{1,0:T(8,128)(2,1)S(1)}, bf16[512,512]{1,0:T(8,128)(2,1)S(1)}, u32[]{:S(2)}, u32[]{:S(2)}) %collective-permute-start.20) | collective-permute-done | bytes 524320 | tf_op jit(solution)/shard_map/ppermute | solution.py:231
  95.1 0.7 collective-permute-start.21
  95.8 1.3 collective-permute-start.23
  97.1 9.2 %collective-permute-done.17.farthest = bf16[512,512]{1,0:T(8,128)(2,1)S(1)} collective-permute-done((bf16[512,512]{1,0:T(8,128)(2,1)S(1)}, bf16[512,512]{1,0:T(8,128)(2,1)S(1)}, u32[]{:S(2)}, u32[]{:S(2)}) %collective-permute-start.17) | collective-permute-done | bytes 524320 | tf_op jit(solution)/shard_map/ppermute | solution.py:231
  106.4 1.3 collective-permute-start.24
  107.7 3.0 %interpolate.6.rest_0_ = bf16[32,96,768]{2,1,0:T(8,128)(2,1)} custom-call(s32[4]{0:T(128)S(1)} %pad_add_fusion.place, s32[4,4,1]{2,1,0:T(4,128)S(1)} %copy.28.send, s32[2,3,3]{2,1,0:T(4,128)S(1)} %copy.29.slots, bf16[1,3,3,256,256]{4,3,2,1,0:T(8,128)(2,1)S(1)} %copy-done, bf16[5,512,256]{2,1,0:T(8,128)(2,1)S(1)} %spread.3.field), custom_call_target="tpu_custom_call" | custom-call | tf_op jit(solution)/shard_map/interpolate/pallas_call | solution.py:158
  110.7 2.8 %spread.4.field = bf16[5,512,256]{2,1,0:T(8,128)(2,1)S(1)} custom-call(s32[4]{0:T(128)S(1)} %pad_add_fusion.place, s32[4,4,1]{2,1,0:T(4,128)S(1)} %copy.28.send, bf16[2,5,256,256]{3,2,1,0:T(8,128)(2,1)S(1)} %merge_taps.1.coef_own, bf16[2,2,2,3,5,32,256]{6,5,4,3,2,1,0:T(8,128)(2,1)S(1)} %pad_maximum_fusion.coef_lent, bf16[512,512]{1,0:T(8,128)(2,1)S(1)} %vertical.4.own, ...), custom_call_target="tpu_custom_call" | custom-call | tf_op jit(solution)/shard_map/spread/pallas_call | solution.py:270
  113.5 7.7 %collective-permute-start.26 = (bf16[5,512,256]{2,1,0:T(8,128)(2,1)S(1)}, bf16[5,512,256]{2,1,0:T(8,128)(2,1)S(1)}, u32[]{:S(2)}, u32[]{:S(2)}) collective-permute-start(bf16[5,512,256]{2,1,0:T(8,128)(2,1)S(1)} %spread.4.field), channel_id=1, source_target_pairs={{0,1},{1,0},{2,3},{3,2},{4,5},{5,4},{6,7},{7,6},{8,9},{9,8},{10,11... | collective-permute-start | bytes 3932168 | tf_op jit(solution)/shard_map/ppermute | solution.py:288
  121.1 3.0 %interpolate.7.rest_0_ = bf16[32,96,768]{2,1,0:T(8,128)(2,1)} custom-call(s32[4]{0:T(128)S(1)} %pad_add_fusion.place, s32[4,4,1]{2,1,0:T(4,128)S(1)} %copy.28.send, s32[2,3,3]{2,1,0:T(4,128)S(1)} %copy.29.slots, bf16[1,3,3,256,256]{4,3,2,1,0:T(8,128)(2,1)S(1)} %copy-done, ...), custom_call_target="tpu_custom_call", output_to_operand_aliasing={{}: (5, {})} | custom-call | tf_op jit(solution)/shard_map/interpolate/pallas_call | solution.py:158
  124.1 3.0 %interpolate.8.rest_0_ = bf16[32,96,768]{2,1,0:T(8,128)(2,1)} custom-call(s32[4]{0:T(128)S(1)} %pad_add_fusion.place, s32[4,4,1]{2,1,0:T(4,128)S(1)} %copy.28.send, s32[2,3,3]{2,1,0:T(4,128)S(1)} %copy.29.slots, bf16[1,3,3,256,256]{4,3,2,1,0:T(8,128)(2,1)S(1)} %copy-done, bf16[5,512,256]{2,1,0:T(8,128)(2,1)S(1)} %spread.4.field, ...), custom_call_target="tpu_custom_call", output_to_operand_aliasing={{}: (5, {})} | custom-call | tf_op jit(solution)/shard_map/interpolate/pallas_call | solution.py:158
  127.1 1.8 %collective-permute-done.24.farthest = bf16[512,512]{1,0:T(8,128)(2,1)S(1)} collective-permute-done((bf16[512,512]{1,0:T(8,128)(2,1)S(1)}, bf16[512,512]{1,0:T(8,128)(2,1)S(1)}, u32[]{:S(2)}, u32[]{:S(2)}) %collective-permute-start.24) | collective-permute-done | bytes 524320 | tf_op jit(solution)/shard_map/ppermute | solution.py:231
  128.8 2.8 %spread.5.field = bf16[5,512,256]{2,1,0:T(8,128)(2,1)S(1)} custom-call(s32[4]{0:T(128)S(1)} %pad_add_fusion.place, s32[4,4,1]{2,1,0:T(4,128)S(1)} %copy.28.send, bf16[2,5,256,256]{3,2,1,0:T(8,128)(2,1)S(1)} %merge_taps.1.coef_own, bf16[2,2,2,3,5,32,256]{6,5,4,3,2,1,0:T(8,128)(2,1)S(1)} %pad_maximum_fusion.coef_lent, bf16[512,512]{1,0:T(8,128)(2,1)S(1)} %vertical.5.own, ...), custom_call_target="tpu_custom_call" | custom-call | tf_op jit(solution)/shard_map/spread/pallas_call | solution.py:270
  131.7 4.1 %collective-permute-start.25 = (bf16[5,512,256]{2,1,0:T(8,128)(2,1)S(1)}, bf16[5,512,256]{2,1,0:T(8,128)(2,1)S(1)}, u32[]{:S(2)}, u32[]{:S(2)}) collective-permute-start(bf16[5,512,256]{2,1,0:T(8,128)(2,1)S(1)} %spread.5.field), channel_id=1, source_target_pairs={{0,1},{1,0},{2,3},{3,2},{4,5},{5,4},{6,7},{7,6},{8,9},{9,8},{10,11... | collective-permute-start | bytes 3932168 | tf_op jit(solution)/shard_map/ppermute | solution.py:288
  135.7 3.0 %interpolate.9.rest_0_ = bf16[32,96,768]{2,1,0:T(8,128)(2,1)} custom-call(s32[4]{0:T(128)S(1)} %pad_add_fusion.place, s32[4,4,1]{2,1,0:T(4,128)S(1)} %copy.28.send, s32[2,3,3]{2,1,0:T(4,128)S(1)} %copy.29.slots, bf16[1,3,3,256,256]{4,3,2,1,0:T(8,128)(2,1)S(1)} %copy-done, ...), custom_call_target="tpu_custom_call", output_to_operand_aliasing={{}: (5, {})} | custom-call | tf_op jit(solution)/shard_map/interpolate/pallas_call | solution.py:158
  138.7 3.0 %interpolate.10.rest_0_ = bf16[32,96,768]{2,1,0:T(8,128)(2,1)} custom-call(s32[4]{0:T(128)S(1)} %pad_add_fusion.place, s32[4,4,1]{2,1,0:T(4,128)S(1)} %copy.28.send, s32[2,3,3]{2,1,0:T(4,128)S(1)} %copy.29.slots, bf16[1,3,3,256,256]{4,3,2,1,0:T(8,128)(2,1)S(1)} %copy-done, bf16[5,512,256]{2,1,0:T(8,128)(2,1)S(1)} %spread.5.field, ...), custom_call_target="tpu_custom_call", output_to_operand_aliasing={{}: (5, {})} | custom-call | tf_op jit(solution)/shard_map/interpolate/pallas_call | solution.py:158
  141.7 3.0 %interpolate.11 = bf16[32,96,768]{2,1,0:T(8,128)(2,1)} custom-call(s32[4]{0:T(128)S(1)} %pad_add_fusion.place, s32[4,4,1]{2,1,0:T(4,128)S(1)} %copy.28.send, s32[2,3,3]{2,1,0:T(4,128)S(1)} %copy.29.slots, bf16[1,3,3,256,256]{4,3,2,1,0:T(8,128)(2,1)S(1)} %copy-done, ...), custom_call_target="tpu_custom_call", output_to_operand_aliasing={{}: (5, {})} | custom-call | tf_op jit(solution)/shard_map/interpolate/pallas_call | solution.py:158
  (42 shorter events, 2.9 us)
Async XLA Ops:
  0.0 4.5 %copy-start.4 = (s32[4,4,1]{1,2,0:T(1,128)S(1)}, s32[4,4,1]{1,2,0:T(1,128)}, u32[]{:S(2)}) copy-start(s32[4,4,1]{1,2,0:T(1,128)} %param.11) | copy-start | bytes 196
  0.0 11.0 %copy-start.1 = (bf16[1,2,9,256,256]{4,3,2,1,0:T(8,128)(2,1)S(1)}, bf16[1,2,9,256,256]{4,3,2,1,0:T(8,128)(2,1)}, u32[]{:S(2)}) copy-start(bf16[1,2,9,256,256]{4,3,2,1,0:T(8,128)(2,1)} %param.13) | copy-start | bytes 7077892
  0.0 11.0 %copy-start.3 = (s32[1,2,9]{2,1,0:T(2,128)S(1)}, s32[1,2,9]{2,1,0:T(2,128)}, u32[]{:S(2)}) copy-start(s32[1,2,9]{2,1,0:T(2,128)} %slots.7) | copy-start | bytes 220
  2.5 19.0 %collective-permute-start.3 = (bf16[512,512]{1,0:T(8,128)(2,1)}, bf16[512,512]{1,0:T(8,128)(2,1)}, u32[]{:S(2)}, u32[]{:S(2)}) collective-permute-start(bf16[512,512]{1,0:T(8,128)(2,1)} %bitcast.5.own), channel_id=1, source_target_pairs={{0,2},{2,0},{1,3},{3,1},{4,6},{6,4},{5,7},{7,5},{8,10},{10,8},{9,1... | collective-permute-start | bytes 1572872 | tf_op jit(solution)/shard_map/ppermute | solution.py:190
  11.0 5.8 %copy-start.2 = (bf16[64,64]{1,0:T(8,128)(2,1)S(1)}, bf16[64,64]{1,0:T(8,128)(2,1)}, u32[]{:S(2)}) copy-start(bf16[64,64]{1,0:T(8,128)(2,1)} %vert.1) | copy-start | bytes 24580
  12.5 5.4 %collective-permute-start = (bf16[5,32,256]{2,1,0:T(8,128)(2,1)S(1)}, bf16[5,32,256]{2,1,0:T(8,128)(2,1)S(1)}, u32[]{:S(2)}, u32[]{:S(2)}) collective-permute-start(bf16[5,32,256]{2,1,0:T(8,128)(2,1)S(1)} %get-tuple-element.32), channel_id=1, source_target_pairs={{0,4},{4,0},{8,12},{12,8},{1,5},{5,1},{9,13},{13,9},{2,6},{6,2},{1... | collective-permute-start | bytes 245768 | tf_op jit(solution)/shard_map/ppermute | solution.py:264
  13.8 4.9 %collective-permute-start.1 = (bf16[5,32,256]{2,1,0:T(8,128)(2,1)S(1)}, bf16[5,32,256]{2,1,0:T(8,128)(2,1)S(1)}, u32[]{:S(2)}, u32[]{:S(2)}) collective-permute-start(bf16[5,32,256]{2,1,0:T(8,128)(2,1)S(1)} %get-tuple-element.34), channel_id=1, source_target_pairs={{0,8},{4,12},{8,0},{12,4},{1,9},{5,13},{9,1},{13,5},{2,10},{6,14},... | collective-permute-start | bytes 245768 | tf_op jit(solution)/shard_map/ppermute | solution.py:264
  16.2 5.3 %collective-permute-start.2 = (bf16[5,32,256]{2,1,0:T(8,128)(2,1)S(1)}, bf16[5,32,256]{2,1,0:T(8,128)(2,1)S(1)}, u32[]{:S(2)}, u32[]{:S(2)}) collective-permute-start(bf16[5,32,256]{2,1,0:T(8,128)(2,1)S(1)} %get-tuple-element.33), channel_id=1, source_target_pairs={{0,12},{4,8},{8,4},{12,0},{1,13},{5,9},{9,5},{13,1},{2,14},{6,10},... | collective-permute-start | bytes 245768 | tf_op jit(solution)/shard_map/ppermute | solution.py:264
  23.4 5.1 %collective-permute-start.4 = (bf16[3,5,32,256]{3,2,1,0:T(8,128)(2,1)S(1)}, bf16[3,5,32,256]{3,2,1,0:T(8,128)(2,1)S(1)}, u32[]{:S(2)}, u32[]{:S(2)}) collective-permute-start(bf16[3,5,32,256]{3,2,1,0:T(8,128)(2,1)S(1)} %pad_maximum_fusion.3), channel_id=1, source_target_pairs={{0,2},{2,0},{1,3},{3,1},{4,6},{6,4},{5,7},{7,5},{8,10},{10,8},{9,1... | collective-permute-start | bytes 737288 | tf_op jit(solution)/shard_map/ppermute | solution.py:267
  23.8 10.6 %collective-permute-start.7 = (bf16[512,512]{1,0:T(8,128)(2,1)S(1)}, bf16[512,512]{1,0:T(8,128)(2,1)S(1)}, u32[]{:S(2)}, u32[]{:S(2)}) collective-permute-start(bf16[512,512]{1,0:T(8,128)(2,1)S(1)} %vertical.3.own), channel_id=1, source_target_pairs={{0,4},{4,0},{8,12},{12,8},{1,5},{5,1},{9,13},{13,9},{2,6},{6,2},{1... | collective-permute-start | bytes 1572872 | tf_op jit(solution)/shard_map/ppermute | solution.py:231
  25.0 10.1 %collective-permute-start.9 = (bf16[512,512]{1,0:T(8,128)(2,1)S(1)}, bf16[512,512]{1,0:T(8,128)(2,1)S(1)}, u32[]{:S(2)}, u32[]{:S(2)}) collective-permute-start(bf16[512,512]{1,0:T(8,128)(2,1)S(1)} %vertical.3.own), channel_id=1, source_target_pairs={{4,8},{8,4},{5,9},{9,5},{6,10},{10,6},{7,11},{11,7},{20,24},{24,20... | collective-permute-start | bytes 1572872 | tf_op jit(solution)/shard_map/ppermute | solution.py:236
  28.6 9.1 %collective-permute-start.5 = (bf16[2,3,5,32,256]{4,3,2,1,0:T(8,128)(2,1)S(1)}, bf16[2,3,5,32,256]{4,3,2,1,0:T(8,128)(2,1)S(1)}, u32[]{:S(2)}, u32[]{:S(2)}) collective-permute-start(bf16[2,3,5,32,256]{4,3,2,1,0:T(8,128)(2,1)S(1)} %get-tuple-element.38), channel_id=1, source_target_pairs={{0,16},{16,0},{1,17},{17,1},{2,18},{18,2},{3,19},{19,3},{4,20},{20... | collective-permute-start | bytes 1474568 | tf_op jit(solution)/shard_map/ppermute | solution.py:267
  29.9 12.9 %collective-permute-start.12 = (bf16[512,512]{1,0:T(8,128)(2,1)S(1)}, bf16[512,512]{1,0:T(8,128)(2,1)S(1)}, u32[]{:S(2)}, u32[]{:S(2)}) collective-permute-start(bf16[512,512]{1,0:T(8,128)(2,1)S(1)} %bitcast.33), channel_id=1, source_target_pairs={{0,2},{2,0},{1,3},{3,1},{4,6},{6,4},{5,7},{7,5},{8,10},{10,8},{9,1... | collective-permute-start | bytes 1572872 | tf_op jit(solution)/shard_map/ppermute | solution.py:190
  34.4 12.6 %collective-permute-start.8 = (bf16[512,512]{1,0:T(8,128)(2,1)S(1)}, bf16[512,512]{1,0:T(8,128)(2,1)S(1)}, u32[]{:S(2)}, u32[]{:S(2)}) collective-permute-start(bf16[512,512]{1,0:T(8,128)(2,1)S(1)} %collective-permute-done.7.near), channel_id=1, source_target_pairs={{4,8},{8,4},{5,9},{9,5},{6,10},{10,6},{7,11},{11,7},{20,24},{24,20... | collective-permute-start | bytes 1572872 | tf_op jit(solution)/shard_map/ppermute | solution.py:237
  35.1 15.1 %collective-permute-start.10 = (bf16[512,512]{1,0:T(8,128)(2,1)S(1)}, bf16[512,512]{1,0:T(8,128)(2,1)S(1)}, u32[]{:S(2)}, u32[]{:S(2)}) collective-permute-start(bf16[512,512]{1,0:T(8,128)(2,1)S(1)} %collective-permute-done.9.across), channel_id=1, source_target_pairs={{4,0},{8,12},{5,1},{9,13},{6,2},{10,14},{7,3},{11,15},{20,16},{24,... | collective-permute-start | bytes 1572872 | tf_op jit(solution)/shard_map/ppermute | solution.py:231
  37.8 34.8 %collective-permute-start.6 = (bf16[2,2,3,5,32,256]{5,4,3,2,1,0:T(8,128)(2,1)S(1)}, bf16[2,2,3,5,32,256]{5,4,3,2,1,0:T(8,128)(2,1)S(1)}, u32[]{:S(2)}, u32[]{:S(2)}) collective-permute-start(bf16[2,2,3,5,32,256]{5,4,3,2,1,0:T(8,128)(2,1)S(1)} %get-tuple-element.36), channel_id=1, source_target_pairs={{0,1},{1,0},{2,3},{3,2},{4,5},{5,4},{6,7},{7,6},{8,9},{9,8},{10,11... | collective-permute-start | bytes 2949128 | tf_op jit(solution)/shard_map/ppermute | solution.py:267
  42.5 13.5 %collective-permute-start.19 = (bf16[512,512]{1,0:T(8,128)(2,1)S(1)}, bf16[512,512]{1,0:T(8,128)(2,1)S(1)}, u32[]{:S(2)}, u32[]{:S(2)}) collective-permute-start(bf16[512,512]{1,0:T(8,128)(2,1)S(1)} %bitcast.31), channel_id=1, source_target_pairs={{0,2},{2,0},{1,3},{3,1},{4,6},{6,4},{5,7},{7,5},{8,10},{10,8},{9,1... | collective-permute-start | bytes 1572872 | tf_op jit(solution)/shard_map/ppermute | solution.py:190
  43.5 17.9 %collective-permute-start.13 = (bf16[512,512]{1,0:T(8,128)(2,1)S(1)}, bf16[512,512]{1,0:T(8,128)(2,1)S(1)}, u32[]{:S(2)}, u32[]{:S(2)}) collective-permute-start(bf16[512,512]{1,0:T(8,128)(2,1)S(1)} %vertical.4.own), channel_id=1, source_target_pairs={{0,4},{4,0},{8,12},{12,8},{1,5},{5,1},{9,13},{13,9},{2,6},{6,2},{1... | collective-permute-start | bytes 1572872 | tf_op jit(solution)/shard_map/ppermute | solution.py:231
  46.9 14.5 %collective-permute-start.15 = (bf16[512,512]{1,0:T(8,128)(2,1)S(1)}, bf16[512,512]{1,0:T(8,128)(2,1)S(1)}, u32[]{:S(2)}, u32[]{:S(2)}) collective-permute-start(bf16[512,512]{1,0:T(8,128)(2,1)S(1)} %vertical.4.own), channel_id=1, source_target_pairs={{4,8},{8,4},{5,9},{9,5},{6,10},{10,6},{7,11},{11,7},{20,24},{24,20... | collective-permute-start | bytes 1572872 | tf_op jit(solution)/shard_map/ppermute | solution.py:236
  50.2 22.5 %collective-permute-start.11 = (bf16[512,512]{1,0:T(8,128)(2,1)S(1)}, bf16[512,512]{1,0:T(8,128)(2,1)S(1)}, u32[]{:S(2)}, u32[]{:S(2)}) collective-permute-start(bf16[512,512]{1,0:T(8,128)(2,1)S(1)} %collective-permute-done.8.beyond), channel_id=1, source_target_pairs={{4,0},{8,12},{5,1},{9,13},{6,2},{10,14},{7,3},{11,15},{20,16},{24,... | collective-permute-start | bytes 1572872 | tf_op jit(solution)/shard_map/ppermute | solution.py:231
  61.4 22.6 %collective-permute-start.16 = (bf16[512,512]{1,0:T(8,128)(2,1)S(1)}, bf16[512,512]{1,0:T(8,128)(2,1)S(1)}, u32[]{:S(2)}, u32[]{:S(2)}) collective-permute-start(bf16[512,512]{1,0:T(8,128)(2,1)S(1)} %collective-permute-done.15.across), channel_id=1, source_target_pairs={{4,0},{8,12},{5,1},{9,13},{6,2},{10,14},{7,3},{11,15},{20,16},{24,... | collective-permute-start | bytes 1572872 | tf_op jit(solution)/shard_map/ppermute | solution.py:231
  62.7 21.3 %collective-permute-start.14 = (bf16[512,512]{1,0:T(8,128)(2,1)S(1)}, bf16[512,512]{1,0:T(8,128)(2,1)S(1)}, u32[]{:S(2)}, u32[]{:S(2)}) collective-permute-start(bf16[512,512]{1,0:T(8,128)(2,1)S(1)} %collective-permute-done.13.near), channel_id=1, source_target_pairs={{4,8},{8,4},{5,9},{9,5},{6,10},{10,6},{7,11},{11,7},{20,24},{24,20... | collective-permute-start | bytes 1572872 | tf_op jit(solution)/shard_map/ppermute | solution.py:237
  72.7 22.5 %collective-permute-start.20 = (bf16[512,512]{1,0:T(8,128)(2,1)S(1)}, bf16[512,512]{1,0:T(8,128)(2,1)S(1)}, u32[]{:S(2)}, u32[]{:S(2)}) collective-permute-start(bf16[512,512]{1,0:T(8,128)(2,1)S(1)} %vertical.5.own), channel_id=1, source_target_pairs={{0,4},{4,0},{8,12},{12,8},{1,5},{5,1},{9,13},{13,9},{2,6},{6,2},{1... | collective-permute-start | bytes 1572872 | tf_op jit(solution)/shard_map/ppermute | solution.py:231
  72.9 34.8 %copy-start.5 = (s32[2,3,3]{2,0,1:T(2,128)S(1)}, s32[2,3,3]{2,0,1:T(2,128)}, u32[]{:S(2)}) copy-start(s32[2,3,3]{2,0,1:T(2,128)} %param.14) | copy-start | bytes 220
  72.9 34.8 %copy-start = (bf16[1,3,3,256,256]{4,3,2,1,0:T(8,128)(2,1)S(1)}, bf16[1,3,3,256,256]{4,3,2,1,0:T(8,128)(2,1)}, u32[]{:S(2)}) copy-start(bf16[1,3,3,256,256]{4,3,2,1,0:T(8,128)(2,1)} %coef.11) | copy-start | bytes 3538948
  75.7 45.4 %collective-permute-start.18 = (bf16[5,512,256]{2,1,0:T(8,128)(2,1)S(1)}, bf16[5,512,256]{2,1,0:T(8,128)(2,1)S(1)}, u32[]{:S(2)}, u32[]{:S(2)}) collective-permute-start(bf16[5,512,256]{2,1,0:T(8,128)(2,1)S(1)} %spread.3.field), channel_id=1, source_target_pairs={{0,1},{1,0},{2,3},{3,2},{4,5},{5,4},{6,7},{7,6},{8,9},{9,8},{10,11... | collective-permute-start | bytes 3932168 | tf_op jit(solution)/shard_map/ppermute | solution.py:288
  83.4 12.5 %collective-permute-start.22 = (bf16[512,512]{1,0:T(8,128)(2,1)S(1)}, bf16[512,512]{1,0:T(8,128)(2,1)S(1)}, u32[]{:S(2)}, u32[]{:S(2)}) collective-permute-start(bf16[512,512]{1,0:T(8,128)(2,1)S(1)} %vertical.5.own), channel_id=1, source_target_pairs={{4,8},{8,4},{5,9},{9,5},{6,10},{10,6},{7,11},{11,7},{20,24},{24,20... | collective-permute-start | bytes 1572872 | tf_op jit(solution)/shard_map/ppermute | solution.py:236
  84.1 22.3 %collective-permute-start.17 = (bf16[512,512]{1,0:T(8,128)(2,1)S(1)}, bf16[512,512]{1,0:T(8,128)(2,1)S(1)}, u32[]{:S(2)}, u32[]{:S(2)}) collective-permute-start(bf16[512,512]{1,0:T(8,128)(2,1)S(1)} %collective-permute-done.14.beyond), channel_id=1, source_target_pairs={{4,0},{8,12},{5,1},{9,13},{6,2},{10,14},{7,3},{11,15},{20,16},{24,... | collective-permute-start | bytes 1572872 | tf_op jit(solution)/shard_map/ppermute | solution.py:231
  95.1 11.2 %collective-permute-start.21 = (bf16[512,512]{1,0:T(8,128)(2,1)S(1)}, bf16[512,512]{1,0:T(8,128)(2,1)S(1)}, u32[]{:S(2)}, u32[]{:S(2)}) collective-permute-start(bf16[512,512]{1,0:T(8,128)(2,1)S(1)} %collective-permute-done.20.near), channel_id=1, source_target_pairs={{4,8},{8,4},{5,9},{9,5},{6,10},{10,6},{7,11},{11,7},{20,24},{24,20... | collective-permute-start | bytes 1572872 | tf_op jit(solution)/shard_map/ppermute | solution.py:237
  95.8 31.2 %collective-permute-start.23 = (bf16[512,512]{1,0:T(8,128)(2,1)S(1)}, bf16[512,512]{1,0:T(8,128)(2,1)S(1)}, u32[]{:S(2)}, u32[]{:S(2)}) collective-permute-start(bf16[512,512]{1,0:T(8,128)(2,1)S(1)} %collective-permute-done.22.across), channel_id=1, source_target_pairs={{4,0},{8,12},{5,1},{9,13},{6,2},{10,14},{7,3},{11,15},{20,16},{24,... | collective-permute-start | bytes 1572872 | tf_op jit(solution)/shard_map/ppermute | solution.py:231
  106.4 22.5 %collective-permute-start.24 = (bf16[512,512]{1,0:T(8,128)(2,1)S(1)}, bf16[512,512]{1,0:T(8,128)(2,1)S(1)}, u32[]{:S(2)}, u32[]{:S(2)}) collective-permute-start(bf16[512,512]{1,0:T(8,128)(2,1)S(1)} %collective-permute-done.21.beyond), channel_id=1, source_target_pairs={{4,0},{8,12},{5,1},{9,13},{6,2},{10,14},{7,3},{11,15},{20,16},{24,... | collective-permute-start | bytes 1572872 | tf_op jit(solution)/shard_map/ppermute | solution.py:231
  113.5 22.2 %collective-permute-start.26 = (bf16[5,512,256]{2,1,0:T(8,128)(2,1)S(1)}, bf16[5,512,256]{2,1,0:T(8,128)(2,1)S(1)}, u32[]{:S(2)}, u32[]{:S(2)}) collective-permute-start(bf16[5,512,256]{2,1,0:T(8,128)(2,1)S(1)} %spread.4.field), channel_id=1, source_target_pairs={{0,1},{1,0},{2,3},{3,2},{4,5},{5,4},{6,7},{7,6},{8,9},{9,8},{10,11... | collective-permute-start | bytes 3932168 | tf_op jit(solution)/shard_map/ppermute | solution.py:288
  131.7 10.0 %collective-permute-start.25 = (bf16[5,512,256]{2,1,0:T(8,128)(2,1)S(1)}, bf16[5,512,256]{2,1,0:T(8,128)(2,1)S(1)}, u32[]{:S(2)}, u32[]{:S(2)}) collective-permute-start(bf16[5,512,256]{2,1,0:T(8,128)(2,1)S(1)} %spread.5.field), channel_id=1, source_target_pairs={{0,1},{1,0},{2,3},{3,2},{4,5},{5,4},{6,7},{7,6},{8,9},{9,8},{10,11... | collective-permute-start | bytes 3932168 | tf_op jit(solution)/shard_map/ppermute | solution.py:288

commit v3 on v2

--- a/solution.py
+++ b/solution.py
@@ -28,7 +28,7 @@
     return lax.dot_general(a, b, (((1,), (1,)), ((), ())), preferred_element_type=F32)
 
 
-def merge_kernel(tiles, place, send, slots, coef, out, total):
+def merge_kernel(tiles, place, send, slots, coef, out, pieces, total):
     blocks, taps = coef.shape[:2]
     own = blocks
     t = place[0]
@@ -42,6 +42,10 @@
             entry = jnp.where(slot < own, slot, lent)
             total[b, entry] += coef[b, k].astype(F32)
     out[...] = total[...].astype(BF16)
+    part = pieces.shape[2]
+    start = pl.multiple_of(place[4] * part, part)
+    for d in range(1, tiles):
+        pieces[d - 1] = out[send[t, t ^ d, 0], :, pl.ds(start, part), :]
 
 
 def weight_kernel(levels, place, vert, out):
@@ -94,80 +98,74 @@
     for j in range(blocks + tiles - 1):
         away = max(0, j - blocks + 1)
         source = t ^ away
-        total = None
+        values, matrices = [], []
         for e in range(blocks + tiles - 1):
             hop = max(0, e - blocks + 1)
             lender = source ^ hop
-            if e < blocks:
-                block = e
+            block = e if e < blocks else send[lender, source, 0]
+            values.append(held[t ^ lender, block])
+            if j < blocks:
+                matrices.append(coef_own[j, e])
             else:
-                block = send[lender, source, 0]
-            distance = t ^ lender
-            if j < blocks:
-                matrix = coef_own[j, e]
-            else:
-                matrix = jnp.concatenate(
-                    [
-                        coef_lent[c % 2 ^ sub, c // 4 ^ grp, c // 2 % 2 ^ lev, away - 1, e]
-                        for c in range(8)
-                    ]
-                )
-            part = dot_nt(held[distance, block], matrix)
-            total = part if total is None else total + part
+                pieces = [
+                    coef_lent[c % 2 ^ sub, c // 2 ^ (2 * grp + lev), away - 1, e]
+                    for c in range(8)
+                ]
+                matrices.append(jnp.concatenate(pieces))
+        total = dot_nt(jnp.concatenate(values, 1), jnp.concatenate(matrices, 1))
         out[j] = total.astype(BF16)
 
 
-def interp_kernel(tiles, place, send, slots, coef, field, *rest):
-    out = rest[-1]
+def interp_kernel(tiles, chunk, chunks, half, level, place, send, slots, coef, field, *rest):
+    out, made, done = rest[-3:]
     own = field.shape[0] - tiles + 1
     t, sub = place[0], place[2]
-    p = pl.program_id(0)
-    total = None
-    for j in range(coef.shape[2]):
-        slot = slots[sub, p, j]
-        lender = jnp.maximum(slot - own, 0)
-        distance = t ^ lender
-        lent = jnp.where(distance == 0, send[lender, t, 0], own - 1 + distance)
-        entry = jnp.where(slot < own, slot, lent)
-        part = dot_nt(field[entry], coef[0, 0, j])
-        total = part if total is None else total + part
-    out[...] = total.astype(BF16).reshape(out.shape)
-
-
-def interpolate(chunk, half, tiles, place, send, slots, coef, field, shape, before):
-    levels, members, points = shape
-    count = coef.shape[1]
-    chunks = members // 2 // CHUNK
-    size = coef.shape[-1]
-
-    def place_out(p, place, send, slots):
-        sub = place[2]
-        side = sub if half == 0 else 1 - sub
-        return (0, side * chunks + chunk, p)
-
-    in_specs = [
-        pl.BlockSpec((1, 1) + coef.shape[2:], lambda p, *_: (0, p, 0, 0, 0)),
-        pl.BlockSpec(field.shape, lambda p, *_: (0, 0, 0)),
-    ]
-    operands = [coef, field]
+    side = sub if half == 0 else 1 - sub
+    count, taps, size = coef.shape[1:4]
+    levels, members = made.shape[:2]
+    first = pl.multiple_of((side * chunks + chunk) * members, members)
+    for p in range(count):
+        fields, matrices = [], []
+        for j in range(taps):
+            slot = slots[sub, p, j]
+            lender = jnp.maximum(slot - own, 0)
+            distance = t ^ lender
+            lent = jnp.where(distance == 0, send[lender, t, 0], own - 1 + distance)
+            fields.append(field[jnp.where(slot < own, slot, lent)])
+            matrices.append(coef[0, p, j])
+        value = dot_nt(jnp.concatenate(fields, 1), jnp.concatenate(matrices, 1))
+        made[:, :, p * size : (p + 1) * size] = value.astype(BF16).reshape(levels, members, size)
+    copy = pltpu.make_async_copy(
+        made, out.at[pl.ds(level, levels), pl.ds(first, members)], done
+    )
+    copy.start()
+    copy.wait()
+
+
+def interpolate(chunk, half, level, tiles, place, send, slots, coef, field, shape, before):
+    count, _, size = coef.shape[1:4]
+    chunks = shape[1] // 2 // CHUNK
+    levels = field.shape[1] // CHUNK
+    operands = [place, send, slots, coef, field]
+    in_specs = [SMEM, SMEM, SMEM, VMEM, VMEM]
     aliases = {}
     if before is not None:
+        aliases = {len(operands): 0}
+        operands.append(before)
         in_specs.append(HBM)
-        operands.append(before)
-        aliases = {5: 0}
     return pl.pallas_call(
-        functools.partial(interp_kernel, tiles),
-        grid_spec=pltpu.PrefetchScalarGridSpec(
-            num_scalar_prefetch=3,
-            grid=(count,),
-            in_specs=in_specs,
-            out_specs=pl.BlockSpec((levels, CHUNK, size), place_out),
-        ),
+        functools.partial(interp_kernel, tiles, chunk, chunks, half, level),
+        in_specs=in_specs,
+        out_specs=HBM,
         out_shape=jax.ShapeDtypeStruct(shape, BF16),
+        scratch_shapes=[
+            pltpu.VMEM((levels, CHUNK, count * size), BF16),
+            pltpu.SemaphoreType.DMA,
+        ],
         input_output_aliases=aliases,
         compiler_params=params(),
         name="interpolate",
-    )(place, send, slots, *operands)
+    )(*operands)
 
 
 def local(
@@ -179,25 +177,38 @@
     halves = lax.axis_size("sub")
     points = interp_coef.shape[1] * size
     t, lev, sub, grp = (lax.axis_index(n) for n in ("tile", "lev", "sub", "grp"))
-    place = jnp.stack([t, lev, sub, grp]).astype(jnp.int32)
+    shares = lax.axis_size("grp") * lax.axis_size("lev") * halves
+    share = (grp * lax.axis_size("lev") + lev) * halves + sub
+    place = jnp.stack([t, lev, sub, grp, share]).astype(jnp.int32)
     chunks = members // CHUNK
     rows = levels * CHUNK
     entries = blocks + tiles - 1
     swap = [(0, 1), (1, 0)]
 
     state = control.transpose(1, 2, 0)
-    mine = [state[:, c * CHUNK : (c + 1) * CHUNK].reshape(rows, nodes) for c in range(chunks)]
+    mine = [state[:, :CHUNK].reshape(rows, nodes)]
+    state = after(state, mine[0])
+    mine += [state[:, c * CHUNK : (c + 1) * CHUNK].reshape(rows, nodes) for c in range(1, chunks)]
     theirs = [lax.ppermute(x, "lev", swap) for x in mine]
 
-    merged = pl.pallas_call(
+    merged, pieces = pl.pallas_call(
         functools.partial(merge_kernel, tiles),
         in_specs=[SMEM, SMEM, SMEM, VMEM],
-        out_specs=VMEM,
-        out_shape=jax.ShapeDtypeStruct((blocks, entries, size, size), BF16),
+        out_specs=[VMEM, VMEM],
+        out_shape=[
+            jax.ShapeDtypeStruct((blocks, entries, size, size), BF16),
+            jax.ShapeDtypeStruct((tiles - 1, entries, size // shares, size), BF16),
+        ],
         scratch_shapes=[pltpu.VMEM((blocks, entries, size, size), F32)],
         compiler_params=params(),
         name="merge_taps",
     )(after(place, *mine), send_list, conv_slots, conv_coef[0])
+
+    share = [
+        lax.ppermute(pieces[d - 1], "tile", [(i, i ^ d) for i in range(tiles)])
+        for d in range(1, tiles)
+    ]
+    share = jnp.stack(share)
 
     weight = pl.pallas_call(
         functools.partial(weight_kernel, levels),
@@ -216,55 +227,50 @@
             out_shape=jax.ShapeDtypeStruct((rows, nodes), BF16),
             compiler_params=params(),
             name="vertical",
-        )(node_count, weight, x, y)
+        )(node_count, after(weight, share), x, y)
         for x, y in zip(mine, theirs)
     ]
     near, across, beyond, far, farthest = ([None] * chunks for _ in range(5))
     edge_both = [(0, 1), (1, 0), (2, 3), (3, 2)]
     middle = [(1, 2), (2, 1)]
     edge_out = [(1, 0), (2, 3)]
-    edge = []
-
-    def edge_send(value, pairs):
-        if len(edge) > 1:
-            value = after(value, edge[-2])
-        edge.append(lax.ppermute(value, "tile", pairs))
-        return edge[-1]
-
-    def do_near(c):
-        near[c] = edge_send(vertical[c], edge_both)
-        across[c] = lax.ppermute(after(vertical[c], *edge[:-1][-2:-1]), "tile", middle)
-        beyond[c] = lax.ppermute(near[c], "tile", middle)
-
-    def do_far(c):
-        far[c] = edge_send(across[c], edge_out)
-
-    def do_farthest(c):
-        farthest[c] = edge_send(beyond[c], edge_out)
-
-    do_near(0)
-    do_far(0)
-    for c in range(1, chunks):
-        do_near(c)
-        do_farthest(c - 1)
-        do_far(c)
-    do_farthest(chunks - 1)
-
-    shares = lax.axis_size("grp") * lax.axis_size("lev") * halves
-    share = (grp * lax.axis_size("lev") + lev) * halves + sub
-    part = size // shares
-    pieces = []
-    for d in range(1, tiles):
-        target = t ^ d
-        block = send_list[t, target, 0]
-        piece = lax.dynamic_slice(
-            merged, (block, 0, share * part, 0), (1, entries, part, size)
-        )[0]
-        ring = [(i, i ^ d) for i in range(tiles)]
-        pieces.append(lax.ppermute(piece, "tile", ring))
-    gathered = after(jnp.stack(pieces), vertical[0])
-    for axis in ("lev", "grp", "sub"):
-        gathered = jnp.stack([gathered, lax.ppermute(gathered, axis, swap)])
+    slots = []
+
+    def slot(kind, c, *others):
+        others = others + tuple(slots[-2] if len(slots) > 1 else ())
+        if kind == "near":
+            value = after(vertical[c], *others)
+            near[c] = lax.ppermute(value, "tile", edge_both)
+            across[c] = lax.ppermute(value, "tile", middle)
+            slots.append((near[c], across[c]))
+        elif kind == "far":
+            far[c] = lax.ppermute(after(across[c], *others), "tile", edge_out)
+            beyond[c] = lax.ppermute(after(near[c], *others), "tile", middle)
+            slots.append((far[c], beyond[c]))
+        else:
+            farthest[c] = lax.ppermute(after(beyond[c], *others), "tile", edge_out)
+            slots.append((farthest[c],))
+
+    slot("near", 0)
+    slot("far", 0, vertical[1])
+    slot("near", 1)
+    slot("farthest", 0)
+    slot("near", 2)
+    slot("far", 1, vertical[2])
+    slot("farthest", 1)
+    slot("far", 2)
+    slot("farthest", 2)
+
+    share = after(share, vertical[0])
+    corner = [(0, 3), (1, 2), (2, 1), (3, 0)]
+    shares = [
+        share,
+        lax.ppermute(share, "lev", swap),
+        lax.ppermute(share, "grp", swap),
+        lax.ppermute(share, ("grp", "lev"), corner),
+    ]
+    gathered = jnp.stack(shares)
+    gathered = jnp.stack([gathered, lax.ppermute(gathered, "sub", swap)])
 
     def spread(place, c):
         return pl.pallas_call(
@@ -288,7 +294,7 @@
         other = lax.ppermute(fields, "sub", swap)
         for half, field in enumerate((fields, other)):
             result = interpolate(
-                c, half, tiles, place, send_list, interp_slots, interp_coef, field, shape, result
+                c, half, 0, tiles, place, send_list, interp_slots, interp_coef, field, shape, result
             )
             if half == 0:
                 ready = [result]

time: 145 us -> 137 us (0.945)
  between operations: 6.62 us -> 1.18 us
  waiting for transfers between devices: 53.8 us -> 50.6 us
  starting transfers between devices: 48.4 us -> 51 us
  Pallas kernels: 32 us -> 30.1 us
    ppermute x21 -> x22, waiting for transfers between devices: 49.3 us -> 43.4 us  [the longest x3 21.9 us: slot(): farthest[c] = lax.ppermute(after(beyond[c], *others), 'tile', edge_out)]
    ppermute x21 -> x22, starting transfers between devices: 26.4 us -> 31.3 us  [the longest x3 8.98 us: slot(): near[c] = lax.ppermute(value, 'tile', edge_both)]
    pallas_call x6, Pallas kernels: 17.8 us -> 14.6 us  [interpolate(): pl.pallas_call(functools.partial(interp_kernel, tiles, chunk, chunks, hal...]
    ppermute x3, starting transfers between devices: 19.4 us -> 16.4 us  [local(): other = lax.ppermute(fields, 'sub', swap)]
    ppermute x3, waiting for transfers between devices: 4.54 us -> 7.23 us  [local(): theirs = [lax.ppermute(x, 'lev', swap) for x in mine]]
  transfers between devices with their start and end apart: 27 -> 28, of which waited for: 12 -> 12; matrix products, arithmetic and copies ran while one was open for 1% -> 2% of each run, Pallas kernels for 19% -> 20%
where the time goes in v3:
time: 137 us
  starting transfers between devices  51 us (37%)
  waiting for transfers between devices  50.6 us (37%)
  Pallas kernels  30.1 us (22%)
  local copies, waits for them, and re-layouts  3.54 us (3%)
    ppermute x3, waiting for transfers between devices, slot(): farthest[c] = lax.ppermute(after(beyond[c], *others), 'tile', edge_out)  21.9 us
    ppermute x3, starting transfers between devices, local(): other = lax.ppermute(fields, 'sub', swap)  16.4 us
    pallas_call x6, Pallas kernels, interpolate(): pl.pallas_call(functools.partial(interp_kernel, tiles, chunk, chunks, hal...  14.6 us
    ppermute x3, waiting for transfers between devices, slot(): far[c] = lax.ppermute(after(across[c], *others), 'tile', edge_out)  11.2 us
    ppermute x3, starting transfers between devices, slot(): near[c] = lax.ppermute(value, 'tile', edge_both)  8.98 us
    pallas_call x3, Pallas kernels, spread(): pl.pallas_call(functools.partial(spread_kernel, tiles), in_specs=[SMEM, S...  8.61 us
    ppermute x3, waiting for transfers between devices, local(): theirs = [lax.ppermute(x, 'lev', swap) for x in mine]  7.23 us
    pallas_call x3, Pallas kernels, local(): pl.pallas_call(vertical_kernel, in_specs=[SMEM, VMEM, VMEM, VMEM], out_sp...  4.36 us
  transfers between devices with their start and end apart: 28, of which 12 were waited for; matrix products, arithmetic and copies ran while one was open for 2% of the time, Pallas kernels for 20%

profile of v3, /device:TPU:1, one launch (start us, length us, event | category | flops | bytes accessed | tf_op | source)
XLA Modules:
  0.0 136.8 jit_solution(11026985256535983914)
XLA Ops:
  0.0 1.2 slice.24
  1.2 2.1 %collective-permute-start.3 = (bf16[512,512]{1,0:T(8,128)(2,1)S(1)}, bf16[512,512]{1,0:T(8,128)(2,1)}, u32[]{:S(2)}, u32[]{:S(2)}) collective-permute-start(bf16[512,512]{1,0:T(8,128)(2,1)S(1)} %bitcast.28), channel_id=1, source_target_pairs={{0,2},{2,0},{1,3},{3,1},{4,6},{6,4},{5,7},{7,5},{8,10},{10,8},{9,1... | collective-permute-start | bytes 1572872 | tf_op jit(solution)/shard_map/ppermute | solution.py:192
  3.4 2.1 %fusion.1 = (bf16[32,16,512]{2,1,0:T(8,128)(2,1)S(1)}, bf16[32,16,512]{2,1,0:T(8,128)(2,1)}) fusion(bf16[32,48,512]{2,1,0:T(8,128)(2,1)} %bitcast.33), kind=kLoop, calls=%fused_computation.7 | loop fusion | bytes 2097152 | tf_op jit(solution)/shard_map/slice | solution.py:191
  5.6 1.4 %merge_taps.1 = (bf16[2,5,256,256]{3,2,1,0:T(8,128)(2,1)S(1)}, bf16[3,5,32,256]{3,2,1,0:T(8,128)(2,1)S(1)}) custom-call(s32[5]{0:T(128)S(1)} %stack.59.place, s32[4,4,1]{2,1,0:T(4,128)S(1)} %copy.28.send, s32[1,2,9]{2,1,0:T(2,128)S(1)} %copy-done.3, bf16[2,9,256,256]{3,2,1,0:T(8,128)(2,1)S(1)} %bitcast.27), custom_call_target="tpu_custom_call" | custom-call | tf_op jit(solution)/shard_map/merge_taps/pallas_call | solution.py:194
  7.1 1.6 %collective-permute-start = (bf16[5,32,256]{2,1,0:T(8,128)(2,1)S(1)}, bf16[5,32,256]{2,1,0:T(8,128)(2,1)S(1)}, u32[]{:S(2)}, u32[]{:S(2)}) collective-permute-start(bf16[5,32,256]{2,1,0:T(8,128)(2,1)S(1)} %get-tuple-element.49), channel_id=1, source_target_pairs={{0,4},{4,0},{8,12},{12,8},{1,5},{5,1},{9,13},{13,9},{2,6},{6,2},{1... | collective-permute-start | bytes 245768 | tf_op jit(solution)/shard_map/ppermute | solution.py:208
  8.7 2.3 %collective-permute-start.1 = (bf16[5,32,256]{2,1,0:T(8,128)(2,1)S(1)}, bf16[5,32,256]{2,1,0:T(8,128)(2,1)S(1)}, u32[]{:S(2)}, u32[]{:S(2)}) collective-permute-start(bf16[5,32,256]{2,1,0:T(8,128)(2,1)S(1)} %get-tuple-element.51), channel_id=1, source_target_pairs={{0,8},{4,12},{8,0},{12,4},{1,9},{5,13},{9,1},{13,5},{2,10},{6,14},... | collective-permute-start | bytes 245768 | tf_op jit(solution)/shard_map/ppermute | solution.py:208
  11.7 1.1 level_weights.1.weight
  12.8 1.0 collective-permute-done.1
  13.8 2.6 %collective-permute-done.2 = bf16[5,32,256]{2,1,0:T(8,128)(2,1)S(1)} collective-permute-done((bf16[5,32,256]{2,1,0:T(8,128)(2,1)S(1)}, bf16[5,32,256]{2,1,0:T(8,128)(2,1)S(1)}, u32[]{:S(2)}, u32[]{:S(2)}) %collective-permute-start.2) | collective-permute-done | bytes 81952 | tf_op jit(solution)/shard_map/ppermute | solution.py:208
  16.4 1.7 %vertical.3.own = bf16[512,512]{1,0:T(8,128)(2,1)S(1)} custom-call(s32[1]{0:T(128)S(6)} %copy.35.count, bf16[2,512,512]{2,1,0:T(8,128)(2,1)S(1)} %level_weights.1.weight, bf16[512,512]{1,0:T(8,128)(2,1)S(1)} %bitcast.29, bf16[512,512]{1,0:T(8,128)(2,1)} %collective-permute-done.3.other), custom_call_target="tpu_custom_call" | custom-call | tf_op jit(solution)/shard_map/vertical/pallas_call | solution.py:223
  18.1 0.7 collective-permute-start.11
  18.8 4.6 %collective-permute-start.8 = (bf16[512,512]{1,0:T(8,128)(2,1)S(1)}, bf16[512,512]{1,0:T(8,128)(2,1)S(1)}, u32[]{:S(2)}, u32[]{:S(2)}) collective-permute-start(bf16[512,512]{1,0:T(8,128)(2,1)S(1)} %vertical.3.own), channel_id=1, source_target_pairs={{0,4},{4,0},{8,12},{12,8},{1,5},{5,1},{9,13},{13,9},{2,6},{6,2},{1... | collective-permute-start | bytes 1572872 | tf_op jit(solution)/shard_map/ppermute | solution.py:243
  23.4 1.2 collective-permute-start.4
  24.6 1.2 collective-permute-start.5
  26.3 2.1 %collective-permute-start.6 = (bf16[3,5,32,256]{3,2,1,0:T(8,128)(2,1)S(1)}, bf16[3,5,32,256]{3,2,1,0:T(8,128)(2,1)S(1)}, u32[]{:S(2)}, u32[]{:S(2)}) collective-permute-start(bf16[3,5,32,256]{3,2,1,0:T(8,128)(2,1)S(1)} %pad_maximum_fusion.2), channel_id=1, source_target_pairs={{0,18},{2,16},{16,2},{18,0},{1,19},{3,17},{17,3},{19,1},{4,22},{6,... | collective-permute-start | bytes 737288 | tf_op jit(solution)/shard_map/ppermute | solution.py:270
  28.4 1.9 %vertical.4.own = bf16[512,512]{1,0:T(8,128)(2,1)S(1)} custom-call(s32[1]{0:T(128)S(6)} %copy.35.count, bf16[2,512,512]{2,1,0:T(8,128)(2,1)S(1)} %level_weights.1.weight, bf16[512,512]{1,0:T(8,128)(2,1)} %bitcast.7.own, bf16[512,512]{1,0:T(8,128)(2,1)} %collective-permute-done.9.other), custom_call_target="tpu_custom_call" | custom-call | tf_op jit(solution)/shard_map/vertical/pallas_call | solution.py:223
  30.4 1.3 collective-permute-start.12
  31.7 2.0 %collective-permute-done.8.near = bf16[512,512]{1,0:T(8,128)(2,1)S(1)} collective-permute-done((bf16[512,512]{1,0:T(8,128)(2,1)S(1)}, bf16[512,512]{1,0:T(8,128)(2,1)S(1)}, u32[]{:S(2)}, u32[]{:S(2)}) %collective-permute-start.8) | collective-permute-done | bytes 524320 | tf_op jit(solution)/shard_map/ppermute | solution.py:243
  34.4 2.8 %collective-permute-done.6 = bf16[3,5,32,256]{3,2,1,0:T(8,128)(2,1)S(1)} collective-permute-done((bf16[3,5,32,256]{3,2,1,0:T(8,128)(2,1)S(1)}, bf16[3,5,32,256]{3,2,1,0:T(8,128)(2,1)S(1)}, u32[]{:S(2)}, u32[]{:S(2)}) %collective-permute-start.6) | collective-permute-done | bytes 245792 | tf_op jit(solution)/shard_map/ppermute | solution.py:270
  37.4 2.0 %collective-permute-start.7 = (bf16[4,3,5,32,256]{4,3,2,1,0:T(8,128)(2,1)S(1)}, bf16[4,3,5,32,256]{4,3,2,1,0:T(8,128)(2,1)S(1)}, u32[]{:S(2)}, u32[]{:S(2)}) collective-permute-start(bf16[4,3,5,32,256]{4,3,2,1,0:T(8,128)(2,1)S(1)} %get-tuple-element.48), channel_id=1, source_target_pairs={{0,1},{1,0},{2,3},{3,2},{4,5},{5,4},{6,7},{7,6},{8,9},{9,8},{10,11... | collective-permute-start | bytes 2949128 | tf_op jit(solution)/shard_map/ppermute | solution.py:273
  39.4 1.2 collective-permute-start.15
  40.7 2.0 %collective-permute-start.14 = (bf16[512,512]{1,0:T(8,128)(2,1)S(1)}, bf16[512,512]{1,0:T(8,128)(2,1)S(1)}, u32[]{:S(2)}, u32[]{:S(2)}) collective-permute-start(bf16[512,512]{1,0:T(8,128)(2,1)S(1)} %vertical.4.own), channel_id=1, source_target_pairs={{0,4},{4,0},{8,12},{12,8},{1,5},{5,1},{9,13},{13,9},{2,6},{6,2},{1... | collective-permute-start | bytes 1572872 | tf_op jit(solution)/shard_map/ppermute | solution.py:243
  42.7 1.5 %collective-permute-done.12.far = bf16[512,512]{1,0:T(8,128)(2,1)S(1)} collective-permute-done((bf16[512,512]{1,0:T(8,128)(2,1)S(1)}, bf16[512,512]{1,0:T(8,128)(2,1)S(1)}, u32[]{:S(2)}, u32[]{:S(2)}) %collective-permute-start.12) | collective-permute-done | bytes 524320 | tf_op jit(solution)/shard_map/ppermute | solution.py:247
  44.9 1.3 collective-permute-start.13
  46.2 6.7 %collective-permute-done.15.other = bf16[512,512]{1,0:T(8,128)(2,1)S(1)} collective-permute-done((bf16[512,512]{1,0:T(8,128)(2,1)S(1)}, bf16[512,512]{1,0:T(8,128)(2,1)S(1)}, u32[]{:S(2)}, u32[]{:S(2)}) %collective-permute-start.15) | collective-permute-done | bytes 524320 | tf_op jit(solution)/shard_map/ppermute | solution.py:192
  52.9 0.7 vertical.5.own
  53.7 1.8 %collective-permute-done.14.near = bf16[512,512]{1,0:T(8,128)(2,1)S(1)} collective-permute-done((bf16[512,512]{1,0:T(8,128)(2,1)S(1)}, bf16[512,512]{1,0:T(8,128)(2,1)S(1)}, u32[]{:S(2)}, u32[]{:S(2)}) %collective-permute-start.14) | collective-permute-done | bytes 524320 | tf_op jit(solution)/shard_map/ppermute | solution.py:243
  55.4 2.4 %collective-permute-start.19 = (bf16[512,512]{1,0:T(8,128)(2,1)S(1)}, bf16[512,512]{1,0:T(8,128)(2,1)S(1)}, u32[]{:S(2)}, u32[]{:S(2)}) collective-permute-start(bf16[512,512]{1,0:T(8,128)(2,1)S(1)} %vertical.5.own), channel_id=1, source_target_pairs={{0,4},{4,0},{8,12},{12,8},{1,5},{5,1},{9,13},{13,9},{2,6},{6,2},{1... | collective-permute-start | bytes 1572872 | tf_op jit(solution)/shard_map/ppermute | solution.py:243
  58.5 8.2 %collective-permute-done.13.farthest = bf16[512,512]{1,0:T(8,128)(2,1)S(1)} collective-permute-done((bf16[512,512]{1,0:T(8,128)(2,1)S(1)}, bf16[512,512]{1,0:T(8,128)(2,1)S(1)}, u32[]{:S(2)}, u32[]{:S(2)}) %collective-permute-start.13) | collective-permute-done | bytes 524320 | tf_op jit(solution)/shard_map/ppermute | solution.py:251
  67.4 1.3 collective-permute-start.18
  68.9 2.8 %spread.3.field = bf16[5,512,256]{2,1,0:T(8,128)(2,1)S(1)} custom-call(s32[5]{0:T(128)S(1)} %stack.59.place, s32[4,4,1]{2,1,0:T(4,128)S(1)} %copy.28.send, bf16[2,5,256,256]{3,2,1,0:T(8,128)(2,1)S(1)} %get-tuple-element.27.coef_own, bf16[2,4,3,5,32,256]{5,4,3,2,1,0:T(8,128)(2,1)S(1)} %pad_maximum_fusion.coef_lent, bf16[512,512]{1,0:T(8,128)(2,1)S(1)} %vertical.3.own, ...), custom_call_target="tpu_custom_call" | custom-call | tf_op jit(solution)/shard_map/spread/pallas_call | solution.py:276
  71.7 6.5 %collective-permute-start.22 = (bf16[5,512,256]{2,1,0:T(8,128)(2,1)S(1)}, bf16[5,512,256]{2,1,0:T(8,128)(2,1)S(1)}, u32[]{:S(2)}, u32[]{:S(2)}) collective-permute-start(bf16[5,512,256]{2,1,0:T(8,128)(2,1)S(1)} %spread.3.field), channel_id=1, source_target_pairs={{0,1},{1,0},{2,3},{3,2},{4,5},{5,4},{6,7},{7,6},{8,9},{9,8},{10,11... | collective-permute-start | bytes 3932168 | tf_op jit(solution)/shard_map/ppermute | solution.py:294
  78.2 1.3 collective-permute-start.21
  79.5 9.7 %collective-permute-done.18.far = bf16[512,512]{1,0:T(8,128)(2,1)S(1)} collective-permute-done((bf16[512,512]{1,0:T(8,128)(2,1)S(1)}, bf16[512,512]{1,0:T(8,128)(2,1)S(1)}, u32[]{:S(2)}, u32[]{:S(2)}) %collective-permute-start.18) | collective-permute-done | bytes 524320 | tf_op jit(solution)/shard_map/ppermute | solution.py:247
  89.8 1.3 collective-permute-start.24
  91.1 9.2 %collective-permute-done.21.farthest = bf16[512,512]{1,0:T(8,128)(2,1)S(1)} collective-permute-done((bf16[512,512]{1,0:T(8,128)(2,1)S(1)}, bf16[512,512]{1,0:T(8,128)(2,1)S(1)}, u32[]{:S(2)}, u32[]{:S(2)}) %collective-permute-start.21) | collective-permute-done | bytes 524320 | tf_op jit(solution)/shard_map/ppermute | solution.py:251
  100.4 1.3 collective-permute-start.25
  101.7 2.4 %interpolate.6.rest_0_ = bf16[32,96,768]{2,1,0:T(8,128)(2,1)} custom-call(s32[5]{0:T(128)S(1)} %stack.59.place, s32[4,4,1]{2,1,0:T(4,128)S(1)} %copy.28.send, s32[2,3,3]{2,1,0:T(4,128)S(1)} %copy.29.slots, bf16[1,3,3,256,256]{4,3,2,1,0:T(8,128)(2,1)S(1)} %copy-done, bf16[5,512,256]{2,1,0:T(8,128)(2,1)S(1)} %spread.3.field), custom_call_target="tpu_custom_call" | custom-call | tf_op jit(solution)/shard_map/interpolate/pallas_call | solution.py:156
  104.1 2.8 %spread.4.field = bf16[5,512,256]{2,1,0:T(8,128)(2,1)S(1)} custom-call(s32[5]{0:T(128)S(1)} %stack.59.place, s32[4,4,1]{2,1,0:T(4,128)S(1)} %copy.28.send, bf16[2,5,256,256]{3,2,1,0:T(8,128)(2,1)S(1)} %get-tuple-element.27.coef_own, bf16[2,4,3,5,32,256]{5,4,3,2,1,0:T(8,128)(2,1)S(1)} %pad_maximum_fusion.coef_lent, bf16[512,512]{1,0:T(8,128)(2,1)S(1)} %vertical.4.own, ...), custom_call_target="tpu_custom_call" | custom-call | tf_op jit(solution)/shard_map/spread/pallas_call | solution.py:276
  107.0 6.5 %collective-permute-start.27 = (bf16[5,512,256]{2,1,0:T(8,128)(2,1)S(1)}, bf16[5,512,256]{2,1,0:T(8,128)(2,1)S(1)}, u32[]{:S(2)}, u32[]{:S(2)}) collective-permute-start(bf16[5,512,256]{2,1,0:T(8,128)(2,1)S(1)} %spread.4.field), channel_id=1, source_target_pairs={{0,1},{1,0},{2,3},{3,2},{4,5},{5,4},{6,7},{7,6},{8,9},{9,8},{10,11... | collective-permute-start | bytes 3932168 | tf_op jit(solution)/shard_map/ppermute | solution.py:294
  113.4 2.4 %interpolate.7.rest_0_ = bf16[32,96,768]{2,1,0:T(8,128)(2,1)} custom-call(s32[5]{0:T(128)S(1)} %stack.59.place, s32[4,4,1]{2,1,0:T(4,128)S(1)} %copy.28.send, s32[2,3,3]{2,1,0:T(4,128)S(1)} %copy.29.slots, bf16[1,3,3,256,256]{4,3,2,1,0:T(8,128)(2,1)S(1)} %copy-done, ...), custom_call_target="tpu_custom_call", output_to_operand_aliasing={{}: (5, {})} | custom-call | tf_op jit(solution)/shard_map/interpolate/pallas_call | solution.py:156
  115.9 2.4 %interpolate.8.rest_0_ = bf16[32,96,768]{2,1,0:T(8,128)(2,1)} custom-call(s32[5]{0:T(128)S(1)} %stack.59.place, s32[4,4,1]{2,1,0:T(4,128)S(1)} %copy.28.send, s32[2,3,3]{2,1,0:T(4,128)S(1)} %copy.29.slots, bf16[1,3,3,256,256]{4,3,2,1,0:T(8,128)(2,1)S(1)} %copy-done, bf16[5,512,256]{2,1,0:T(8,128)(2,1)S(1)} %spread.4.field, ...), custom_call_target="tpu_custom_call", output_to_operand_aliasing={{}: (5, {})} | custom-call | tf_op jit(solution)/shard_map/interpolate/pallas_call | solution.py:156
  118.3 4.5 %collective-permute-done.25.farthest = bf16[512,512]{1,0:T(8,128)(2,1)S(1)} collective-permute-done((bf16[512,512]{1,0:T(8,128)(2,1)S(1)}, bf16[512,512]{1,0:T(8,128)(2,1)S(1)}, u32[]{:S(2)}, u32[]{:S(2)}) %collective-permute-start.25) | collective-permute-done | bytes 524320 | tf_op jit(solution)/shard_map/ppermute | solution.py:251
  122.8 3.0 %spread.5.field = bf16[5,512,256]{2,1,0:T(8,128)(2,1)S(1)} custom-call(s32[5]{0:T(128)S(1)} %stack.59.place, s32[4,4,1]{2,1,0:T(4,128)S(1)} %copy.28.send, bf16[2,5,256,256]{3,2,1,0:T(8,128)(2,1)S(1)} %get-tuple-element.27.coef_own, bf16[2,4,3,5,32,256]{5,4,3,2,1,0:T(8,128)(2,1)S(1)} %pad_maximum_fusion.coef_lent, bf16[512,512]{1,0:T(8,128)(2,1)S(1)} %vertical.5.own, ...), custom_call_target="tpu_custom_call" | custom-call | tf_op jit(solution)/shard_map/spread/pallas_call | solution.py:276
  125.8 3.5 %collective-permute-start.26 = (bf16[5,512,256]{2,1,0:T(8,128)(2,1)S(1)}, bf16[5,512,256]{2,1,0:T(8,128)(2,1)S(1)}, u32[]{:S(2)}, u32[]{:S(2)}) collective-permute-start(bf16[5,512,256]{2,1,0:T(8,128)(2,1)S(1)} %spread.5.field), channel_id=1, source_target_pairs={{0,1},{1,0},{2,3},{3,2},{4,5},{5,4},{6,7},{7,6},{8,9},{9,8},{10,11... | collective-permute-start | bytes 3932168 | tf_op jit(solution)/shard_map/ppermute | solution.py:294
  129.3 2.4 %interpolate.9.rest_0_ = bf16[32,96,768]{2,1,0:T(8,128)(2,1)} custom-call(s32[5]{0:T(128)S(1)} %stack.59.place, s32[4,4,1]{2,1,0:T(4,128)S(1)} %copy.28.send, s32[2,3,3]{2,1,0:T(4,128)S(1)} %copy.29.slots, bf16[1,3,3,256,256]{4,3,2,1,0:T(8,128)(2,1)S(1)} %copy-done, ...), custom_call_target="tpu_custom_call", output_to_operand_aliasing={{}: (5, {})} | custom-call | tf_op jit(solution)/shard_map/interpolate/pallas_call | solution.py:156
  131.7 2.4 %interpolate.10.rest_0_ = bf16[32,96,768]{2,1,0:T(8,128)(2,1)} custom-call(s32[5]{0:T(128)S(1)} %stack.59.place, s32[4,4,1]{2,1,0:T(4,128)S(1)} %copy.28.send, s32[2,3,3]{2,1,0:T(4,128)S(1)} %copy.29.slots, bf16[1,3,3,256,256]{4,3,2,1,0:T(8,128)(2,1)S(1)} %copy-done, bf16[5,512,256]{2,1,0:T(8,128)(2,1)S(1)} %spread.5.field, ...), custom_call_target="tpu_custom_call", output_to_operand_aliasing={{}: (5, {})} | custom-call | tf_op jit(solution)/shard_map/interpolate/pallas_call | solution.py:156
  134.2 2.4 %interpolate.11 = bf16[32,96,768]{2,1,0:T(8,128)(2,1)} custom-call(s32[5]{0:T(128)S(1)} %stack.59.place, s32[4,4,1]{2,1,0:T(4,128)S(1)} %copy.28.send, s32[2,3,3]{2,1,0:T(4,128)S(1)} %copy.29.slots, bf16[1,3,3,256,256]{4,3,2,1,0:T(8,128)(2,1)S(1)} %copy-done, bf16[5,512,256]{2,1,0:T(8,128)(2,1)S(1)} %collective-permute-done.26.field, ...), custom_call_target="tpu_custom_call", output_to_operand_aliasing={{}: (5, {})} | custom-call | tf_op jit(solution)/shard_map/interpolate/pallas_call | solution.py:156
  (43 shorter events, 4.6 us)
Async XLA Ops:
  0.0 5.5 %copy-start.5 = (s32[4,4,1]{1,2,0:T(1,128)S(1)}, s32[4,4,1]{1,2,0:T(1,128)}, u32[]{:S(2)}) copy-start(s32[4,4,1]{1,2,0:T(1,128)} %param.11) | copy-start | bytes 196
  0.0 5.6 %copy-start.1 = (bf16[1,2,9,256,256]{4,3,2,1,0:T(8,128)(2,1)S(1)}, bf16[1,2,9,256,256]{4,3,2,1,0:T(8,128)(2,1)}, u32[]{:S(2)}) copy-start(bf16[1,2,9,256,256]{4,3,2,1,0:T(8,128)(2,1)} %param.13) | copy-start | bytes 7077892
  0.0 5.6 %copy-start.3 = (s32[1,2,9]{2,1,0:T(2,128)S(1)}, s32[1,2,9]{2,1,0:T(2,128)}, u32[]{:S(2)}) copy-start(s32[1,2,9]{2,1,0:T(2,128)} %slots.7) | copy-start | bytes 220
  1.2 15.1 %collective-permute-start.3 = (bf16[512,512]{1,0:T(8,128)(2,1)S(1)}, bf16[512,512]{1,0:T(8,128)(2,1)}, u32[]{:S(2)}, u32[]{:S(2)}) collective-permute-start(bf16[512,512]{1,0:T(8,128)(2,1)S(1)} %bitcast.28), channel_id=1, source_target_pairs={{0,2},{2,0},{1,3},{3,1},{4,6},{6,4},{5,7},{7,5},{8,10},{10,8},{9,1... | collective-permute-start | bytes 1572872 | tf_op jit(solution)/shard_map/ppermute | solution.py:192
  5.4 6.2 %copy-start.2 = (bf16[64,64]{1,0:T(8,128)(2,1)S(1)}, bf16[64,64]{1,0:T(8,128)(2,1)}, u32[]{:S(2)}) copy-start(bf16[64,64]{1,0:T(8,128)(2,1)} %vert.1) | copy-start | bytes 24580
  5.4 20.9 %collective-permute-start.9 = (bf16[512,512]{1,0:T(8,128)(2,1)}, bf16[512,512]{1,0:T(8,128)(2,1)}, u32[]{:S(2)}, u32[]{:S(2)}) collective-permute-start(bf16[512,512]{1,0:T(8,128)(2,1)} %bitcast.7.own), channel_id=1, source_target_pairs={{0,2},{2,0},{1,3},{3,1},{4,6},{6,4},{5,7},{7,5},{8,10},{10,8},{9,1... | collective-permute-start | bytes 1572872 | tf_op jit(solution)/shard_map/ppermute | solution.py:192
  7.1 5.6 %collective-permute-start = (bf16[5,32,256]{2,1,0:T(8,128)(2,1)S(1)}, bf16[5,32,256]{2,1,0:T(8,128)(2,1)S(1)}, u32[]{:S(2)}, u32[]{:S(2)}) collective-permute-start(bf16[5,32,256]{2,1,0:T(8,128)(2,1)S(1)} %get-tuple-element.49), channel_id=1, source_target_pairs={{0,4},{4,0},{8,12},{12,8},{1,5},{5,1},{9,13},{13,9},{2,6},{6,2},{1... | collective-permute-start | bytes 245768 | tf_op jit(solution)/shard_map/ppermute | solution.py:208
  8.7 5.1 %collective-permute-start.1 = (bf16[5,32,256]{2,1,0:T(8,128)(2,1)S(1)}, bf16[5,32,256]{2,1,0:T(8,128)(2,1)S(1)}, u32[]{:S(2)}, u32[]{:S(2)}) collective-permute-start(bf16[5,32,256]{2,1,0:T(8,128)(2,1)S(1)} %get-tuple-element.51), channel_id=1, source_target_pairs={{0,8},{4,12},{8,0},{12,4},{1,9},{5,13},{9,1},{13,5},{2,10},{6,14},... | collective-permute-start | bytes 245768 | tf_op jit(solution)/shard_map/ppermute | solution.py:208
  11.0 5.3 %collective-permute-start.2 = (bf16[5,32,256]{2,1,0:T(8,128)(2,1)S(1)}, bf16[5,32,256]{2,1,0:T(8,128)(2,1)S(1)}, u32[]{:S(2)}, u32[]{:S(2)}) collective-permute-start(bf16[5,32,256]{2,1,0:T(8,128)(2,1)S(1)} %get-tuple-element.50), channel_id=1, source_target_pairs={{0,12},{4,8},{8,4},{12,0},{1,13},{5,9},{9,5},{13,1},{2,14},{6,10},... | collective-permute-start | bytes 245768 | tf_op jit(solution)/shard_map/ppermute | solution.py:208
  18.1 12.2 %collective-permute-start.11 = (bf16[512,512]{1,0:T(8,128)(2,1)S(1)}, bf16[512,512]{1,0:T(8,128)(2,1)S(1)}, u32[]{:S(2)}, u32[]{:S(2)}) collective-permute-start(bf16[512,512]{1,0:T(8,128)(2,1)S(1)} %vertical.3.own), channel_id=1, source_target_pairs={{4,8},{8,4},{5,9},{9,5},{6,10},{10,6},{7,11},{11,7},{20,24},{24,20... | collective-permute-start | bytes 1572872 | tf_op jit(solution)/shard_map/ppermute | solution.py:244
  18.8 14.9 %collective-permute-start.8 = (bf16[512,512]{1,0:T(8,128)(2,1)S(1)}, bf16[512,512]{1,0:T(8,128)(2,1)S(1)}, u32[]{:S(2)}, u32[]{:S(2)}) collective-permute-start(bf16[512,512]{1,0:T(8,128)(2,1)S(1)} %vertical.3.own), channel_id=1, source_target_pairs={{0,4},{4,0},{8,12},{12,8},{1,5},{5,1},{9,13},{13,9},{2,6},{6,2},{1... | collective-permute-start | bytes 1572872 | tf_op jit(solution)/shard_map/ppermute | solution.py:243
  23.4 11.0 %collective-permute-start.4 = (bf16[3,5,32,256]{3,2,1,0:T(8,128)(2,1)S(1)}, bf16[3,5,32,256]{3,2,1,0:T(8,128)(2,1)S(1)}, u32[]{:S(2)}, u32[]{:S(2)}) collective-permute-start(bf16[3,5,32,256]{3,2,1,0:T(8,128)(2,1)S(1)} %pad_maximum_fusion.2), channel_id=1, source_target_pairs={{0,2},{2,0},{1,3},{3,1},{4,6},{6,4},{5,7},{7,5},{8,10},{10,8},{9,1... | collective-permute-start | bytes 737288 | tf_op jit(solution)/shard_map/ppermute | solution.py:268
  24.6 9.8 %collective-permute-start.5 = (bf16[3,5,32,256]{3,2,1,0:T(8,128)(2,1)S(1)}, bf16[3,5,32,256]{3,2,1,0:T(8,128)(2,1)S(1)}, u32[]{:S(2)}, u32[]{:S(2)}) collective-permute-start(bf16[3,5,32,256]{3,2,1,0:T(8,128)(2,1)S(1)} %pad_maximum_fusion.2), channel_id=1, source_target_pairs={{0,16},{16,0},{1,17},{17,1},{2,18},{18,2},{3,19},{19,3},{4,20},{20... | collective-permute-start | bytes 737288 | tf_op jit(solution)/shard_map/ppermute | solution.py:269
  26.3 10.9 %collective-permute-start.6 = (bf16[3,5,32,256]{3,2,1,0:T(8,128)(2,1)S(1)}, bf16[3,5,32,256]{3,2,1,0:T(8,128)(2,1)S(1)}, u32[]{:S(2)}, u32[]{:S(2)}) collective-permute-start(bf16[3,5,32,256]{3,2,1,0:T(8,128)(2,1)S(1)} %pad_maximum_fusion.2), channel_id=1, source_target_pairs={{0,18},{2,16},{16,2},{18,0},{1,19},{3,17},{17,3},{19,1},{4,22},{6,... | collective-permute-start | bytes 737288 | tf_op jit(solution)/shard_map/ppermute | solution.py:270
  30.4 13.8 %collective-permute-start.12 = (bf16[512,512]{1,0:T(8,128)(2,1)S(1)}, bf16[512,512]{1,0:T(8,128)(2,1)S(1)}, u32[]{:S(2)}, u32[]{:S(2)}) collective-permute-start(bf16[512,512]{1,0:T(8,128)(2,1)S(1)} %collective-permute-done.11.across), channel_id=1, source_target_pairs={{4,0},{8,12},{5,1},{9,13},{6,2},{10,14},{7,3},{11,15},{20,16},{24,... | collective-permute-start | bytes 1572872 | tf_op jit(solution)/shard_map/ppermute | solution.py:247
  33.7 11.2 %collective-permute-start.10 = (bf16[512,512]{1,0:T(8,128)(2,1)S(1)}, bf16[512,512]{1,0:T(8,128)(2,1)S(1)}, u32[]{:S(2)}, u32[]{:S(2)}) collective-permute-start(bf16[512,512]{1,0:T(8,128)(2,1)S(1)} %collective-permute-done.8.near), channel_id=1, source_target_pairs={{4,8},{8,4},{5,9},{9,5},{6,10},{10,6},{7,11},{11,7},{20,24},{24,20... | collective-permute-start | bytes 1572872 | tf_op jit(solution)/shard_map/ppermute | solution.py:248
  37.4 31.2 %collective-permute-start.7 = (bf16[4,3,5,32,256]{4,3,2,1,0:T(8,128)(2,1)S(1)}, bf16[4,3,5,32,256]{4,3,2,1,0:T(8,128)(2,1)S(1)}, u32[]{:S(2)}, u32[]{:S(2)}) collective-permute-start(bf16[4,3,5,32,256]{4,3,2,1,0:T(8,128)(2,1)S(1)} %get-tuple-element.48), channel_id=1, source_target_pairs={{0,1},{1,0},{2,3},{3,2},{4,5},{5,4},{6,7},{7,6},{8,9},{9,8},{10,11... | collective-permute-start | bytes 2949128 | tf_op jit(solution)/shard_map/ppermute | solution.py:273
  39.4 13.5 %collective-permute-start.15 = (bf16[512,512]{1,0:T(8,128)(2,1)S(1)}, bf16[512,512]{1,0:T(8,128)(2,1)S(1)}, u32[]{:S(2)}, u32[]{:S(2)}) collective-permute-start(bf16[512,512]{1,0:T(8,128)(2,1)S(1)} %bitcast.30), channel_id=1, source_target_pairs={{0,2},{2,0},{1,3},{3,1},{4,6},{6,4},{5,7},{7,5},{8,10},{10,8},{9,1... | collective-permute-start | bytes 1572872 | tf_op jit(solution)/shard_map/ppermute | solution.py:192
  40.7 14.8 %collective-permute-start.14 = (bf16[512,512]{1,0:T(8,128)(2,1)S(1)}, bf16[512,512]{1,0:T(8,128)(2,1)S(1)}, u32[]{:S(2)}, u32[]{:S(2)}) collective-permute-start(bf16[512,512]{1,0:T(8,128)(2,1)S(1)} %vertical.4.own), channel_id=1, source_target_pairs={{0,4},{4,0},{8,12},{12,8},{1,5},{5,1},{9,13},{13,9},{2,6},{6,2},{1... | collective-permute-start | bytes 1572872 | tf_op jit(solution)/shard_map/ppermute | solution.py:243
  44.2 11.2 %collective-permute-start.17 = (bf16[512,512]{1,0:T(8,128)(2,1)S(1)}, bf16[512,512]{1,0:T(8,128)(2,1)S(1)}, u32[]{:S(2)}, u32[]{:S(2)}) collective-permute-start(bf16[512,512]{1,0:T(8,128)(2,1)S(1)} %vertical.4.own), channel_id=1, source_target_pairs={{4,8},{8,4},{5,9},{9,5},{6,10},{10,6},{7,11},{11,7},{20,24},{24,20... | collective-permute-start | bytes 1572872 | tf_op jit(solution)/shard_map/ppermute | solution.py:244
  44.9 21.8 %collective-permute-start.13 = (bf16[512,512]{1,0:T(8,128)(2,1)S(1)}, bf16[512,512]{1,0:T(8,128)(2,1)S(1)}, u32[]{:S(2)}, u32[]{:S(2)}) collective-permute-start(bf16[512,512]{1,0:T(8,128)(2,1)S(1)} %collective-permute-done.10.beyond), channel_id=1, source_target_pairs={{4,0},{8,12},{5,1},{9,13},{6,2},{10,14},{7,3},{11,15},{20,16},{24,... | collective-permute-start | bytes 1572872 | tf_op jit(solution)/shard_map/ppermute | solution.py:251
  55.4 22.7 %collective-permute-start.19 = (bf16[512,512]{1,0:T(8,128)(2,1)S(1)}, bf16[512,512]{1,0:T(8,128)(2,1)S(1)}, u32[]{:S(2)}, u32[]{:S(2)}) collective-permute-start(bf16[512,512]{1,0:T(8,128)(2,1)S(1)} %vertical.5.own), channel_id=1, source_target_pairs={{0,4},{4,0},{8,12},{12,8},{1,5},{5,1},{9,13},{13,9},{2,6},{6,2},{1... | collective-permute-start | bytes 1572872 | tf_op jit(solution)/shard_map/ppermute | solution.py:243
  57.8 20.3 %collective-permute-start.20 = (bf16[512,512]{1,0:T(8,128)(2,1)S(1)}, bf16[512,512]{1,0:T(8,128)(2,1)S(1)}, u32[]{:S(2)}, u32[]{:S(2)}) collective-permute-start(bf16[512,512]{1,0:T(8,128)(2,1)S(1)} %vertical.5.own), channel_id=1, source_target_pairs={{4,8},{8,4},{5,9},{9,5},{6,10},{10,6},{7,11},{11,7},{20,24},{24,20... | collective-permute-start | bytes 1572872 | tf_op jit(solution)/shard_map/ppermute | solution.py:244
  66.7 11.5 %collective-permute-start.16 = (bf16[512,512]{1,0:T(8,128)(2,1)S(1)}, bf16[512,512]{1,0:T(8,128)(2,1)S(1)}, u32[]{:S(2)}, u32[]{:S(2)}) collective-permute-start(bf16[512,512]{1,0:T(8,128)(2,1)S(1)} %collective-permute-done.14.near), channel_id=1, source_target_pairs={{4,8},{8,4},{5,9},{9,5},{6,10},{10,6},{7,11},{11,7},{20,24},{24,20... | collective-permute-start | bytes 1572872 | tf_op jit(solution)/shard_map/ppermute | solution.py:248
  67.4 21.8 %collective-permute-start.18 = (bf16[512,512]{1,0:T(8,128)(2,1)S(1)}, bf16[512,512]{1,0:T(8,128)(2,1)S(1)}, u32[]{:S(2)}, u32[]{:S(2)}) collective-permute-start(bf16[512,512]{1,0:T(8,128)(2,1)S(1)} %collective-permute-done.17.across), channel_id=1, source_target_pairs={{4,0},{8,12},{5,1},{9,13},{6,2},{10,14},{7,3},{11,15},{20,16},{24,... | collective-permute-start | bytes 1572872 | tf_op jit(solution)/shard_map/ppermute | solution.py:247
  68.9 32.8 %copy-start.4 = (s32[2,3,3]{2,0,1:T(2,128)S(1)}, s32[2,3,3]{2,0,1:T(2,128)}, u32[]{:S(2)}) copy-start(s32[2,3,3]{2,0,1:T(2,128)} %param.14) | copy-start | bytes 220
  68.9 32.8 %copy-start = (bf16[1,3,3,256,256]{4,3,2,1,0:T(8,128)(2,1)S(1)}, bf16[1,3,3,256,256]{4,3,2,1,0:T(8,128)(2,1)}, u32[]{:S(2)}) copy-start(bf16[1,3,3,256,256]{4,3,2,1,0:T(8,128)(2,1)} %coef.11) | copy-start | bytes 3538948
  71.7 41.7 %collective-permute-start.22 = (bf16[5,512,256]{2,1,0:T(8,128)(2,1)S(1)}, bf16[5,512,256]{2,1,0:T(8,128)(2,1)S(1)}, u32[]{:S(2)}, u32[]{:S(2)}) collective-permute-start(bf16[5,512,256]{2,1,0:T(8,128)(2,1)S(1)} %spread.3.field), channel_id=1, source_target_pairs={{0,1},{1,0},{2,3},{3,2},{4,5},{5,4},{6,7},{7,6},{8,9},{9,8},{10,11... | collective-permute-start | bytes 3932168 | tf_op jit(solution)/shard_map/ppermute | solution.py:294
  78.2 22.2 %collective-permute-start.21 = (bf16[512,512]{1,0:T(8,128)(2,1)S(1)}, bf16[512,512]{1,0:T(8,128)(2,1)S(1)}, u32[]{:S(2)}, u32[]{:S(2)}) collective-permute-start(bf16[512,512]{1,0:T(8,128)(2,1)S(1)} %collective-permute-done.16.beyond), channel_id=1, source_target_pairs={{4,0},{8,12},{5,1},{9,13},{6,2},{10,14},{7,3},{11,15},{20,16},{24,... | collective-permute-start | bytes 1572872 | tf_op jit(solution)/shard_map/ppermute | solution.py:251
  89.1 11.2 %collective-permute-start.23 = (bf16[512,512]{1,0:T(8,128)(2,1)S(1)}, bf16[512,512]{1,0:T(8,128)(2,1)S(1)}, u32[]{:S(2)}, u32[]{:S(2)}) collective-permute-start(bf16[512,512]{1,0:T(8,128)(2,1)S(1)} %collective-permute-done.19.near), channel_id=1, source_target_pairs={{4,8},{8,4},{5,9},{9,5},{6,10},{10,6},{7,11},{11,7},{20,24},{24,20... | collective-permute-start | bytes 1572872 | tf_op jit(solution)/shard_map/ppermute | solution.py:248
  89.8 28.5 %collective-permute-start.24 = (bf16[512,512]{1,0:T(8,128)(2,1)S(1)}, bf16[512,512]{1,0:T(8,128)(2,1)S(1)}, u32[]{:S(2)}, u32[]{:S(2)}) collective-permute-start(bf16[512,512]{1,0:T(8,128)(2,1)S(1)} %collective-permute-done.20.across), channel_id=1, source_target_pairs={{4,0},{8,12},{5,1},{9,13},{6,2},{10,14},{7,3},{11,15},{20,16},{24,... | collective-permute-start | bytes 1572872 | tf_op jit(solution)/shard_map/ppermute | solution.py:247
  100.4 22.5 %collective-permute-start.25 = (bf16[512,512]{1,0:T(8,128)(2,1)S(1)}, bf16[512,512]{1,0:T(8,128)(2,1)S(1)}, u32[]{:S(2)}, u32[]{:S(2)}) collective-permute-start(bf16[512,512]{1,0:T(8,128)(2,1)S(1)} %collective-permute-done.23.beyond), channel_id=1, source_target_pairs={{4,0},{8,12},{5,1},{9,13},{6,2},{10,14},{7,3},{11,15},{20,16},{24,... | collective-permute-start | bytes 1572872 | tf_op jit(solution)/shard_map/ppermute | solution.py:251
  107.0 22.3 %collective-permute-start.27 = (bf16[5,512,256]{2,1,0:T(8,128)(2,1)S(1)}, bf16[5,512,256]{2,1,0:T(8,128)(2,1)S(1)}, u32[]{:S(2)}, u32[]{:S(2)}) collective-permute-start(bf16[5,512,256]{2,1,0:T(8,128)(2,1)S(1)} %spread.4.field), channel_id=1, source_target_pairs={{0,1},{1,0},{2,3},{3,2},{4,5},{5,4},{6,7},{7,6},{8,9},{9,8},{10,11... | collective-permute-start | bytes 3932168 | tf_op jit(solution)/shard_map/ppermute | solution.py:294
  125.8 8.4 %collective-permute-start.26 = (bf16[5,512,256]{2,1,0:T(8,128)(2,1)S(1)}, bf16[5,512,256]{2,1,0:T(8,128)(2,1)S(1)}, u32[]{:S(2)}, u32[]{:S(2)}) collective-permute-start(bf16[5,512,256]{2,1,0:T(8,128)(2,1)S(1)} %spread.5.field), channel_id=1, source_target_pairs={{0,1},{1,0},{2,3},{3,2},{4,5},{5,4},{6,7},{7,6},{8,9},{9,8},{10,11... | collective-permute-start | bytes 3932168 | tf_op jit(solution)/shard_map/ppermute | solution.py:294

commit v4 on v3

--- a/solution.py
+++ b/solution.py
@@ -74,36 +74,49 @@
     out[...] = jnp.where(node < count[0], value, 0.0).astype(BF16)
 
 
-def spread_kernel(
-    tiles, place, send, coef_own, coef_lent, own, near, beyond, across, far, farthest, out, held, sems
-):
+def spread_kernel(tiles, last, place, send, coef_own, coef_lent, *rest):
+    blocks, entries, size, _ = coef_own.shape
     t, lev, sub, grp = (place[i] for i in range(4))
     inner = jnp.logical_and(t > 0, t < tiles - 1)
-    blocks, _, size = held.shape[1:]
+    out, held, sems = rest[-3:]
+    rows = held.shape[-2]
+    waits = []
 
     def fetch(source, d):
         for b in range(blocks):
             part = source.at[:, pl.ds(b * size, size)]
             pltpu.make_async_copy(part, held.at[d, b], sems.at[d, b]).start()
 
-    fetch(own, 0)
-    fetch(near, 1)
-    pl.when(inner)(functools.partial(fetch, beyond, 2))
-    pl.when(inner)(functools.partial(fetch, across, 3))
-    pl.when(jnp.logical_not(inner))(functools.partial(fetch, far, 2))
-    pl.when(jnp.logical_not(inner))(functools.partial(fetch, farthest, 3))
-    for d in range(tiles):
+    def expect(d):
         for b in range(blocks):
             pltpu.make_async_copy(held.at[d, b], held.at[d, b], sems.at[d, b]).wait()
-    for j in range(blocks + tiles - 1):
+
+    known = []
+    if last is not True:
+        own, near, beyond, far = rest[:4]
+        fetch(own, 0)
+        fetch(near, 1)
+        pl.when(inner)(functools.partial(fetch, beyond, 2))
+        pl.when(jnp.logical_not(inner))(functools.partial(fetch, far, 2))
+        known = [0, 1, 2]
+    if last is not False:
+        across, farthest = rest[-5:-3]
+        pl.when(inner)(functools.partial(fetch, across, 3))
+        pl.when(jnp.logical_not(inner))(functools.partial(fetch, farthest, 3))
+        known.append(3)
+    for d in known:
+        expect(d)
+    for j in range(entries):
         away = max(0, j - blocks + 1)
         source = t ^ away
         values, matrices = [], []
-        for e in range(blocks + tiles - 1):
+        for e in range(entries):
             hop = max(0, e - blocks + 1)
+            if away ^ hop not in known:
+                continue
             lender = source ^ hop
             block = e if e < blocks else send[lender, source, 0]
-            values.append(held[t ^ lender, block])
+            values.append(held[away ^ hop, block])
             if j < blocks:
                 matrices.append(coef_own[j, e])
             else:
@@ -113,54 +126,59 @@
                 ]
                 matrices.append(jnp.concatenate(pieces))
         total = dot_nt(jnp.concatenate(values, 1), jnp.concatenate(matrices, 1))
-        out[j] = total.astype(BF16)
-
-
-def interp_kernel(tiles, chunk, chunks, half, level, place, send, slots, coef, field, *rest):
-    out, made, done = rest[-3:]
-    own = field.shape[0] - tiles + 1
+        if last is True:
+            total += rest[0][j]
+        out[j] = total.astype(out.dtype)
+
+
+def interp_kernel(tiles, chunks, jobs, place, send, slots, coef, *rest):
+    out, made, sems = rest[-3:]
     t, sub = place[0], place[2]
-    side = sub if half == 0 else 1 - sub
-    count, taps, size = coef.shape[1:4]
-    levels, members = made.shape[:2]
-    first = pl.multiple_of((side * chunks + chunk) * members, members)
-    for p in range(count):
-        fields, matrices = [], []
-        for j in range(taps):
-            slot = slots[sub, p, j]
-            lender = jnp.maximum(slot - own, 0)
-            distance = t ^ lender
-            lent = jnp.where(distance == 0, send[lender, t, 0], own - 1 + distance)
-            fields.append(field[jnp.where(slot < own, slot, lent)])
-            matrices.append(coef[0, p, j])
-        value = dot_nt(jnp.concatenate(fields, 1), jnp.concatenate(matrices, 1))
-        made[:, :, p * size : (p + 1) * size] = value.astype(BF16).reshape(levels, members, size)
-    copy = pltpu.make_async_copy(
-        made, out.at[pl.ds(level, levels), pl.ds(first, members)], done
-    )
-    copy.start()
-    copy.wait()
-
-
-def interpolate(chunk, half, level, tiles, place, send, slots, coef, field, shape, before):
-    count, _, size = coef.shape[1:4]
-    chunks = shape[1] // 2 // CHUNK
-    levels = field.shape[1] // CHUNK
-    operands = [place, send, slots, coef, field]
-    in_specs = [SMEM, SMEM, SMEM, VMEM, VMEM]
+    levels, members = made.shape[1:3]
+    own = rest[0].shape[0] - tiles + 1
+    size = coef.shape[-1]
+    copies = []
+    for i, (chunk, half) in enumerate(jobs):
+        field = rest[i]
+        side = sub if half == 0 else 1 - sub
+        first = pl.multiple_of((side * chunks + chunk) * members, members)
+        for p in range(coef.shape[1]):
+            fields, matrices = [], []
+            for j in range(coef.shape[2]):
+                slot = slots[sub, p, j]
+                lender = jnp.maximum(slot - own, 0)
+                distance = t ^ lender
+                lent = jnp.where(distance == 0, send[lender, t, 0], own - 1 + distance)
+                fields.append(field[jnp.where(slot < own, slot, lent)])
+                matrices.append(coef[0, p, j])
+            value = dot_nt(jnp.concatenate(fields, 1), jnp.concatenate(matrices, 1))
+            value = value.astype(BF16).reshape(levels, members, size)
+            made[i, :, :, p * size : (p + 1) * size] = value
+        copies.append(
+            pltpu.make_async_copy(made.at[i], out.at[:, pl.ds(first, members)], sems.at[i])
+        )
+        copies[-1].start()
+    for copy in copies:
+        copy.wait()
+
+
+def interpolate(jobs, tiles, place, send, slots, coef, fields, shape, before):
+    levels, members, points = shape
+    operands = [place, send, slots, coef, *fields]
+    in_specs = [SMEM, SMEM, SMEM, VMEM] + [VMEM] * len(fields)
     aliases = {}
     if before is not None:
         aliases = {len(operands): 0}
         operands.append(before)
         in_specs.append(HBM)
     return pl.pallas_call(
-        functools.partial(interp_kernel, tiles, chunk, chunks, half, level),
+        functools.partial(interp_kernel, tiles, members // 2 // CHUNK, jobs),
         in_specs=in_specs,
         out_specs=HBM,
         out_shape=jax.ShapeDtypeStruct(shape, BF16),
         scratch_shapes=[
-            pltpu.VMEM((levels, CHUNK, count * size), BF16),
-            pltpu.SemaphoreType.DMA,
+            pltpu.VMEM((len(jobs), levels, CHUNK, points), BF16),
+            pltpu.SemaphoreType.DMA((len(jobs),)),
         ],
         input_output_aliases=aliases,
         compiler_params=params(),
@@ -272,32 +290,47 @@
     gathered = jnp.stack(shares)
     gathered = jnp.stack([gathered, lax.ppermute(gathered, "sub", swap)])
 
-    def spread(place, c):
+    def spread(place, c, last, *sources):
+        count = len(sources) - (last is True)
         return pl.pallas_call(
-            functools.partial(spread_kernel, tiles),
-            in_specs=[SMEM, SMEM, VMEM, VMEM] + [HBM] * 6,
+            functools.partial(spread_kernel, tiles, last),
+            in_specs=[SMEM, SMEM, VMEM, VMEM]
+            + [VMEM] * (len(sources) - count)
+            + [HBM] * count,
             out_specs=VMEM,
-            out_shape=jax.ShapeDtypeStruct((entries, rows, size), BF16),
+            out_shape=jax.ShapeDtypeStruct((entries, rows, size), F32 if last is False else BF16),
             scratch_shapes=[
                 pltpu.VMEM((tiles, blocks, rows, size), BF16),
                 pltpu.SemaphoreType.DMA((tiles, blocks)),
             ],
             compiler_params=params(),
             name="spread",
-        )(place, send_list, merged, gathered, vertical[c], near[c], beyond[c], across[c], far[c], farthest[c])
+        )(place, send_list, merged, gathered, *sources)
 
     shape = (levels, halves * members, points)
+
+    def flush(jobs, result):
+        which, fields = zip(*jobs)
+        return interpolate(
+            which, tiles, place, send_list, interp_slots, interp_coef, fields, shape, result
+        )
+
     result = None
     ready = []
+    jobs = []
     for c in range(chunks):
-        fields = spread(after(place, *ready), c)
-        other = lax.ppermute(fields, "sub", swap)
-        for half, field in enumerate((fields, other)):
-            result = interpolate(
-                c, half, 0, tiles, place, send_list, interp_slots, interp_coef, field, shape, result
-            )
-            if half == 0:
-                ready = [result]
+        held = after(place, *ready)
+        early = (vertical[c], near[c], beyond[c], far[c])
+        late = (across[c], farthest[c])
+        if c + 1 < chunks:
+            fields = spread(held, c, None, *early, *late)
+        else:
+            fields = spread(held, c, True, spread(held, c, False, *early), *late)
+        jobs.append(((c, 0), fields))
+        result = flush(jobs, result)
+        ready = [result]
+        jobs = [((c, 1), lax.ppermute(fields, "sub", swap))]
+    result = flush(jobs, result)
     return result.transpose(2, 0, 1)
 
 

time: 137 us -> 134 us (0.978)
  starting transfers between devices: 51 us -> 54.2 us
  waiting for transfers between devices: 50.6 us -> 47.6 us
  Pallas kernels: 30.1 us -> 27.3 us
    ppermute x3, waiting for transfers between devices: 21.9 us -> 13.8 us  [slot(): farthest[c] = lax.ppermute(after(beyond[c], *others), 'tile', edge_out)]
    ppermute x3, starting transfers between devices: 16.4 us -> 24.5 us  [local(): jobs = [((c, 1), lax.ppermute(fields, 'sub', swap))]]
    ppermute x3, starting transfers between devices: 8.98 us -> 4.97 us  [slot(): near[c] = lax.ppermute(value, 'tile', edge_both)]
    ppermute x1, waiting for transfers between devices: 2.85 us -> 0.01 us  [local(): lax.ppermute(share, ('grp', 'lev'), corner)]
    pallas_call x9 -> x8, Pallas kernels: 23.2 us -> 20.4 us  [the longest x4 11 us: interpolate(): pl.pallas_call(functools.partial(interp_kernel, tiles, members // 2 // CH...]
    ppermute x3, waiting for transfers between devices: 3.57 us -> 6.13 us  [local(): lax.ppermute(pieces[d - 1], 'tile', [(i, i ^ d) for i in range(tiles)])]
    ppermute x1, waiting for transfers between devices: 0.01 us -> 2.11 us  [local(): lax.ppermute(share, 'grp', swap)]
    ppermute x3, waiting for transfers between devices: 11.2 us -> 12.8 us  [slot(): far[c] = lax.ppermute(after(across[c], *others), 'tile', edge_out)]
  transfers between devices with their start and end apart: 28 -> 28, of which waited for: 12 -> 11; matrix products, arithmetic and copies ran while one was open for 2% -> 2% of each run, Pallas kernels for 20% -> 19%
where the time goes in v4:
time: 134 us
  starting transfers between devices  54.2 us (40%)
  waiting for transfers between devices  47.6 us (36%)
  Pallas kernels  27.3 us (20%)
  local copies, waits for them, and re-layouts  3.54 us (3%)
    ppermute x3, starting transfers between devices, local(): jobs = [((c, 1), lax.ppermute(fields, 'sub', swap))]  24.5 us
    ppermute x3, waiting for transfers between devices, slot(): farthest[c] = lax.ppermute(after(beyond[c], *others), 'tile', edge_out)  13.8 us
    ppermute x3, waiting for transfers between devices, slot(): far[c] = lax.ppermute(after(across[c], *others), 'tile', edge_out)  12.8 us
    pallas_call x4, Pallas kernels, interpolate(): pl.pallas_call(functools.partial(interp_kernel, tiles, members // 2 // CH...  11 us
    pallas_call x4, Pallas kernels, spread(): pl.pallas_call(functools.partial(spread_kernel, tiles, last), in_specs=[S...  9.42 us
    ppermute x3, waiting for transfers between devices, local(): theirs = [lax.ppermute(x, 'lev', swap) for x in mine]  7.91 us
    ppermute x3, waiting for transfers between devices, local(): lax.ppermute(pieces[d - 1], 'tile', [(i, i ^ d) for i in range(tiles)])  6.13 us
    ppermute x3, starting transfers between devices, slot(): near[c] = lax.ppermute(value, 'tile', edge_both)  4.97 us
  transfers between devices with their start and end apart: 28, of which 11 were waited for; matrix products, arithmetic and copies ran while one was open for 2% of the time, Pallas kernels for 19%

profile of v4, /device:TPU:1, one launch (start us, length us, event | category | flops | bytes accessed | tf_op | source)
XLA Modules:
  0.0 134.0 jit_solution(9431911965968273552)
XLA Ops:
  0.0 1.2 slice.24
  1.2 2.1 %collective-permute-start.3 = (bf16[512,512]{1,0:T(8,128)(2,1)S(1)}, bf16[512,512]{1,0:T(8,128)(2,1)}, u32[]{:S(2)}, u32[]{:S(2)}) collective-permute-start(bf16[512,512]{1,0:T(8,128)(2,1)S(1)} %bitcast.28), channel_id=1, source_target_pairs={{0,2},{2,0},{1,3},{3,1},{4,6},{6,4},{5,7},{7,5},{8,10},{10,8},{9,1... | collective-permute-start | bytes 1572872 | tf_op jit(solution)/shard_map/ppermute | solution.py:210
  3.4 2.1 %fusion.1 = (bf16[32,16,512]{2,1,0:T(8,128)(2,1)S(1)}, bf16[32,16,512]{2,1,0:T(8,128)(2,1)}) fusion(bf16[32,48,512]{2,1,0:T(8,128)(2,1)} %bitcast.33), kind=kLoop, calls=%fused_computation.7 | loop fusion | bytes 2097152 | tf_op jit(solution)/shard_map/slice | solution.py:209
  5.6 1.4 %merge_taps.1 = (bf16[2,5,256,256]{3,2,1,0:T(8,128)(2,1)S(1)}, bf16[3,5,32,256]{3,2,1,0:T(8,128)(2,1)S(1)}) custom-call(s32[5]{0:T(128)S(1)} %stack.59.place, s32[4,4,1]{2,1,0:T(4,128)S(1)} %copy.23.send, s32[1,2,9]{2,1,0:T(2,128)S(1)} %copy-done.3, bf16[2,9,256,256]{3,2,1,0:T(8,128)(2,1)S(1)} %bitcast.27), custom_call_target="tpu_custom_call" | custom-call | tf_op jit(solution)/shard_map/merge_taps/pallas_call | solution.py:212
  7.1 1.6 %collective-permute-start = (bf16[5,32,256]{2,1,0:T(8,128)(2,1)S(1)}, bf16[5,32,256]{2,1,0:T(8,128)(2,1)S(1)}, u32[]{:S(2)}, u32[]{:S(2)}) collective-permute-start(bf16[5,32,256]{2,1,0:T(8,128)(2,1)S(1)} %get-tuple-element.49), channel_id=1, source_target_pairs={{0,4},{4,0},{8,12},{12,8},{1,5},{5,1},{9,13},{13,9},{2,6},{6,2},{1... | collective-permute-start | bytes 245768 | tf_op jit(solution)/shard_map/ppermute | solution.py:226
  8.7 2.2 %collective-permute-start.2 = (bf16[5,32,256]{2,1,0:T(8,128)(2,1)S(1)}, bf16[5,32,256]{2,1,0:T(8,128)(2,1)S(1)}, u32[]{:S(2)}, u32[]{:S(2)}) collective-permute-start(bf16[5,32,256]{2,1,0:T(8,128)(2,1)S(1)} %get-tuple-element.50), channel_id=1, source_target_pairs={{0,12},{4,8},{8,4},{12,0},{1,13},{5,9},{9,5},{13,1},{2,14},{6,10},... | collective-permute-start | bytes 245768 | tf_op jit(solution)/shard_map/ppermute | solution.py:226
  11.7 1.1 level_weights.1.weight
  12.8 1.3 collective-permute-done.2
  14.1 4.8 %collective-permute-done.1 = bf16[5,32,256]{2,1,0:T(8,128)(2,1)S(1)} collective-permute-done((bf16[5,32,256]{2,1,0:T(8,128)(2,1)S(1)}, bf16[5,32,256]{2,1,0:T(8,128)(2,1)S(1)}, u32[]{:S(2)}, u32[]{:S(2)}) %collective-permute-start.1) | collective-permute-done | bytes 81952 | tf_op jit(solution)/shard_map/ppermute | solution.py:226
  18.9 1.7 %vertical.3.rest_0_ = bf16[512,512]{1,0:T(8,128)(2,1)S(1)} custom-call(s32[1]{0:T(128)S(6)} %copy.28.count, bf16[2,512,512]{2,1,0:T(8,128)(2,1)S(1)} %level_weights.1.weight, bf16[512,512]{1,0:T(8,128)(2,1)S(1)} %bitcast.29, bf16[512,512]{1,0:T(8,128)(2,1)} %collective-permute-done.3.other), custom_call_target="tpu_custom_call" | custom-call | tf_op jit(solution)/shard_map/vertical/pallas_call | solution.py:241
  20.7 0.7 collective-permute-start.11
  21.4 0.8 collective-permute-start.8
  22.2 2.2 %collective-permute-start.6 = (bf16[3,5,32,256]{3,2,1,0:T(8,128)(2,1)S(1)}, bf16[3,5,32,256]{3,2,1,0:T(8,128)(2,1)S(1)}, u32[]{:S(2)}, u32[]{:S(2)}) collective-permute-start(bf16[3,5,32,256]{3,2,1,0:T(8,128)(2,1)S(1)} %pad_maximum_fusion.2), channel_id=1, source_target_pairs={{0,18},{2,16},{16,2},{18,0},{1,19},{3,17},{17,3},{19,1},{4,22},{6,... | collective-permute-start | bytes 737288 | tf_op jit(solution)/shard_map/ppermute | solution.py:288
  24.6 1.7 %collective-permute-done.9.other = bf16[512,512]{1,0:T(8,128)(2,1)} collective-permute-done((bf16[512,512]{1,0:T(8,128)(2,1)}, bf16[512,512]{1,0:T(8,128)(2,1)}, u32[]{:S(2)}, u32[]{:S(2)}) %collective-permute-start.9) | collective-permute-done | bytes 524320 | tf_op jit(solution)/shard_map/ppermute | solution.py:210
  26.3 1.1 collective-permute-start.4
  27.5 1.9 %vertical.4.rest_0_ = bf16[512,512]{1,0:T(8,128)(2,1)S(1)} custom-call(s32[1]{0:T(128)S(6)} %copy.28.count, bf16[2,512,512]{2,1,0:T(8,128)(2,1)S(1)} %level_weights.1.weight, bf16[512,512]{1,0:T(8,128)(2,1)} %bitcast.7.own, bf16[512,512]{1,0:T(8,128)(2,1)} %collective-permute-done.9.other), custom_call_target="tpu_custom_call" | custom-call | tf_op jit(solution)/shard_map/vertical/pallas_call | solution.py:241
  29.4 1.3 collective-permute-start.12
  30.7 2.7 %collective-permute-done.8.rest_1_ = bf16[512,512]{1,0:T(8,128)(2,1)S(1)} collective-permute-done((bf16[512,512]{1,0:T(8,128)(2,1)S(1)}, bf16[512,512]{1,0:T(8,128)(2,1)S(1)}, u32[]{:S(2)}, u32[]{:S(2)}) %collective-permute-start.8) | collective-permute-done | bytes 524320 | tf_op jit(solution)/shard_map/ppermute | solution.py:261
  34.2 2.1 %collective-permute-done.5 = bf16[3,5,32,256]{3,2,1,0:T(8,128)(2,1)S(1)} collective-permute-done((bf16[3,5,32,256]{3,2,1,0:T(8,128)(2,1)S(1)}, bf16[3,5,32,256]{3,2,1,0:T(8,128)(2,1)S(1)}, u32[]{:S(2)}, u32[]{:S(2)}) %collective-permute-start.5) | collective-permute-done | bytes 245792 | tf_op jit(solution)/shard_map/ppermute | solution.py:287
  36.4 1.8 %collective-permute-start.7 = (bf16[4,3,5,32,256]{4,3,2,1,0:T(8,128)(2,1)S(1)}, bf16[4,3,5,32,256]{4,3,2,1,0:T(8,128)(2,1)S(1)}, u32[]{:S(2)}, u32[]{:S(2)}) collective-permute-start(bf16[4,3,5,32,256]{4,3,2,1,0:T(8,128)(2,1)S(1)} %get-tuple-element.48), channel_id=1, source_target_pairs={{0,1},{1,0},{2,3},{3,2},{4,5},{5,4},{6,7},{7,6},{8,9},{9,8},{10,11... | collective-permute-start | bytes 2949128 | tf_op jit(solution)/shard_map/ppermute | solution.py:291
  38.3 1.5 %collective-permute-start.16 = (bf16[512,512]{1,0:T(8,128)(2,1)S(1)}, bf16[512,512]{1,0:T(8,128)(2,1)S(1)}, u32[]{:S(2)}, u32[]{:S(2)}) collective-permute-start(bf16[512,512]{1,0:T(8,128)(2,1)S(1)} %bitcast.30), channel_id=1, source_target_pairs={{0,2},{2,0},{1,3},{3,1},{4,6},{6,4},{5,7},{7,5},{8,10},{10,8},{9,1... | collective-permute-start | bytes 1572872 | tf_op jit(solution)/shard_map/ppermute | solution.py:210
  40.4 3.8 %collective-permute-done.12.rest_3_ = bf16[512,512]{1,0:T(8,128)(2,1)S(1)} collective-permute-done((bf16[512,512]{1,0:T(8,128)(2,1)S(1)}, bf16[512,512]{1,0:T(8,128)(2,1)S(1)}, u32[]{:S(2)}, u32[]{:S(2)}) %collective-permute-start.12) | collective-permute-done | bytes 524320 | tf_op jit(solution)/shard_map/ppermute | solution.py:265
  44.3 1.3 collective-permute-start.13
  45.6 6.2 %collective-permute-done.16.other = bf16[512,512]{1,0:T(8,128)(2,1)S(1)} collective-permute-done((bf16[512,512]{1,0:T(8,128)(2,1)S(1)}, bf16[512,512]{1,0:T(8,128)(2,1)S(1)}, u32[]{:S(2)}, u32[]{:S(2)}) %collective-permute-start.16) | collective-permute-done | bytes 524320 | tf_op jit(solution)/shard_map/ppermute | solution.py:210
  51.8 0.7 vertical.5.rest_0_
  52.5 2.1 %collective-permute-done.15.rest_1_ = bf16[512,512]{1,0:T(8,128)(2,1)S(1)} collective-permute-done((bf16[512,512]{1,0:T(8,128)(2,1)S(1)}, bf16[512,512]{1,0:T(8,128)(2,1)S(1)}, u32[]{:S(2)}, u32[]{:S(2)}) %collective-permute-start.15) | collective-permute-done | bytes 524320 | tf_op jit(solution)/shard_map/ppermute | solution.py:261
  54.6 4.1 %collective-permute-start.20 = (bf16[512,512]{1,0:T(8,128)(2,1)S(1)}, bf16[512,512]{1,0:T(8,128)(2,1)S(1)}, u32[]{:S(2)}, u32[]{:S(2)}) collective-permute-start(bf16[512,512]{1,0:T(8,128)(2,1)S(1)} %vertical.5.rest_0_), channel_id=1, source_target_pairs={{0,4},{4,0},{8,12},{12,8},{1,5},{5,1},{9,13},{13,9},{2,6},{6,2},{1... | collective-permute-start | bytes 1572872 | tf_op jit(solution)/shard_map/ppermute | solution.py:261
  58.6 7.2 %collective-permute-done.13.rest_5_ = bf16[512,512]{1,0:T(8,128)(2,1)S(1)} collective-permute-done((bf16[512,512]{1,0:T(8,128)(2,1)S(1)}, bf16[512,512]{1,0:T(8,128)(2,1)S(1)}, u32[]{:S(2)}, u32[]{:S(2)}) %collective-permute-start.13) | collective-permute-done | bytes 524320 | tf_op jit(solution)/shard_map/ppermute | solution.py:269
  65.8 1.3 collective-permute-start.19
  67.1 0.7 collective-permute-start.17
  67.8 0.7 collective-permute-start.21
  68.7 2.8 %spread.4.rest_0_ = bf16[5,512,256]{2,1,0:T(8,128)(2,1)S(1)} custom-call(s32[5]{0:T(128)S(1)} %stack.59.place, s32[4,4,1]{2,1,0:T(4,128)S(1)} %copy.23.send, bf16[2,5,256,256]{3,2,1,0:T(8,128)(2,1)S(1)} %get-tuple-element.27.coef_own, bf16[2,4,3,5,32,256]{5,4,3,2,1,0:T(8,128)(2,1)S(1)} %pad_maximum_fusion.coef_lent, bf16[512,512]{1,0:T(8,128)(2,1)S(1)} %vertical.3.rest_0_, ...), custom_call_target="tpu_custom_call" | custom-call | tf_op jit(solution)/shard_map/spread/pallas_call | solution.py:295
  71.5 7.7 %collective-permute-start.14 = (bf16[5,512,256]{2,1,0:T(8,128)(2,1)S(1)}, bf16[5,512,256]{2,1,0:T(8,128)(2,1)S(1)}, u32[]{:S(2)}, u32[]{:S(2)}) collective-permute-start(bf16[5,512,256]{2,1,0:T(8,128)(2,1)S(1)} %spread.4.rest_0_), channel_id=1, source_target_pairs={{0,1},{1,0},{2,3},{3,2},{4,5},{5,4},{6,7},{7,6},{8,9},{9,8},{10,11... | collective-permute-start | bytes 3932168 | tf_op jit(solution)/shard_map/ppermute | solution.py:332
  79.3 9.0 %collective-permute-done.19.rest_3_ = bf16[512,512]{1,0:T(8,128)(2,1)S(1)} collective-permute-done((bf16[512,512]{1,0:T(8,128)(2,1)S(1)}, bf16[512,512]{1,0:T(8,128)(2,1)S(1)}, u32[]{:S(2)}, u32[]{:S(2)}) %collective-permute-start.19) | collective-permute-done | bytes 524320 | tf_op jit(solution)/shard_map/ppermute | solution.py:265
  88.3 1.3 collective-permute-start.22
  89.6 0.7 collective-permute-start.23
  90.3 1.3 collective-permute-start.24
  91.6 6.6 %collective-permute-done.22.rest_5_ = bf16[512,512]{1,0:T(8,128)(2,1)S(1)} collective-permute-done((bf16[512,512]{1,0:T(8,128)(2,1)S(1)}, bf16[512,512]{1,0:T(8,128)(2,1)S(1)}, u32[]{:S(2)}, u32[]{:S(2)}) %collective-permute-start.22) | collective-permute-done | bytes 524320 | tf_op jit(solution)/shard_map/ppermute | solution.py:269
  98.2 1.3 collective-permute-start.25
  99.5 2.4 %interpolate.4.rest_2_ = bf16[32,96,768]{2,1,0:T(8,128)(2,1)} custom-call(s32[5]{0:T(128)S(1)} %stack.59.place, s32[4,4,1]{2,1,0:T(4,128)S(1)} %copy.23.send, s32[2,3,3]{2,1,0:T(4,128)S(1)} %copy.24.slots, bf16[1,3,3,256,256]{4,3,2,1,0:T(8,128)(2,1)S(1)} %copy-done, bf16[5,512,256]{2,1,0:T(8,128)(2,1)S(1)} %spread.4.rest_0_), custom_call_target="tpu_custom_call" | custom-call | tf_op jit(solution)/shard_map/interpolate/pallas_call | solution.py:174
  102.0 2.8 %spread.5.rest_1_ = bf16[5,512,256]{2,1,0:T(8,128)(2,1)S(1)} custom-call(s32[5]{0:T(128)S(1)} %stack.59.place, s32[4,4,1]{2,1,0:T(4,128)S(1)} %copy.23.send, bf16[2,5,256,256]{3,2,1,0:T(8,128)(2,1)S(1)} %get-tuple-element.27.coef_own, bf16[2,4,3,5,32,256]{5,4,3,2,1,0:T(8,128)(2,1)S(1)} %pad_maximum_fusion.coef_lent, bf16[512,512]{1,0:T(8,128)(2,1)S(1)} %vertical.4.rest_0_, ...), custom_call_target="tpu_custom_call" | custom-call | tf_op jit(solution)/shard_map/spread/pallas_call | solution.py:295
  104.8 12.9 %collective-permute-start.27 = (bf16[5,512,256]{2,1,0:T(8,128)(2,1)S(1)}, bf16[5,512,256]{2,1,0:T(8,128)(2,1)S(1)}, u32[]{:S(2)}, u32[]{:S(2)}) collective-permute-start(bf16[5,512,256]{2,1,0:T(8,128)(2,1)S(1)} %spread.5.rest_1_), channel_id=1, source_target_pairs={{0,1},{1,0},{2,3},{3,2},{4,5},{5,4},{6,7},{7,6},{8,9},{9,8},{10,11... | collective-permute-start | bytes 3932168 | tf_op jit(solution)/shard_map/ppermute | solution.py:332
  117.7 3.1 %interpolate.5.rest_2_ = bf16[32,96,768]{2,1,0:T(8,128)(2,1)} custom-call(s32[5]{0:T(128)S(1)} %stack.59.place, s32[4,4,1]{2,1,0:T(4,128)S(1)} %copy.23.send, s32[2,3,3]{2,1,0:T(4,128)S(1)} %copy.24.slots, bf16[1,3,3,256,256]{4,3,2,1,0:T(8,128)(2,1)S(1)} %copy-done, ...), custom_call_target="tpu_custom_call", output_to_operand_aliasing={{}: (6, {})} | custom-call | tf_op jit(solution)/shard_map/interpolate/pallas_call | solution.py:174
  120.8 2.4 %spread.6.rest_0_ = f32[5,512,256]{2,1,0:T(8,128)S(1)} custom-call(s32[5]{0:T(128)S(1)} %stack.59.place, s32[4,4,1]{2,1,0:T(4,128)S(1)} %copy.23.send, bf16[2,5,256,256]{3,2,1,0:T(8,128)(2,1)S(1)} %get-tuple-element.27.coef_own, bf16[2,4,3,5,32,256]{5,4,3,2,1,0:T(8,128)(2,1)S(1)} %pad_maximum_fusion.coef_lent, bf16[512,512]{1,0:T(8,128)(2,1)S(1)} %vertical.5.rest_0_, ...), custom_call_target="tpu_custom_call" | custom-call | tf_op jit(solution)/shard_map/spread/pallas_call | solution.py:295
  123.2 1.4 %spread.7.rest_1_ = bf16[5,512,256]{2,1,0:T(8,128)(2,1)S(1)} custom-call(s32[5]{0:T(128)S(1)} %stack.59.place, s32[4,4,1]{2,1,0:T(4,128)S(1)} %copy.23.send, bf16[2,5,256,256]{3,2,1,0:T(8,128)(2,1)S(1)} %get-tuple-element.27.coef_own, bf16[2,4,3,5,32,256]{5,4,3,2,1,0:T(8,128)(2,1)S(1)} %pad_maximum_fusion.coef_lent, f32[5,512,256]{2,1,0:T(8,128)S(1)} %spread.6.rest_0_, ...), custom_call_target="tpu_custom_call" | custom-call | tf_op jit(solution)/shard_map/spread/pallas_call | solution.py:295
  124.6 3.9 %collective-permute-start.26 = (bf16[5,512,256]{2,1,0:T(8,128)(2,1)S(1)}, bf16[5,512,256]{2,1,0:T(8,128)(2,1)S(1)}, u32[]{:S(2)}, u32[]{:S(2)}) collective-permute-start(bf16[5,512,256]{2,1,0:T(8,128)(2,1)S(1)} %spread.7.rest_1_), channel_id=1, source_target_pairs={{0,1},{1,0},{2,3},{3,2},{4,5},{5,4},{6,7},{7,6},{8,9},{9,8},{10,11... | collective-permute-start | bytes 3932168 | tf_op jit(solution)/shard_map/ppermute | solution.py:332
  128.5 3.1 %interpolate.6.rest_1_ = bf16[32,96,768]{2,1,0:T(8,128)(2,1)} custom-call(s32[5]{0:T(128)S(1)} %stack.59.place, s32[4,4,1]{2,1,0:T(4,128)S(1)} %copy.23.send, s32[2,3,3]{2,1,0:T(4,128)S(1)} %copy.24.slots, bf16[1,3,3,256,256]{4,3,2,1,0:T(8,128)(2,1)S(1)} %copy-done, ...), custom_call_target="tpu_custom_call", output_to_operand_aliasing={{}: (6, {})} | custom-call | tf_op jit(solution)/shard_map/interpolate/pallas_call | solution.py:174
  131.6 2.4 %interpolate.7 = bf16[32,96,768]{2,1,0:T(8,128)(2,1)} custom-call(s32[5]{0:T(128)S(1)} %stack.59.place, s32[4,4,1]{2,1,0:T(4,128)S(1)} %copy.23.send, s32[2,3,3]{2,1,0:T(4,128)S(1)} %copy.24.slots, bf16[1,3,3,256,256]{4,3,2,1,0:T(8,128)(2,1)S(1)} %copy-done, ...), custom_call_target="tpu_custom_call", output_to_operand_aliasing={{}: (5, {})} | custom-call | tf_op jit(solution)/shard_map/interpolate/pallas_call | solution.py:174
  (42 shorter events, 2.5 us)
Async XLA Ops:
  0.0 5.4 %copy-start.5 = (s32[4,4,1]{1,2,0:T(1,128)S(1)}, s32[4,4,1]{1,2,0:T(1,128)}, u32[]{:S(2)}) copy-start(s32[4,4,1]{1,2,0:T(1,128)} %param.11) | copy-start | bytes 196
  0.0 5.6 %copy-start.1 = (bf16[1,2,9,256,256]{4,3,2,1,0:T(8,128)(2,1)S(1)}, bf16[1,2,9,256,256]{4,3,2,1,0:T(8,128)(2,1)}, u32[]{:S(2)}) copy-start(bf16[1,2,9,256,256]{4,3,2,1,0:T(8,128)(2,1)} %param.13) | copy-start | bytes 7077892
  0.0 5.6 %copy-start.3 = (s32[1,2,9]{2,1,0:T(2,128)S(1)}, s32[1,2,9]{2,1,0:T(2,128)}, u32[]{:S(2)}) copy-start(s32[1,2,9]{2,1,0:T(2,128)} %slots.5) | copy-start | bytes 220
  1.2 17.7 %collective-permute-start.3 = (bf16[512,512]{1,0:T(8,128)(2,1)S(1)}, bf16[512,512]{1,0:T(8,128)(2,1)}, u32[]{:S(2)}, u32[]{:S(2)}) collective-permute-start(bf16[512,512]{1,0:T(8,128)(2,1)S(1)} %bitcast.28), channel_id=1, source_target_pairs={{0,2},{2,0},{1,3},{3,1},{4,6},{6,4},{5,7},{7,5},{8,10},{10,8},{9,1... | collective-permute-start | bytes 1572872 | tf_op jit(solution)/shard_map/ppermute | solution.py:210
  5.4 6.2 %copy-start.2 = (bf16[64,64]{1,0:T(8,128)(2,1)S(1)}, bf16[64,64]{1,0:T(8,128)(2,1)}, u32[]{:S(2)}) copy-start(bf16[64,64]{1,0:T(8,128)(2,1)} %vert.1) | copy-start | bytes 24580
  5.4 20.9 %collective-permute-start.9 = (bf16[512,512]{1,0:T(8,128)(2,1)}, bf16[512,512]{1,0:T(8,128)(2,1)}, u32[]{:S(2)}, u32[]{:S(2)}) collective-permute-start(bf16[512,512]{1,0:T(8,128)(2,1)} %bitcast.7.own), channel_id=1, source_target_pairs={{0,2},{2,0},{1,3},{3,1},{4,6},{6,4},{5,7},{7,5},{8,10},{10,8},{9,1... | collective-permute-start | bytes 1572872 | tf_op jit(solution)/shard_map/ppermute | solution.py:210
  7.1 5.6 %collective-permute-start = (bf16[5,32,256]{2,1,0:T(8,128)(2,1)S(1)}, bf16[5,32,256]{2,1,0:T(8,128)(2,1)S(1)}, u32[]{:S(2)}, u32[]{:S(2)}) collective-permute-start(bf16[5,32,256]{2,1,0:T(8,128)(2,1)S(1)} %get-tuple-element.49), channel_id=1, source_target_pairs={{0,4},{4,0},{8,12},{12,8},{1,5},{5,1},{9,13},{13,9},{2,6},{6,2},{1... | collective-permute-start | bytes 245768 | tf_op jit(solution)/shard_map/ppermute | solution.py:226
  8.7 5.4 %collective-permute-start.2 = (bf16[5,32,256]{2,1,0:T(8,128)(2,1)S(1)}, bf16[5,32,256]{2,1,0:T(8,128)(2,1)S(1)}, u32[]{:S(2)}, u32[]{:S(2)}) collective-permute-start(bf16[5,32,256]{2,1,0:T(8,128)(2,1)S(1)} %get-tuple-element.50), channel_id=1, source_target_pairs={{0,12},{4,8},{8,4},{12,0},{1,13},{5,9},{9,5},{13,1},{2,14},{6,10},... | collective-permute-start | bytes 245768 | tf_op jit(solution)/shard_map/ppermute | solution.py:226
  10.9 8.0 %collective-permute-start.1 = (bf16[5,32,256]{2,1,0:T(8,128)(2,1)S(1)}, bf16[5,32,256]{2,1,0:T(8,128)(2,1)S(1)}, u32[]{:S(2)}, u32[]{:S(2)}) collective-permute-start(bf16[5,32,256]{2,1,0:T(8,128)(2,1)S(1)} %get-tuple-element.51), channel_id=1, source_target_pairs={{0,8},{4,12},{8,0},{12,4},{1,9},{5,13},{9,1},{13,5},{2,10},{6,14},... | collective-permute-start | bytes 245768 | tf_op jit(solution)/shard_map/ppermute | solution.py:226
  20.7 8.7 %collective-permute-start.11 = (bf16[512,512]{1,0:T(8,128)(2,1)S(1)}, bf16[512,512]{1,0:T(8,128)(2,1)S(1)}, u32[]{:S(2)}, u32[]{:S(2)}) collective-permute-start(bf16[512,512]{1,0:T(8,128)(2,1)S(1)} %vertical.3.rest_0_), channel_id=1, source_target_pairs={{4,8},{8,4},{5,9},{9,5},{6,10},{10,6},{7,11},{11,7},{20,24},{24,20... | collective-permute-start | bytes 1572872 | tf_op jit(solution)/shard_map/ppermute | solution.py:262
  21.4 12.1 %collective-permute-start.8 = (bf16[512,512]{1,0:T(8,128)(2,1)S(1)}, bf16[512,512]{1,0:T(8,128)(2,1)S(1)}, u32[]{:S(2)}, u32[]{:S(2)}) collective-permute-start(bf16[512,512]{1,0:T(8,128)(2,1)S(1)} %vertical.3.rest_0_), channel_id=1, source_target_pairs={{0,4},{4,0},{8,12},{12,8},{1,5},{5,1},{9,13},{13,9},{2,6},{6,2},{1... | collective-permute-start | bytes 1572872 | tf_op jit(solution)/shard_map/ppermute | solution.py:261
  22.2 11.9 %collective-permute-start.6 = (bf16[3,5,32,256]{3,2,1,0:T(8,128)(2,1)S(1)}, bf16[3,5,32,256]{3,2,1,0:T(8,128)(2,1)S(1)}, u32[]{:S(2)}, u32[]{:S(2)}) collective-permute-start(bf16[3,5,32,256]{3,2,1,0:T(8,128)(2,1)S(1)} %pad_maximum_fusion.2), channel_id=1, source_target_pairs={{0,18},{2,16},{16,2},{18,0},{1,19},{3,17},{17,3},{19,1},{4,22},{6,... | collective-permute-start | bytes 737288 | tf_op jit(solution)/shard_map/ppermute | solution.py:288
  24.4 11.9 %collective-permute-start.5 = (bf16[3,5,32,256]{3,2,1,0:T(8,128)(2,1)S(1)}, bf16[3,5,32,256]{3,2,1,0:T(8,128)(2,1)S(1)}, u32[]{:S(2)}, u32[]{:S(2)}) collective-permute-start(bf16[3,5,32,256]{3,2,1,0:T(8,128)(2,1)S(1)} %pad_maximum_fusion.2), channel_id=1, source_target_pairs={{0,16},{16,0},{1,17},{17,1},{2,18},{18,2},{3,19},{19,3},{4,20},{20... | collective-permute-start | bytes 737288 | tf_op jit(solution)/shard_map/ppermute | solution.py:287
  26.3 9.9 %collective-permute-start.4 = (bf16[3,5,32,256]{3,2,1,0:T(8,128)(2,1)S(1)}, bf16[3,5,32,256]{3,2,1,0:T(8,128)(2,1)S(1)}, u32[]{:S(2)}, u32[]{:S(2)}) collective-permute-start(bf16[3,5,32,256]{3,2,1,0:T(8,128)(2,1)S(1)} %pad_maximum_fusion.2), channel_id=1, source_target_pairs={{0,2},{2,0},{1,3},{3,1},{4,6},{6,4},{5,7},{7,5},{8,10},{10,8},{9,1... | collective-permute-start | bytes 737288 | tf_op jit(solution)/shard_map/ppermute | solution.py:286
  29.4 14.8 %collective-permute-start.12 = (bf16[512,512]{1,0:T(8,128)(2,1)S(1)}, bf16[512,512]{1,0:T(8,128)(2,1)S(1)}, u32[]{:S(2)}, u32[]{:S(2)}) collective-permute-start(bf16[512,512]{1,0:T(8,128)(2,1)S(1)} %collective-permute-done.11.rest_4_), channel_id=1, source_target_pairs={{4,0},{8,12},{5,1},{9,13},{6,2},{10,14},{7,3},{11,15},{20,16},{24,... | collective-permute-start | bytes 1572872 | tf_op jit(solution)/shard_map/ppermute | solution.py:265
  33.5 10.9 %collective-permute-start.10 = (bf16[512,512]{1,0:T(8,128)(2,1)S(1)}, bf16[512,512]{1,0:T(8,128)(2,1)S(1)}, u32[]{:S(2)}, u32[]{:S(2)}) collective-permute-start(bf16[512,512]{1,0:T(8,128)(2,1)S(1)} %collective-permute-done.8.rest_1_), channel_id=1, source_target_pairs={{4,8},{8,4},{5,9},{9,5},{6,10},{10,6},{7,11},{11,7},{20,24},{24,20... | collective-permute-start | bytes 1572872 | tf_op jit(solution)/shard_map/ppermute | solution.py:266
  36.4 32.1 %collective-permute-start.7 = (bf16[4,3,5,32,256]{4,3,2,1,0:T(8,128)(2,1)S(1)}, bf16[4,3,5,32,256]{4,3,2,1,0:T(8,128)(2,1)S(1)}, u32[]{:S(2)}, u32[]{:S(2)}) collective-permute-start(bf16[4,3,5,32,256]{4,3,2,1,0:T(8,128)(2,1)S(1)} %get-tuple-element.48), channel_id=1, source_target_pairs={{0,1},{1,0},{2,3},{3,2},{4,5},{5,4},{6,7},{7,6},{8,9},{9,8},{10,11... | collective-permute-start | bytes 2949128 | tf_op jit(solution)/shard_map/ppermute | solution.py:291
  38.3 13.5 %collective-permute-start.16 = (bf16[512,512]{1,0:T(8,128)(2,1)S(1)}, bf16[512,512]{1,0:T(8,128)(2,1)S(1)}, u32[]{:S(2)}, u32[]{:S(2)}) collective-permute-start(bf16[512,512]{1,0:T(8,128)(2,1)S(1)} %bitcast.30), channel_id=1, source_target_pairs={{0,2},{2,0},{1,3},{3,1},{4,6},{6,4},{5,7},{7,5},{8,10},{10,8},{9,1... | collective-permute-start | bytes 1572872 | tf_op jit(solution)/shard_map/ppermute | solution.py:210
  39.8 12.7 %collective-permute-start.18 = (bf16[512,512]{1,0:T(8,128)(2,1)S(1)}, bf16[512,512]{1,0:T(8,128)(2,1)S(1)}, u32[]{:S(2)}, u32[]{:S(2)}) collective-permute-start(bf16[512,512]{1,0:T(8,128)(2,1)S(1)} %vertical.4.rest_0_), channel_id=1, source_target_pairs={{4,8},{8,4},{5,9},{9,5},{6,10},{10,6},{7,11},{11,7},{20,24},{24,20... | collective-permute-start | bytes 1572872 | tf_op jit(solution)/shard_map/ppermute | solution.py:262
  44.2 10.3 %collective-permute-start.15 = (bf16[512,512]{1,0:T(8,128)(2,1)S(1)}, bf16[512,512]{1,0:T(8,128)(2,1)S(1)}, u32[]{:S(2)}, u32[]{:S(2)}) collective-permute-start(bf16[512,512]{1,0:T(8,128)(2,1)S(1)} %vertical.4.rest_0_), channel_id=1, source_target_pairs={{0,4},{4,0},{8,12},{12,8},{1,5},{5,1},{9,13},{13,9},{2,6},{6,2},{1... | collective-permute-start | bytes 1572872 | tf_op jit(solution)/shard_map/ppermute | solution.py:261
  44.3 21.5 %collective-permute-start.13 = (bf16[512,512]{1,0:T(8,128)(2,1)S(1)}, bf16[512,512]{1,0:T(8,128)(2,1)S(1)}, u32[]{:S(2)}, u32[]{:S(2)}) collective-permute-start(bf16[512,512]{1,0:T(8,128)(2,1)S(1)} %collective-permute-done.10.rest_2_), channel_id=1, source_target_pairs={{4,0},{8,12},{5,1},{9,13},{6,2},{10,14},{7,3},{11,15},{20,16},{24,... | collective-permute-start | bytes 1572872 | tf_op jit(solution)/shard_map/ppermute | solution.py:269
  54.6 24.7 %collective-permute-start.20 = (bf16[512,512]{1,0:T(8,128)(2,1)S(1)}, bf16[512,512]{1,0:T(8,128)(2,1)S(1)}, u32[]{:S(2)}, u32[]{:S(2)}) collective-permute-start(bf16[512,512]{1,0:T(8,128)(2,1)S(1)} %vertical.5.rest_0_), channel_id=1, source_target_pairs={{0,4},{4,0},{8,12},{12,8},{1,5},{5,1},{9,13},{13,9},{2,6},{6,2},{1... | collective-permute-start | bytes 1572872 | tf_op jit(solution)/shard_map/ppermute | solution.py:261
  65.8 22.5 %collective-permute-start.19 = (bf16[512,512]{1,0:T(8,128)(2,1)S(1)}, bf16[512,512]{1,0:T(8,128)(2,1)S(1)}, u32[]{:S(2)}, u32[]{:S(2)}) collective-permute-start(bf16[512,512]{1,0:T(8,128)(2,1)S(1)} %collective-permute-done.18.rest_4_), channel_id=1, source_target_pairs={{4,0},{8,12},{5,1},{9,13},{6,2},{10,14},{7,3},{11,15},{20,16},{24,... | collective-permute-start | bytes 1572872 | tf_op jit(solution)/shard_map/ppermute | solution.py:265
  67.1 21.2 %collective-permute-start.17 = (bf16[512,512]{1,0:T(8,128)(2,1)S(1)}, bf16[512,512]{1,0:T(8,128)(2,1)S(1)}, u32[]{:S(2)}, u32[]{:S(2)}) collective-permute-start(bf16[512,512]{1,0:T(8,128)(2,1)S(1)} %collective-permute-done.15.rest_1_), channel_id=1, source_target_pairs={{4,8},{8,4},{5,9},{9,5},{6,10},{10,6},{7,11},{11,7},{20,24},{24,20... | collective-permute-start | bytes 1572872 | tf_op jit(solution)/shard_map/ppermute | solution.py:266
  67.8 20.5 %collective-permute-start.21 = (bf16[512,512]{1,0:T(8,128)(2,1)S(1)}, bf16[512,512]{1,0:T(8,128)(2,1)S(1)}, u32[]{:S(2)}, u32[]{:S(2)}) collective-permute-start(bf16[512,512]{1,0:T(8,128)(2,1)S(1)} %vertical.5.rest_0_), channel_id=1, source_target_pairs={{4,8},{8,4},{5,9},{9,5},{6,10},{10,6},{7,11},{11,7},{20,24},{24,20... | collective-permute-start | bytes 1572872 | tf_op jit(solution)/shard_map/ppermute | solution.py:262
  68.7 30.8 %copy-start.4 = (s32[2,3,3]{2,0,1:T(2,128)S(1)}, s32[2,3,3]{2,0,1:T(2,128)}, u32[]{:S(2)}) copy-start(s32[2,3,3]{2,0,1:T(2,128)} %param.14) | copy-start | bytes 220
  68.7 30.8 %copy-start = (bf16[1,3,3,256,256]{4,3,2,1,0:T(8,128)(2,1)S(1)}, bf16[1,3,3,256,256]{4,3,2,1,0:T(8,128)(2,1)}, u32[]{:S(2)}) copy-start(bf16[1,3,3,256,256]{4,3,2,1,0:T(8,128)(2,1)} %coef.7) | copy-start | bytes 3538948
  71.5 46.2 %collective-permute-start.14 = (bf16[5,512,256]{2,1,0:T(8,128)(2,1)S(1)}, bf16[5,512,256]{2,1,0:T(8,128)(2,1)S(1)}, u32[]{:S(2)}, u32[]{:S(2)}) collective-permute-start(bf16[5,512,256]{2,1,0:T(8,128)(2,1)S(1)} %spread.4.rest_0_), channel_id=1, source_target_pairs={{0,1},{1,0},{2,3},{3,2},{4,5},{5,4},{6,7},{7,6},{8,9},{9,8},{10,11... | collective-permute-start | bytes 3932168 | tf_op jit(solution)/shard_map/ppermute | solution.py:332
  88.3 9.9 %collective-permute-start.22 = (bf16[512,512]{1,0:T(8,128)(2,1)S(1)}, bf16[512,512]{1,0:T(8,128)(2,1)S(1)}, u32[]{:S(2)}, u32[]{:S(2)}) collective-permute-start(bf16[512,512]{1,0:T(8,128)(2,1)S(1)} %collective-permute-done.17.rest_2_), channel_id=1, source_target_pairs={{4,0},{8,12},{5,1},{9,13},{6,2},{10,14},{7,3},{11,15},{20,16},{24,... | collective-permute-start | bytes 1572872 | tf_op jit(solution)/shard_map/ppermute | solution.py:269
  89.6 8.6 %collective-permute-start.23 = (bf16[512,512]{1,0:T(8,128)(2,1)S(1)}, bf16[512,512]{1,0:T(8,128)(2,1)S(1)}, u32[]{:S(2)}, u32[]{:S(2)}) collective-permute-start(bf16[512,512]{1,0:T(8,128)(2,1)S(1)} %collective-permute-done.20.rest_1_), channel_id=1, source_target_pairs={{4,8},{8,4},{5,9},{9,5},{6,10},{10,6},{7,11},{11,7},{20,24},{24,20... | collective-permute-start | bytes 1572872 | tf_op jit(solution)/shard_map/ppermute | solution.py:266
  90.3 30.5 %collective-permute-start.24 = (bf16[512,512]{1,0:T(8,128)(2,1)S(1)}, bf16[512,512]{1,0:T(8,128)(2,1)S(1)}, u32[]{:S(2)}, u32[]{:S(2)}) collective-permute-start(bf16[512,512]{1,0:T(8,128)(2,1)S(1)} %collective-permute-done.21.rest_1_), channel_id=1, source_target_pairs={{4,0},{8,12},{5,1},{9,13},{6,2},{10,14},{7,3},{11,15},{20,16},{24,... | collective-permute-start | bytes 1572872 | tf_op jit(solution)/shard_map/ppermute | solution.py:265
  98.2 25.0 %collective-permute-start.25 = (bf16[512,512]{1,0:T(8,128)(2,1)S(1)}, bf16[512,512]{1,0:T(8,128)(2,1)S(1)}, u32[]{:S(2)}, u32[]{:S(2)}) collective-permute-start(bf16[512,512]{1,0:T(8,128)(2,1)S(1)} %collective-permute-done.23.rest_2_), channel_id=1, source_target_pairs={{4,0},{8,12},{5,1},{9,13},{6,2},{10,14},{7,3},{11,15},{20,16},{24,... | collective-permute-start | bytes 1572872 | tf_op jit(solution)/shard_map/ppermute | solution.py:269
  104.8 23.7 %collective-permute-start.27 = (bf16[5,512,256]{2,1,0:T(8,128)(2,1)S(1)}, bf16[5,512,256]{2,1,0:T(8,128)(2,1)S(1)}, u32[]{:S(2)}, u32[]{:S(2)}) collective-permute-start(bf16[5,512,256]{2,1,0:T(8,128)(2,1)S(1)} %spread.5.rest_1_), channel_id=1, source_target_pairs={{0,1},{1,0},{2,3},{3,2},{4,5},{5,4},{6,7},{7,6},{8,9},{9,8},{10,11... | collective-permute-start | bytes 3932168 | tf_op jit(solution)/shard_map/ppermute | solution.py:332
  124.6 6.9 %collective-permute-start.26 = (bf16[5,512,256]{2,1,0:T(8,128)(2,1)S(1)}, bf16[5,512,256]{2,1,0:T(8,128)(2,1)S(1)}, u32[]{:S(2)}, u32[]{:S(2)}) collective-permute-start(bf16[5,512,256]{2,1,0:T(8,128)(2,1)S(1)} %spread.7.rest_1_), channel_id=1, source_target_pairs={{0,1},{1,0},{2,3},{3,2},{4,5},{5,4},{6,7},{7,6},{8,9},{9,8},{10,11... | collective-permute-start | bytes 3932168 | tf_op jit(solution)/shard_map/ppermute | solution.py:332

commit v5 on v4

--- a/solution.py
+++ b/solution.py
@@ -206,8 +206,13 @@
     state = control.transpose(1, 2, 0)
     mine = [state[:, :CHUNK].reshape(rows, nodes)]
     state = after(state, mine[0])
-    mine += [state[:, c * CHUNK : (c + 1) * CHUNK].reshape(rows, nodes) for c in range(1, chunks)]
-    theirs = [lax.ppermute(x, "lev", swap) for x in mine]
+    valid = lax.broadcasted_iota(jnp.int32, (levels, CHUNK, nodes), 2) < node_count[0]
+    parts = [state[:, c * CHUNK : (c + 1) * CHUNK] for c in range(1, chunks)]
+    parts[-1] = jnp.where(valid, parts[-1], 0)
+    mine += [x.reshape(rows, nodes) for x in parts]
+    edge_both = [(0, 1), (1, 0), (2, 3), (3, 2)]
+    raw = lax.ppermute(mine[-1], "tile", edge_both)
+    theirs = [lax.ppermute(mine[0], "lev", swap)]
 
     merged, pieces = pl.pallas_call(
         functools.partial(merge_kernel, tiles),
@@ -237,19 +242,23 @@
         name="level_weights",
     )(after(place, merged), vert_coef)
 
-    vertical = [
-        pl.pallas_call(
+    theirs += [lax.ppermute(after(x, share), "lev", swap) for x in mine[1:]]
+
+    def do_vertical(count, x, y, *others):
+        return pl.pallas_call(
             vertical_kernel,
             in_specs=[SMEM, VMEM, VMEM, VMEM],
             out_specs=VMEM,
             out_shape=jax.ShapeDtypeStruct((rows, nodes), BF16),
             compiler_params=params(),
             name="vertical",
-        )(node_count, after(weight, share), x, y)
-        for x, y in zip(mine, theirs)
-    ]
+        )(count, after(weight, *others), x, y)
+
+    vertical = [do_vertical(node_count, x, y, share, *([raw] if i else [])) for i, (x, y) in enumerate(zip(mine, theirs))]
+    raw_other = lax.ppermute(after(raw, theirs[-1]), "lev", swap)
+    everywhere = jnp.full((1,), nodes, jnp.int32)
+
     near, across, beyond, far, farthest = ([None] * chunks for _ in range(5))
-    edge_both = [(0, 1), (1, 0), (2, 3), (3, 2)]
     middle = [(1, 2), (2, 1)]
     edge_out = [(1, 0), (2, 3)]
     slots = []
@@ -258,8 +267,11 @@
         others = others + tuple(slots[-2] if len(slots) > 1 else ())
         if kind == "near":
             value = after(vertical[c], *others)
+            across[c] = lax.ppermute(value, "tile", middle)
+            if c + 1 == chunks:
+                near[c] = do_vertical(everywhere, raw, raw_other)
+                return
             near[c] = lax.ppermute(value, "tile", edge_both)
-            across[c] = lax.ppermute(value, "tile", middle)
             slots.append((near[c], across[c]))
         elif kind == "far":
             far[c] = lax.ppermute(after(across[c], *others), "tile", edge_out)
@@ -273,9 +285,9 @@
     slot("far", 0, vertical[1])
     slot("near", 1)
     slot("farthest", 0)
+    slot("far", 1, vertical[2])
     slot("near", 2)
-    slot("far", 1, vertical[2])
-    slot("farthest", 1)
+    slot("farthest", 1, near[2])
     slot("far", 2)
     slot("farthest", 2)
 

time: 134 us -> 129 us (0.963)
  starting transfers between devices: 54.2 us -> 34.3 us
  waiting for transfers between devices: 47.6 us -> 61.5 us
    ppermute x3, starting transfers between devices: 24.5 us -> 8.48 us  [local(): jobs = [((c, 1), lax.ppermute(fields, 'sub', swap))]]
    ppermute x3, waiting for transfers between devices: 13.8 us -> 25.8 us  [slot(): farthest[c] = lax.ppermute(after(beyond[c], *others), 'tile', edge_out)]
    ppermute x3, waiting for transfers between devices: 12.8 us -> 7.28 us  [slot(): far[c] = lax.ppermute(after(across[c], *others), 'tile', edge_out)]
    ppermute x3 -> x5, waiting for transfers between devices: 7.91 us -> 13.2 us  [the longest x2 11.9 us: local(): theirs += [lax.ppermute(after(x, share), 'lev', swap) for x in mine[1:]]]
    ppermute x3 -> x2, waiting for transfers between devices: 4.8 us -> 0.26 us  [slot(): near[c] = lax.ppermute(value, 'tile', edge_both)]
    ppermute x3 -> x2, starting transfers between devices: 4.97 us -> 0.52 us  [slot(): near[c] = lax.ppermute(value, 'tile', edge_both)]
    ppermute x1, waiting for transfers between devices: 0.01 us -> 4.31 us  [local(): lax.ppermute(share, 'lev', swap)]
    ppermute x1, waiting for transfers between devices: 0.01 us -> 3.99 us  [local(): lax.ppermute(share, ('grp', 'lev'), corner)]
  transfers between devices with their start and end apart: 28 -> 29, of which waited for: 11 -> 13; matrix products, arithmetic and copies ran while one was open for 2% -> 2% of each run, Pallas kernels for 19% -> 19%
where the time goes in v5:
time: 129 us
  waiting for transfers between devices  61.5 us (48%)
  starting transfers between devices  34.3 us (27%)
  Pallas kernels  27.1 us (21%)
  local copies, waits for them, and re-layouts  2.95 us (2%)
  other arithmetic  1.66 us (1%)
    ppermute x3, waiting for transfers between devices, slot(): farthest[c] = lax.ppermute(after(beyond[c], *others), 'tile', edge_out)  25.8 us
    ppermute x2, waiting for transfers between devices, local(): theirs += [lax.ppermute(after(x, share), 'lev', swap) for x in mine[1:]]  11.9 us
    pallas_call x4, Pallas kernels, interpolate(): pl.pallas_call(functools.partial(interp_kernel, tiles, members // 2 // CH...  11 us
    pallas_call x4, Pallas kernels, spread(): pl.pallas_call(functools.partial(spread_kernel, tiles, last), in_specs=[S...  9.59 us
    ppermute x3, starting transfers between devices, local(): jobs = [((c, 1), lax.ppermute(fields, 'sub', swap))]  8.48 us
    ppermute x3, waiting for transfers between devices, slot(): far[c] = lax.ppermute(after(across[c], *others), 'tile', edge_out)  7.28 us
    ppermute x3, waiting for transfers between devices, local(): lax.ppermute(pieces[d - 1], 'tile', [(i, i ^ d) for i in range(tiles)])  6.71 us
    ppermute x1, waiting for transfers between devices, local(): lax.ppermute(share, 'lev', swap)  4.31 us
  transfers between devices with their start and end apart: 29, of which 13 were waited for; matrix products, arithmetic and copies ran while one was open for 2% of the time, Pallas kernels for 19%

profile of v5, /device:TPU:1, one launch (start us, length us, event | category | flops | bytes accessed | tf_op | source)
XLA Modules:
  0.0 128.7 jit_solution(8170166075053877492)
XLA Ops:
  0.0 2.0 %slice.24 = bf16[32,16,512]{2,1,0:T(8,128)(2,1)} slice(bf16[32,48,512]{2,1,0:T(8,128)(2,1)} %bitcast.35), slice={[0:32], [0:16], [0:512]} | slice | bytes 1048576 | tf_op jit(solution)/shard_map/slice | solution.py:207
  2.0 2.0 %collective-permute-start.3 = (bf16[512,512]{1,0:T(8,128)(2,1)}, bf16[512,512]{1,0:T(8,128)(2,1)}, u32[]{:S(2)}, u32[]{:S(2)}) collective-permute-start(bf16[512,512]{1,0:T(8,128)(2,1)} %bitcast.6.own), channel_id=1, source_target_pairs={{0,2},{2,0},{1,3},{3,1},{4,6},{6,4},{5,7},{7,5},{8,10},{10,8},{9,1... | collective-permute-start | bytes 1572872 | tf_op jit(solution)/shard_map/ppermute | solution.py:215
  4.7 0.8 copy.23.send
  5.5 1.3 slice_select_fusion
  6.9 1.4 %merge_taps.1 = (bf16[2,5,256,256]{3,2,1,0:T(8,128)(2,1)S(1)}, bf16[3,5,32,256]{3,2,1,0:T(8,128)(2,1)S(1)}) custom-call(s32[5]{0:T(128)S(1)} %stack.59.place, s32[4,4,1]{2,1,0:T(4,128)S(1)} %copy.23.send, s32[1,2,9]{2,1,0:T(2,128)S(1)} %copy-done.3, bf16[2,9,256,256]{3,2,1,0:T(8,128)(2,1)S(1)} %bitcast.29), custom_call_target="tpu_custom_call" | custom-call | tf_op jit(solution)/shard_map/merge_taps/pallas_call | solution.py:217
  8.4 1.4 %collective-permute-start = (bf16[5,32,256]{2,1,0:T(8,128)(2,1)S(1)}, bf16[5,32,256]{2,1,0:T(8,128)(2,1)S(1)}, u32[]{:S(2)}, u32[]{:S(2)}) collective-permute-start(bf16[5,32,256]{2,1,0:T(8,128)(2,1)S(1)} %get-tuple-element.57), channel_id=1, source_target_pairs={{0,4},{4,0},{8,12},{12,8},{1,5},{5,1},{9,13},{13,9},{2,6},{6,2},{1... | collective-permute-start | bytes 245768 | tf_op jit(solution)/shard_map/ppermute | solution.py:231
  9.7 2.2 %collective-permute-start.2 = (bf16[5,32,256]{2,1,0:T(8,128)(2,1)S(1)}, bf16[5,32,256]{2,1,0:T(8,128)(2,1)S(1)}, u32[]{:S(2)}, u32[]{:S(2)}) collective-permute-start(bf16[5,32,256]{2,1,0:T(8,128)(2,1)S(1)} %get-tuple-element.58), channel_id=1, source_target_pairs={{0,12},{4,8},{8,4},{12,0},{1,13},{5,9},{9,5},{13,1},{2,14},{6,10},... | collective-permute-start | bytes 245768 | tf_op jit(solution)/shard_map/ppermute | solution.py:231
  12.0 1.2 collective-permute-start.9
  13.3 2.2 %collective-permute-done.2 = bf16[5,32,256]{2,1,0:T(8,128)(2,1)S(1)} collective-permute-done((bf16[5,32,256]{2,1,0:T(8,128)(2,1)S(1)}, bf16[5,32,256]{2,1,0:T(8,128)(2,1)S(1)}, u32[]{:S(2)}, u32[]{:S(2)}) %collective-permute-start.2) | collective-permute-done | bytes 81952 | tf_op jit(solution)/shard_map/ppermute | solution.py:231
  15.5 4.5 %collective-permute-done.1 = bf16[5,32,256]{2,1,0:T(8,128)(2,1)S(1)} collective-permute-done((bf16[5,32,256]{2,1,0:T(8,128)(2,1)S(1)}, bf16[5,32,256]{2,1,0:T(8,128)(2,1)S(1)}, u32[]{:S(2)}, u32[]{:S(2)}) %collective-permute-start.1) | collective-permute-done | bytes 81952 | tf_op jit(solution)/shard_map/ppermute | solution.py:231
  20.3 1.1 level_weights.1.weight
  21.4 1.9 %vertical.4.rest_0_ = bf16[512,512]{1,0:T(8,128)(2,1)S(1)} custom-call(s32[1]{0:T(128)} %copy.28.count, bf16[2,512,512]{2,1,0:T(8,128)(2,1)S(1)} %level_weights.1.weight, bf16[512,512]{1,0:T(8,128)(2,1)} %bitcast.6.own, bf16[512,512]{1,0:T(8,128)(2,1)} %collective-permute-done.3.other), custom_call_target="tpu_custom_call" | custom-call | tf_op jit(solution)/shard_map/vertical/pallas_call | solution.py:248
  23.3 0.7 collective-permute-start.12
  24.6 2.2 %collective-permute-start.6 = (bf16[3,5,32,256]{3,2,1,0:T(8,128)(2,1)S(1)}, bf16[3,5,32,256]{3,2,1,0:T(8,128)(2,1)S(1)}, u32[]{:S(2)}, u32[]{:S(2)}) collective-permute-start(bf16[3,5,32,256]{3,2,1,0:T(8,128)(2,1)S(1)} %pad_maximum_fusion.2), channel_id=1, source_target_pairs={{0,18},{2,16},{16,2},{18,0},{1,19},{3,17},{17,3},{19,1},{4,22},{6,... | collective-permute-start | bytes 737288 | tf_op jit(solution)/shard_map/ppermute | solution.py:300
  26.7 1.3 collective-permute-done.9.own
  28.0 1.2 collective-permute-start.5
  29.2 3.3 %collective-permute-done.10.other = bf16[512,512]{1,0:T(8,128)(2,1)S(1)} collective-permute-done((bf16[512,512]{1,0:T(8,128)(2,1)S(1)}, bf16[512,512]{1,0:T(8,128)(2,1)S(1)}, u32[]{:S(2)}, u32[]{:S(2)}) %collective-permute-start.10) | collective-permute-done | bytes 524320 | tf_op jit(solution)/shard_map/ppermute | solution.py:245
  32.8 0.7 vertical.5.rest_0_
  33.5 1.3 %collective-permute-start.13 = (bf16[512,512]{1,0:T(8,128)(2,1)S(1)}, bf16[512,512]{1,0:T(8,128)(2,1)S(1)}, u32[]{:S(2)}, u32[]{:S(2)}) collective-permute-start(bf16[512,512]{1,0:T(8,128)(2,1)S(1)} %collective-permute-done.12.rest_4_), channel_id=1, source_target_pairs={{4,0},{8,12},{5,1},{9,13},{6,2},{10,14},{7,3},{11,15},{20,16},{24,... | collective-permute-start | bytes 1572872 | tf_op jit(solution)/shard_map/ppermute | solution.py:277
  34.8 4.0 %collective-permute-done.6 = bf16[3,5,32,256]{3,2,1,0:T(8,128)(2,1)S(1)} collective-permute-done((bf16[3,5,32,256]{3,2,1,0:T(8,128)(2,1)S(1)}, bf16[3,5,32,256]{3,2,1,0:T(8,128)(2,1)S(1)}, u32[]{:S(2)}, u32[]{:S(2)}) %collective-permute-start.6) | collective-permute-done | bytes 245792 | tf_op jit(solution)/shard_map/ppermute | solution.py:300
  38.8 4.3 %collective-permute-done.4 = bf16[3,5,32,256]{3,2,1,0:T(8,128)(2,1)S(1)} collective-permute-done((bf16[3,5,32,256]{3,2,1,0:T(8,128)(2,1)S(1)}, bf16[3,5,32,256]{3,2,1,0:T(8,128)(2,1)S(1)}, u32[]{:S(2)}, u32[]{:S(2)}) %collective-permute-start.4) | collective-permute-done | bytes 245792 | tf_op jit(solution)/shard_map/ppermute | solution.py:298
  43.3 1.9 %collective-permute-start.7 = (bf16[4,3,5,32,256]{4,3,2,1,0:T(8,128)(2,1)S(1)}, bf16[4,3,5,32,256]{4,3,2,1,0:T(8,128)(2,1)S(1)}, u32[]{:S(2)}, u32[]{:S(2)}) collective-permute-start(bf16[4,3,5,32,256]{4,3,2,1,0:T(8,128)(2,1)S(1)} %get-tuple-element.56), channel_id=1, source_target_pairs={{0,1},{1,0},{2,3},{3,2},{4,5},{5,4},{6,7},{7,6},{8,9},{9,8},{10,11... | collective-permute-start | bytes 2949128 | tf_op jit(solution)/shard_map/ppermute | solution.py:303
  45.2 0.7 collective-permute-start.11
  46.9 2.7 %collective-permute-done.13.rest_3_ = bf16[512,512]{1,0:T(8,128)(2,1)S(1)} collective-permute-done((bf16[512,512]{1,0:T(8,128)(2,1)S(1)}, bf16[512,512]{1,0:T(8,128)(2,1)S(1)}, u32[]{:S(2)}, u32[]{:S(2)}) %collective-permute-start.13) | collective-permute-done | bytes 524320 | tf_op jit(solution)/shard_map/ppermute | solution.py:277
  49.7 1.3 collective-permute-start.14
  50.9 8.6 %collective-permute-done.17.other = bf16[512,512]{1,0:T(8,128)(2,1)S(1)} collective-permute-done((bf16[512,512]{1,0:T(8,128)(2,1)S(1)}, bf16[512,512]{1,0:T(8,128)(2,1)S(1)}, u32[]{:S(2)}, u32[]{:S(2)}) %collective-permute-start.17) | collective-permute-done | bytes 524320 | tf_op jit(solution)/shard_map/ppermute | solution.py:245
  59.8 0.7 vertical.6.rest_0_
  61.4 1.3 %collective-permute-start.20 = (bf16[512,512]{1,0:T(8,128)(2,1)S(1)}, bf16[512,512]{1,0:T(8,128)(2,1)S(1)}, u32[]{:S(2)}, u32[]{:S(2)}) collective-permute-start(bf16[512,512]{1,0:T(8,128)(2,1)S(1)} %collective-permute-done.18.rest_4_), channel_id=1, source_target_pairs={{4,0},{8,12},{5,1},{9,13},{6,2},{10,14},{7,3},{11,15},{20,16},{24,... | collective-permute-start | bytes 1572872 | tf_op jit(solution)/shard_map/ppermute | solution.py:277
  62.9 10.0 %collective-permute-done.14.rest_5_ = bf16[512,512]{1,0:T(8,128)(2,1)S(1)} collective-permute-done((bf16[512,512]{1,0:T(8,128)(2,1)S(1)}, bf16[512,512]{1,0:T(8,128)(2,1)S(1)}, u32[]{:S(2)}, u32[]{:S(2)}) %collective-permute-start.14) | collective-permute-done | bytes 524320 | tf_op jit(solution)/shard_map/ppermute | solution.py:281
  73.0 2.8 %spread.4.rest_0_ = bf16[5,512,256]{2,1,0:T(8,128)(2,1)S(1)} custom-call(s32[5]{0:T(128)S(1)} %stack.59.place, s32[4,4,1]{2,1,0:T(4,128)S(1)} %copy.23.send, bf16[2,5,256,256]{3,2,1,0:T(8,128)(2,1)S(1)} %get-tuple-element.31.coef_own, bf16[2,4,3,5,32,256]{5,4,3,2,1,0:T(8,128)(2,1)S(1)} %pad_maximum_fusion.coef_lent, bf16[512,512]{1,0:T(8,128)(2,1)S(1)} %vertical.4.rest_0_, ...), custom_call_target="tpu_custom_call" | custom-call | tf_op jit(solution)/shard_map/spread/pallas_call | solution.py:307
  75.8 2.3 %collective-permute-start.15 = (bf16[5,512,256]{2,1,0:T(8,128)(2,1)S(1)}, bf16[5,512,256]{2,1,0:T(8,128)(2,1)S(1)}, u32[]{:S(2)}, u32[]{:S(2)}) collective-permute-start(bf16[5,512,256]{2,1,0:T(8,128)(2,1)S(1)} %spread.4.rest_0_), channel_id=1, source_target_pairs={{0,1},{1,0},{2,3},{3,2},{4,5},{5,4},{6,7},{7,6},{8,9},{9,8},{10,11... | collective-permute-start | bytes 3932168 | tf_op jit(solution)/shard_map/ppermute | solution.py:344
  78.1 0.7 vertical.7.rest_1_
  78.8 0.7 collective-permute-start.24
  79.6 1.3 %collective-permute-start.22 = (bf16[512,512]{1,0:T(8,128)(2,1)S(1)}, bf16[512,512]{1,0:T(8,128)(2,1)S(1)}, u32[]{:S(2)}, u32[]{:S(2)}) collective-permute-start(bf16[512,512]{1,0:T(8,128)(2,1)S(1)} %collective-permute-done.19.rest_2_), channel_id=1, source_target_pairs={{4,0},{8,12},{5,1},{9,13},{6,2},{10,14},{7,3},{11,15},{20,16},{24,... | collective-permute-start | bytes 1572872 | tf_op jit(solution)/shard_map/ppermute | solution.py:281
  80.9 4.6 %collective-permute-done.20.rest_3_ = bf16[512,512]{1,0:T(8,128)(2,1)S(1)} collective-permute-done((bf16[512,512]{1,0:T(8,128)(2,1)S(1)}, bf16[512,512]{1,0:T(8,128)(2,1)S(1)}, u32[]{:S(2)}, u32[]{:S(2)}) %collective-permute-start.20) | collective-permute-done | bytes 524320 | tf_op jit(solution)/shard_map/ppermute | solution.py:277
  86.1 1.3 %collective-permute-start.25 = (bf16[512,512]{1,0:T(8,128)(2,1)S(1)}, bf16[512,512]{1,0:T(8,128)(2,1)S(1)}, u32[]{:S(2)}, u32[]{:S(2)}) collective-permute-start(bf16[512,512]{1,0:T(8,128)(2,1)S(1)} %collective-permute-done.24.rest_1_), channel_id=1, source_target_pairs={{4,0},{8,12},{5,1},{9,13},{6,2},{10,14},{7,3},{11,15},{20,16},{24,... | collective-permute-start | bytes 1572872 | tf_op jit(solution)/shard_map/ppermute | solution.py:277
  87.4 7.9 %collective-permute-done.22.rest_5_ = bf16[512,512]{1,0:T(8,128)(2,1)S(1)} collective-permute-done((bf16[512,512]{1,0:T(8,128)(2,1)S(1)}, bf16[512,512]{1,0:T(8,128)(2,1)S(1)}, u32[]{:S(2)}, u32[]{:S(2)}) %collective-permute-start.22) | collective-permute-done | bytes 524320 | tf_op jit(solution)/shard_map/ppermute | solution.py:281
  95.4 1.3 collective-permute-start.26
  96.7 2.4 %interpolate.4.rest_2_ = bf16[32,96,768]{2,1,0:T(8,128)(2,1)} custom-call(s32[5]{0:T(128)S(1)} %stack.59.place, s32[4,4,1]{2,1,0:T(4,128)S(1)} %copy.23.send, s32[2,3,3]{2,1,0:T(4,128)S(1)} %copy.24.slots, bf16[1,3,3,256,256]{4,3,2,1,0:T(8,128)(2,1)S(1)} %copy-done, bf16[5,512,256]{2,1,0:T(8,128)(2,1)S(1)} %spread.4.rest_0_), custom_call_target="tpu_custom_call" | custom-call | tf_op jit(solution)/shard_map/interpolate/pallas_call | solution.py:174
  99.1 2.8 %spread.5.rest_1_ = bf16[5,512,256]{2,1,0:T(8,128)(2,1)S(1)} custom-call(s32[5]{0:T(128)S(1)} %stack.59.place, s32[4,4,1]{2,1,0:T(4,128)S(1)} %copy.23.send, bf16[2,5,256,256]{3,2,1,0:T(8,128)(2,1)S(1)} %get-tuple-element.31.coef_own, bf16[2,4,3,5,32,256]{5,4,3,2,1,0:T(8,128)(2,1)S(1)} %pad_maximum_fusion.coef_lent, bf16[512,512]{1,0:T(8,128)(2,1)S(1)} %vertical.5.rest_0_, ...), custom_call_target="tpu_custom_call" | custom-call | tf_op jit(solution)/shard_map/spread/pallas_call | solution.py:307
  102.0 3.7 %collective-permute-start.28 = (bf16[5,512,256]{2,1,0:T(8,128)(2,1)S(1)}, bf16[5,512,256]{2,1,0:T(8,128)(2,1)S(1)}, u32[]{:S(2)}, u32[]{:S(2)}) collective-permute-start(bf16[5,512,256]{2,1,0:T(8,128)(2,1)S(1)} %spread.5.rest_1_), channel_id=1, source_target_pairs={{0,1},{1,0},{2,3},{3,2},{4,5},{5,4},{6,7},{7,6},{8,9},{9,8},{10,11... | collective-permute-start | bytes 3932168 | tf_op jit(solution)/shard_map/ppermute | solution.py:344
  105.7 3.1 %interpolate.5.rest_2_ = bf16[32,96,768]{2,1,0:T(8,128)(2,1)} custom-call(s32[5]{0:T(128)S(1)} %stack.59.place, s32[4,4,1]{2,1,0:T(4,128)S(1)} %copy.23.send, s32[2,3,3]{2,1,0:T(4,128)S(1)} %copy.24.slots, bf16[1,3,3,256,256]{4,3,2,1,0:T(8,128)(2,1)S(1)} %copy-done, ...), custom_call_target="tpu_custom_call", output_to_operand_aliasing={{}: (6, {})} | custom-call | tf_op jit(solution)/shard_map/interpolate/pallas_call | solution.py:174
  108.8 2.5 %spread.6.rest_0_ = f32[5,512,256]{2,1,0:T(8,128)S(1)} custom-call(s32[5]{0:T(128)S(1)} %stack.59.place, s32[4,4,1]{2,1,0:T(4,128)S(1)} %copy.23.send, bf16[2,5,256,256]{3,2,1,0:T(8,128)(2,1)S(1)} %get-tuple-element.31.coef_own, bf16[2,4,3,5,32,256]{5,4,3,2,1,0:T(8,128)(2,1)S(1)} %pad_maximum_fusion.coef_lent, bf16[512,512]{1,0:T(8,128)(2,1)S(1)} %vertical.6.rest_0_, ...), custom_call_target="tpu_custom_call" | custom-call | tf_op jit(solution)/shard_map/spread/pallas_call | solution.py:307
  111.3 7.8 %collective-permute-done.26.rest_2_ = bf16[512,512]{1,0:T(8,128)(2,1)S(1)} collective-permute-done((bf16[512,512]{1,0:T(8,128)(2,1)S(1)}, bf16[512,512]{1,0:T(8,128)(2,1)S(1)}, u32[]{:S(2)}, u32[]{:S(2)}) %collective-permute-start.26) | collective-permute-done | bytes 524320 | tf_op jit(solution)/shard_map/ppermute | solution.py:281
  119.2 1.4 %spread.7.rest_1_ = bf16[5,512,256]{2,1,0:T(8,128)(2,1)S(1)} custom-call(s32[5]{0:T(128)S(1)} %stack.59.place, s32[4,4,1]{2,1,0:T(4,128)S(1)} %copy.23.send, bf16[2,5,256,256]{3,2,1,0:T(8,128)(2,1)S(1)} %get-tuple-element.31.coef_own, bf16[2,4,3,5,32,256]{5,4,3,2,1,0:T(8,128)(2,1)S(1)} %pad_maximum_fusion.coef_lent, f32[5,512,256]{2,1,0:T(8,128)S(1)} %spread.6.rest_0_, ...), custom_call_target="tpu_custom_call" | custom-call | tf_op jit(solution)/shard_map/spread/pallas_call | solution.py:307
  120.6 2.4 %collective-permute-start.27 = (bf16[5,512,256]{2,1,0:T(8,128)(2,1)S(1)}, bf16[5,512,256]{2,1,0:T(8,128)(2,1)S(1)}, u32[]{:S(2)}, u32[]{:S(2)}) collective-permute-start(bf16[5,512,256]{2,1,0:T(8,128)(2,1)S(1)} %spread.7.rest_1_), channel_id=1, source_target_pairs={{0,1},{1,0},{2,3},{3,2},{4,5},{5,4},{6,7},{7,6},{8,9},{9,8},{10,11... | collective-permute-start | bytes 3932168 | tf_op jit(solution)/shard_map/ppermute | solution.py:344
  123.0 3.1 %interpolate.6.rest_1_ = bf16[32,96,768]{2,1,0:T(8,128)(2,1)} custom-call(s32[5]{0:T(128)S(1)} %stack.59.place, s32[4,4,1]{2,1,0:T(4,128)S(1)} %copy.23.send, s32[2,3,3]{2,1,0:T(4,128)S(1)} %copy.24.slots, bf16[1,3,3,256,256]{4,3,2,1,0:T(8,128)(2,1)S(1)} %copy-done, ...), custom_call_target="tpu_custom_call", output_to_operand_aliasing={{}: (6, {})} | custom-call | tf_op jit(solution)/shard_map/interpolate/pallas_call | solution.py:174
  126.1 2.4 %interpolate.7 = bf16[32,96,768]{2,1,0:T(8,128)(2,1)} custom-call(s32[5]{0:T(128)S(1)} %stack.59.place, s32[4,4,1]{2,1,0:T(4,128)S(1)} %copy.23.send, s32[2,3,3]{2,1,0:T(4,128)S(1)} %copy.24.slots, bf16[1,3,3,256,256]{4,3,2,1,0:T(8,128)(2,1)S(1)} %copy-done, ...), custom_call_target="tpu_custom_call", output_to_operand_aliasing={{}: (5, {})} | custom-call | tf_op jit(solution)/shard_map/interpolate/pallas_call | solution.py:174
  (44 shorter events, 4.7 us)
Async XLA Ops:
  0.0 6.9 %copy-start.1 = (bf16[1,2,9,256,256]{4,3,2,1,0:T(8,128)(2,1)S(1)}, bf16[1,2,9,256,256]{4,3,2,1,0:T(8,128)(2,1)}, u32[]{:S(2)}) copy-start(bf16[1,2,9,256,256]{4,3,2,1,0:T(8,128)(2,1)} %param.13) | copy-start | bytes 7077892
  0.0 6.9 %copy-start.3 = (s32[1,2,9]{2,1,0:T(2,128)S(1)}, s32[1,2,9]{2,1,0:T(2,128)}, u32[]{:S(2)}) copy-start(s32[1,2,9]{2,1,0:T(2,128)} %slots.5) | copy-start | bytes 220
  2.0 19.4 %collective-permute-start.3 = (bf16[512,512]{1,0:T(8,128)(2,1)}, bf16[512,512]{1,0:T(8,128)(2,1)}, u32[]{:S(2)}, u32[]{:S(2)}) collective-permute-start(bf16[512,512]{1,0:T(8,128)(2,1)} %bitcast.6.own), channel_id=1, source_target_pairs={{0,2},{2,0},{1,3},{3,1},{4,6},{6,4},{5,7},{7,5},{8,10},{10,8},{9,1... | collective-permute-start | bytes 1572872 | tf_op jit(solution)/shard_map/ppermute | solution.py:215
  6.8 13.5 %copy-start.2 = (bf16[64,64]{1,0:T(8,128)(2,1)S(1)}, bf16[64,64]{1,0:T(8,128)(2,1)}, u32[]{:S(2)}) copy-start(bf16[64,64]{1,0:T(8,128)(2,1)} %vert.1) | copy-start | bytes 24580
  8.4 4.9 %collective-permute-start = (bf16[5,32,256]{2,1,0:T(8,128)(2,1)S(1)}, bf16[5,32,256]{2,1,0:T(8,128)(2,1)S(1)}, u32[]{:S(2)}, u32[]{:S(2)}) collective-permute-start(bf16[5,32,256]{2,1,0:T(8,128)(2,1)S(1)} %get-tuple-element.57), channel_id=1, source_target_pairs={{0,4},{4,0},{8,12},{12,8},{1,5},{5,1},{9,13},{13,9},{2,6},{6,2},{1... | collective-permute-start | bytes 245768 | tf_op jit(solution)/shard_map/ppermute | solution.py:231
  9.7 5.8 %collective-permute-start.2 = (bf16[5,32,256]{2,1,0:T(8,128)(2,1)S(1)}, bf16[5,32,256]{2,1,0:T(8,128)(2,1)S(1)}, u32[]{:S(2)}, u32[]{:S(2)}) collective-permute-start(bf16[5,32,256]{2,1,0:T(8,128)(2,1)S(1)} %get-tuple-element.58), channel_id=1, source_target_pairs={{0,12},{4,8},{8,4},{12,0},{1,13},{5,9},{9,5},{13,1},{2,14},{6,10},... | collective-permute-start | bytes 245768 | tf_op jit(solution)/shard_map/ppermute | solution.py:231
  11.9 8.1 %collective-permute-start.1 = (bf16[5,32,256]{2,1,0:T(8,128)(2,1)S(1)}, bf16[5,32,256]{2,1,0:T(8,128)(2,1)S(1)}, u32[]{:S(2)}, u32[]{:S(2)}) collective-permute-start(bf16[5,32,256]{2,1,0:T(8,128)(2,1)S(1)} %get-tuple-element.59), channel_id=1, source_target_pairs={{0,8},{4,12},{8,0},{12,4},{1,9},{5,13},{9,1},{13,5},{2,10},{6,14},... | collective-permute-start | bytes 245768 | tf_op jit(solution)/shard_map/ppermute | solution.py:231
  12.0 16.0 %collective-permute-start.9 = (bf16[512,512]{1,0:T(8,128)(2,1)S(1)}, bf16[512,512]{1,0:T(8,128)(2,1)S(1)}, u32[]{:S(2)}, u32[]{:S(2)}) collective-permute-start(bf16[512,512]{1,0:T(8,128)(2,1)S(1)} %bitcast.30), channel_id=1, source_target_pairs={{0,4},{4,0},{8,12},{12,8},{1,5},{5,1},{9,13},{13,9},{2,6},{6,2},{1... | collective-permute-start | bytes 1572872 | tf_op jit(solution)/shard_map/ppermute | solution.py:214
  20.0 12.5 %collective-permute-start.10 = (bf16[512,512]{1,0:T(8,128)(2,1)S(1)}, bf16[512,512]{1,0:T(8,128)(2,1)S(1)}, u32[]{:S(2)}, u32[]{:S(2)}) collective-permute-start(bf16[512,512]{1,0:T(8,128)(2,1)S(1)} %bitcast.33), channel_id=1, source_target_pairs={{0,2},{2,0},{1,3},{3,1},{4,6},{6,4},{5,7},{7,5},{8,10},{10,8},{9,1... | collective-permute-start | bytes 1572872 | tf_op jit(solution)/shard_map/ppermute | solution.py:245
  23.3 10.2 %collective-permute-start.12 = (bf16[512,512]{1,0:T(8,128)(2,1)S(1)}, bf16[512,512]{1,0:T(8,128)(2,1)S(1)}, u32[]{:S(2)}, u32[]{:S(2)}) collective-permute-start(bf16[512,512]{1,0:T(8,128)(2,1)S(1)} %vertical.4.rest_0_), channel_id=1, source_target_pairs={{4,8},{8,4},{5,9},{9,5},{6,10},{10,6},{7,11},{11,7},{20,24},{24,20... | collective-permute-start | bytes 1572872 | tf_op jit(solution)/shard_map/ppermute | solution.py:270
  24.0 21.2 %collective-permute-start.8 = (bf16[512,512]{1,0:T(8,128)(2,1)S(1)}, bf16[512,512]{1,0:T(8,128)(2,1)S(1)}, u32[]{:S(2)}, u32[]{:S(2)}) collective-permute-start(bf16[512,512]{1,0:T(8,128)(2,1)S(1)} %vertical.4.rest_0_), channel_id=1, source_target_pairs={{0,4},{4,0},{8,12},{12,8},{1,5},{5,1},{9,13},{13,9},{2,6},{6,2},{1... | collective-permute-start | bytes 1572872 | tf_op jit(solution)/shard_map/ppermute | solution.py:274
  24.6 14.3 %collective-permute-start.6 = (bf16[3,5,32,256]{3,2,1,0:T(8,128)(2,1)S(1)}, bf16[3,5,32,256]{3,2,1,0:T(8,128)(2,1)S(1)}, u32[]{:S(2)}, u32[]{:S(2)}) collective-permute-start(bf16[3,5,32,256]{3,2,1,0:T(8,128)(2,1)S(1)} %pad_maximum_fusion.2), channel_id=1, source_target_pairs={{0,18},{2,16},{16,2},{18,0},{1,19},{3,17},{17,3},{19,1},{4,22},{6,... | collective-permute-start | bytes 737288 | tf_op jit(solution)/shard_map/ppermute | solution.py:300
  28.0 10.8 %collective-permute-start.5 = (bf16[3,5,32,256]{3,2,1,0:T(8,128)(2,1)S(1)}, bf16[3,5,32,256]{3,2,1,0:T(8,128)(2,1)S(1)}, u32[]{:S(2)}, u32[]{:S(2)}) collective-permute-start(bf16[3,5,32,256]{3,2,1,0:T(8,128)(2,1)S(1)} %pad_maximum_fusion.2), channel_id=1, source_target_pairs={{0,16},{16,0},{1,17},{17,1},{2,18},{18,2},{3,19},{19,3},{4,20},{20... | collective-permute-start | bytes 737288 | tf_op jit(solution)/shard_map/ppermute | solution.py:299
  32.6 10.6 %collective-permute-start.4 = (bf16[3,5,32,256]{3,2,1,0:T(8,128)(2,1)S(1)}, bf16[3,5,32,256]{3,2,1,0:T(8,128)(2,1)S(1)}, u32[]{:S(2)}, u32[]{:S(2)}) collective-permute-start(bf16[3,5,32,256]{3,2,1,0:T(8,128)(2,1)S(1)} %pad_maximum_fusion.2), channel_id=1, source_target_pairs={{0,2},{2,0},{1,3},{3,1},{4,6},{6,4},{5,7},{7,5},{8,10},{10,8},{9,1... | collective-permute-start | bytes 737288 | tf_op jit(solution)/shard_map/ppermute | solution.py:298
  33.5 16.1 %collective-permute-start.13 = (bf16[512,512]{1,0:T(8,128)(2,1)S(1)}, bf16[512,512]{1,0:T(8,128)(2,1)S(1)}, u32[]{:S(2)}, u32[]{:S(2)}) collective-permute-start(bf16[512,512]{1,0:T(8,128)(2,1)S(1)} %collective-permute-done.12.rest_4_), channel_id=1, source_target_pairs={{4,0},{8,12},{5,1},{9,13},{6,2},{10,14},{7,3},{11,15},{20,16},{24,... | collective-permute-start | bytes 1572872 | tf_op jit(solution)/shard_map/ppermute | solution.py:277
  43.3 19.4 %collective-permute-start.7 = (bf16[4,3,5,32,256]{4,3,2,1,0:T(8,128)(2,1)S(1)}, bf16[4,3,5,32,256]{4,3,2,1,0:T(8,128)(2,1)S(1)}, u32[]{:S(2)}, u32[]{:S(2)}) collective-permute-start(bf16[4,3,5,32,256]{4,3,2,1,0:T(8,128)(2,1)S(1)} %get-tuple-element.56), channel_id=1, source_target_pairs={{0,1},{1,0},{2,3},{3,2},{4,5},{5,4},{6,7},{7,6},{8,9},{9,8},{10,11... | collective-permute-start | bytes 2949128 | tf_op jit(solution)/shard_map/ppermute | solution.py:303
  45.2 4.4 %collective-permute-start.11 = (bf16[512,512]{1,0:T(8,128)(2,1)S(1)}, bf16[512,512]{1,0:T(8,128)(2,1)S(1)}, u32[]{:S(2)}, u32[]{:S(2)}) collective-permute-start(bf16[512,512]{1,0:T(8,128)(2,1)S(1)} %collective-permute-done.8.rest_1_), channel_id=1, source_target_pairs={{4,8},{8,4},{5,9},{9,5},{6,10},{10,6},{7,11},{11,7},{20,24},{24,20... | collective-permute-start | bytes 1572872 | tf_op jit(solution)/shard_map/ppermute | solution.py:278
  45.9 13.6 %collective-permute-start.17 = (bf16[512,512]{1,0:T(8,128)(2,1)S(1)}, bf16[512,512]{1,0:T(8,128)(2,1)S(1)}, u32[]{:S(2)}, u32[]{:S(2)}) collective-permute-start(bf16[512,512]{1,0:T(8,128)(2,1)S(1)} %bitcast.31), channel_id=1, source_target_pairs={{0,2},{2,0},{1,3},{3,1},{4,6},{6,4},{5,7},{7,5},{8,10},{10,8},{9,1... | collective-permute-start | bytes 1572872 | tf_op jit(solution)/shard_map/ppermute | solution.py:245
  46.2 14.2 %collective-permute-start.18 = (bf16[512,512]{1,0:T(8,128)(2,1)S(1)}, bf16[512,512]{1,0:T(8,128)(2,1)S(1)}, u32[]{:S(2)}, u32[]{:S(2)}) collective-permute-start(bf16[512,512]{1,0:T(8,128)(2,1)S(1)} %vertical.5.rest_0_), channel_id=1, source_target_pairs={{4,8},{8,4},{5,9},{9,5},{6,10},{10,6},{7,11},{11,7},{20,24},{24,20... | collective-permute-start | bytes 1572872 | tf_op jit(solution)/shard_map/ppermute | solution.py:270
  49.7 11.1 %collective-permute-start.16 = (bf16[512,512]{1,0:T(8,128)(2,1)S(1)}, bf16[512,512]{1,0:T(8,128)(2,1)S(1)}, u32[]{:S(2)}, u32[]{:S(2)}) collective-permute-start(bf16[512,512]{1,0:T(8,128)(2,1)S(1)} %vertical.5.rest_0_), channel_id=1, source_target_pairs={{0,4},{4,0},{8,12},{12,8},{1,5},{5,1},{9,13},{13,9},{2,6},{6,2},{1... | collective-permute-start | bytes 1572872 | tf_op jit(solution)/shard_map/ppermute | solution.py:274
  49.7 23.3 %collective-permute-start.14 = (bf16[512,512]{1,0:T(8,128)(2,1)S(1)}, bf16[512,512]{1,0:T(8,128)(2,1)S(1)}, u32[]{:S(2)}, u32[]{:S(2)}) collective-permute-start(bf16[512,512]{1,0:T(8,128)(2,1)S(1)} %collective-permute-done.11.rest_2_), channel_id=1, source_target_pairs={{4,0},{8,12},{5,1},{9,13},{6,2},{10,14},{7,3},{11,15},{20,16},{24,... | collective-permute-start | bytes 1572872 | tf_op jit(solution)/shard_map/ppermute | solution.py:281
  59.5 18.6 %collective-permute-start.21 = (bf16[512,512]{1,0:T(8,128)(2,1)S(1)}, bf16[512,512]{1,0:T(8,128)(2,1)S(1)}, u32[]{:S(2)}, u32[]{:S(2)}) collective-permute-start(bf16[512,512]{1,0:T(8,128)(2,1)S(1)} %collective-permute-done.9.own), channel_id=1, source_target_pairs={{0,2},{2,0},{1,3},{3,1},{4,6},{6,4},{5,7},{7,5},{8,10},{10,8},{9,1... | collective-permute-start | bytes 1572872 | tf_op jit(solution)/shard_map/ppermute | solution.py:258
  60.8 18.8 %collective-permute-start.19 = (bf16[512,512]{1,0:T(8,128)(2,1)S(1)}, bf16[512,512]{1,0:T(8,128)(2,1)S(1)}, u32[]{:S(2)}, u32[]{:S(2)}) collective-permute-start(bf16[512,512]{1,0:T(8,128)(2,1)S(1)} %collective-permute-done.16.rest_1_), channel_id=1, source_target_pairs={{4,8},{8,4},{5,9},{9,5},{6,10},{10,6},{7,11},{11,7},{20,24},{24,20... | collective-permute-start | bytes 1572872 | tf_op jit(solution)/shard_map/ppermute | solution.py:278
  61.4 24.0 %collective-permute-start.20 = (bf16[512,512]{1,0:T(8,128)(2,1)S(1)}, bf16[512,512]{1,0:T(8,128)(2,1)S(1)}, u32[]{:S(2)}, u32[]{:S(2)}) collective-permute-start(bf16[512,512]{1,0:T(8,128)(2,1)S(1)} %collective-permute-done.18.rest_4_), channel_id=1, source_target_pairs={{4,0},{8,12},{5,1},{9,13},{6,2},{10,14},{7,3},{11,15},{20,16},{24,... | collective-permute-start | bytes 1572872 | tf_op jit(solution)/shard_map/ppermute | solution.py:277
  75.8 20.9 %copy-start.4 = (s32[2,3,3]{2,0,1:T(2,128)S(1)}, s32[2,3,3]{2,0,1:T(2,128)}, u32[]{:S(2)}) copy-start(s32[2,3,3]{2,0,1:T(2,128)} %param.14) | copy-start | bytes 220
  75.8 20.9 %copy-start = (bf16[1,3,3,256,256]{4,3,2,1,0:T(8,128)(2,1)S(1)}, bf16[1,3,3,256,256]{4,3,2,1,0:T(8,128)(2,1)}, u32[]{:S(2)}) copy-start(bf16[1,3,3,256,256]{4,3,2,1,0:T(8,128)(2,1)} %coef.7) | copy-start | bytes 3538948
  75.8 29.9 %collective-permute-start.15 = (bf16[5,512,256]{2,1,0:T(8,128)(2,1)S(1)}, bf16[5,512,256]{2,1,0:T(8,128)(2,1)S(1)}, u32[]{:S(2)}, u32[]{:S(2)}) collective-permute-start(bf16[5,512,256]{2,1,0:T(8,128)(2,1)S(1)} %spread.4.rest_0_), channel_id=1, source_target_pairs={{0,1},{1,0},{2,3},{3,2},{4,5},{5,4},{6,7},{7,6},{8,9},{9,8},{10,11... | collective-permute-start | bytes 3932168 | tf_op jit(solution)/shard_map/ppermute | solution.py:344
  78.8 7.3 %collective-permute-start.24 = (bf16[512,512]{1,0:T(8,128)(2,1)S(1)}, bf16[512,512]{1,0:T(8,128)(2,1)S(1)}, u32[]{:S(2)}, u32[]{:S(2)}) collective-permute-start(bf16[512,512]{1,0:T(8,128)(2,1)S(1)} %vertical.6.rest_0_), channel_id=1, source_target_pairs={{4,8},{8,4},{5,9},{9,5},{6,10},{10,6},{7,11},{11,7},{20,24},{24,20... | collective-permute-start | bytes 1572872 | tf_op jit(solution)/shard_map/ppermute | solution.py:270
  79.6 15.8 %collective-permute-start.22 = (bf16[512,512]{1,0:T(8,128)(2,1)S(1)}, bf16[512,512]{1,0:T(8,128)(2,1)S(1)}, u32[]{:S(2)}, u32[]{:S(2)}) collective-permute-start(bf16[512,512]{1,0:T(8,128)(2,1)S(1)} %collective-permute-done.19.rest_2_), channel_id=1, source_target_pairs={{4,0},{8,12},{5,1},{9,13},{6,2},{10,14},{7,3},{11,15},{20,16},{24,... | collective-permute-start | bytes 1572872 | tf_op jit(solution)/shard_map/ppermute | solution.py:281
  85.4 10.0 %collective-permute-start.23 = (bf16[512,512]{1,0:T(8,128)(2,1)S(1)}, bf16[512,512]{1,0:T(8,128)(2,1)S(1)}, u32[]{:S(2)}, u32[]{:S(2)}) collective-permute-start(bf16[512,512]{1,0:T(8,128)(2,1)S(1)} %vertical.7.rest_1_), channel_id=1, source_target_pairs={{4,8},{8,4},{5,9},{9,5},{6,10},{10,6},{7,11},{11,7},{20,24},{24,20... | collective-permute-start | bytes 1572872 | tf_op jit(solution)/shard_map/ppermute | solution.py:278
  86.1 22.6 %collective-permute-start.25 = (bf16[512,512]{1,0:T(8,128)(2,1)S(1)}, bf16[512,512]{1,0:T(8,128)(2,1)S(1)}, u32[]{:S(2)}, u32[]{:S(2)}) collective-permute-start(bf16[512,512]{1,0:T(8,128)(2,1)S(1)} %collective-permute-done.24.rest_1_), channel_id=1, source_target_pairs={{4,0},{8,12},{5,1},{9,13},{6,2},{10,14},{7,3},{11,15},{20,16},{24,... | collective-permute-start | bytes 1572872 | tf_op jit(solution)/shard_map/ppermute | solution.py:277
  95.4 23.8 %collective-permute-start.26 = (bf16[512,512]{1,0:T(8,128)(2,1)S(1)}, bf16[512,512]{1,0:T(8,128)(2,1)S(1)}, u32[]{:S(2)}, u32[]{:S(2)}) collective-permute-start(bf16[512,512]{1,0:T(8,128)(2,1)S(1)} %collective-permute-done.23.rest_2_), channel_id=1, source_target_pairs={{4,0},{8,12},{5,1},{9,13},{6,2},{10,14},{7,3},{11,15},{20,16},{24,... | collective-permute-start | bytes 1572872 | tf_op jit(solution)/shard_map/ppermute | solution.py:281
  102.0 21.1 %collective-permute-start.28 = (bf16[5,512,256]{2,1,0:T(8,128)(2,1)S(1)}, bf16[5,512,256]{2,1,0:T(8,128)(2,1)S(1)}, u32[]{:S(2)}, u32[]{:S(2)}) collective-permute-start(bf16[5,512,256]{2,1,0:T(8,128)(2,1)S(1)} %spread.5.rest_1_), channel_id=1, source_target_pairs={{0,1},{1,0},{2,3},{3,2},{4,5},{5,4},{6,7},{7,6},{8,9},{9,8},{10,11... | collective-permute-start | bytes 3932168 | tf_op jit(solution)/shard_map/ppermute | solution.py:344
  120.6 5.5 %collective-permute-start.27 = (bf16[5,512,256]{2,1,0:T(8,128)(2,1)S(1)}, bf16[5,512,256]{2,1,0:T(8,128)(2,1)S(1)}, u32[]{:S(2)}, u32[]{:S(2)}) collective-permute-start(bf16[5,512,256]{2,1,0:T(8,128)(2,1)S(1)} %spread.7.rest_1_), channel_id=1, source_target_pairs={{0,1},{1,0},{2,3},{3,2},{4,5},{5,4},{6,7},{7,6},{8,9},{9,8},{10,11... | collective-permute-start | bytes 3932168 | tf_op jit(solution)/shard_map/ppermute | solution.py:344
